TPU v7x, 32 devices: a whole 2x2x4 slice. The times are simulated.
32 devices in a mesh: seq: 4 (over z), tp: 4 (over y, x), fsdp: 2 (over core).
Axes of the slice: x: 2, y: 2, z: 4, core: 2. Of those that a mesh axis runs over, the one named last changes fastest.
Arguments:
- decoder_in: bfloat16 [32, 128, 1024], P(('seq', 'fsdp')), may hold values from -6 to 6
- memory: bfloat16 [32, 2048, 1024], P(('seq', 'fsdp')), may hold values from -6 to 6
- buckets: int32 [128, 128], replicated, may hold values from 0 to 31
- norm_gains: bfloat16 [3, 1024], P(None, ('seq', 'fsdp')), may hold values from 0.5 to 1.5
- rel_bias: bfloat16 [32, 16], P(('seq', 'fsdp'), 'tp'), may hold values from -4 to 4
- self_q: bfloat16 [1024, 1024], P(('seq', 'fsdp'), 'tp'), may hold values from -0.1875 to 0.1875
- self_kv: bfloat16 [1024, 2, 512], P(('seq', 'fsdp'), None, 'tp'), may hold values from -0.1875 to 0.1875
- self_out: bfloat16 [1024, 1024], P('tp', ('seq', 'fsdp')), may hold values from -0.75 to 0.75
- cross_q: bfloat16 [1024, 1024], P(('seq', 'fsdp'), 'tp'), may hold values from -0.1875 to 0.1875
- cross_kv: bfloat16 [1024, 2, 512], P(('seq', 'fsdp'), None, 'tp'), may hold values from -0.1875 to 0.1875
- cross_out: bfloat16 [1024, 1024], P('tp', ('seq', 'fsdp')), may hold values from -3 to 3
- gate_up: bfloat16 [1024, 2, 2816], P(('seq', 'fsdp'), None, 'tp'), may hold values from -0.1875 to 0.1875
- down: bfloat16 [2816, 1024], P('tp', ('seq', 'fsdp')), may hold values from -0.109375 to 0.109375
- cotangent: bfloat16 [32, 128, 1024], P(('seq', 'fsdp')), may hold values from -6 to 6
Outputs:
- decoder_out: bfloat16 [32, 128, 1024], P(('seq', 'fsdp'))
- decoder_grad: float32 [32, 128, 1024], P(('seq', 'fsdp'))
- memory_grad: bfloat16 [32, 2048, 1024], P(('seq', 'fsdp'), None, 'tp')
- gains_grad: float32 [3, 1024], P(None, ('seq', 'fsdp'))
- bias_grad: float32 [32, 16], P(('seq', 'fsdp'), 'tp')
- self_q_grad: float32 [1024, 1024], P(('seq', 'fsdp'), 'tp')
- self_kv_grad: float32 [1024, 2, 512], P(('seq', 'fsdp'), None, 'tp')
- self_out_grad: float32 [1024, 1024], P('tp', ('seq', 'fsdp'))
- cross_q_grad: float32 [1024, 1024], P(('seq', 'fsdp'), 'tp')
- cross_kv_grad: float32 [1024, 2, 512], P(('seq', 'fsdp'), None, 'tp')
- cross_out_grad: float32 [1024, 1024], P('tp', ('seq', 'fsdp'))
- gate_up_grad: float32 [1024, 2, 2816], P(('seq', 'fsdp'), None, 'tp')
- down_grad: float32 [2816, 1024], P('tp', ('seq', 'fsdp'))
Inputs may be any that keep to these rules, and one draw needn't show every extreme that they name: `buckets`: the bucket of query position i and key position j, the same for every sequence and head.
All inputs are finite; a program needn't handle non-finite values.
Results may differ from a plain program's by a relative error of at most 0.04.
Values may be sent and summed in bfloat16 or wider, within the bound.
No kernel may reach another device: no remote copies, remote signals or barrier semaphores. Data moves between devices by JAX's collectives and lax.ppermute only.
A program may use at most 192 MiB of HBM per device.

v0:
```python
import jax
import jax.numpy as jnp
from jax import lax
from jax.sharding import PartitionSpec as P

DH = 64
NB = 32
MICRO = 2


EPSILON = 1e-06
MASKED = -1e30


def rms_norm(values, gain):
    return values * lax.rsqrt(jnp.mean(values * values, axis=-1, keepdims=True) + EPSILON) * gain


def gelu_product(gate, up):
    return jax.nn.gelu(gate, approximate=True) * up


def flatten(weight):
    return weight.reshape(weight.shape[0], -1)


def gather_weights(
    gains, table, self_q, self_kv, self_out, cross_q, cross_kv, cross_out, gate_up, down
):
    return (
        lax.all_gather(gains, ("seq", "fsdp"), axis=1, tiled=True),
        lax.all_gather(table, ("seq", "fsdp"), axis=0, tiled=True),
        lax.all_gather(self_q, ("seq", "fsdp"), axis=0, tiled=True),
        lax.all_gather(self_kv, ("seq", "fsdp"), axis=0, tiled=True),
        lax.all_gather(self_out, ("seq", "fsdp"), axis=1, tiled=True),
        lax.all_gather(cross_q, ("seq", "fsdp"), axis=0, tiled=True),
        lax.all_gather(cross_kv, ("seq", "fsdp"), axis=0, tiled=True),
        lax.all_gather(cross_out, ("seq", "fsdp"), axis=1, tiled=True),
        lax.all_gather(gate_up, ("seq", "fsdp"), axis=0, tiled=True),
        lax.all_gather(down, ("seq", "fsdp"), axis=1, tiled=True),
    )


def branch_total(partial_value):
    return lax.psum(partial_value.astype(jnp.bfloat16), "tp").astype(jnp.float32)


def input_total(partial_value):
    return lax.psum(partial_value.astype(jnp.bfloat16), "tp").astype(jnp.float32)


def split_heads(query, keys, values):
    batch, rows, width = query.shape
    span = keys.shape[1]
    groups = keys.shape[2] // DH
    ratio = width // DH // groups
    return (
        query.reshape(batch, rows, groups, ratio, DH),
        keys.reshape(batch, span, groups, DH),
        values.reshape(batch, span, groups, DH),
    )


def scores_of(query_heads, key_heads, bias, causal):
    scores = jnp.einsum(
        "bigrd,bjgd->bgrij", query_heads, key_heads, preferred_element_type=jnp.float32
    ) * DH ** (-0.5)
    if bias is not None:
        scores = scores + bias
    if causal is not None:
        scores = jnp.where(causal, scores, MASKED)
    return scores


def attend_forward(query, keys, values, bias, causal):
    query_heads, key_heads, value_heads = split_heads(query, keys, values)
    scores = scores_of(query_heads, key_heads, bias, causal)
    row_max = jnp.max(scores, axis=-1, keepdims=True)
    exponent = jnp.exp(scores - row_max)
    total = jnp.sum(exponent, axis=-1, keepdims=True)
    probs = (exponent / total).astype(jnp.bfloat16)
    mixed = jnp.einsum("bgrij,bjgd->bigrd", probs, value_heads, preferred_element_type=jnp.float32)
    return (mixed.reshape(query.shape).astype(jnp.bfloat16), row_max + jnp.log(total))


def attend_backward(query, keys, values, bias, causal, log_total, grad_mixed):
    query_heads, key_heads, value_heads = split_heads(query, keys, values)
    probs = jnp.exp(scores_of(query_heads, key_heads, bias, causal) - log_total)
    grad_heads = grad_mixed.reshape(query_heads.shape)
    grad_probs = jnp.einsum(
        "bigrd,bjgd->bgrij", grad_heads, value_heads, preferred_element_type=jnp.float32
    )
    inner = jnp.sum(probs * grad_probs, axis=-1, keepdims=True)
    grad_scores = (probs * (grad_probs - inner)).astype(jnp.bfloat16)
    scale = DH ** (-0.5)
    grad_query = (
        jnp.einsum("bgrij,bjgd->bigrd", grad_scores, key_heads, preferred_element_type=jnp.float32)
        * scale
    ).astype(jnp.bfloat16)
    grad_keys = (
        jnp.einsum(
            "bgrij,bigrd->bjgd", grad_scores, query_heads, preferred_element_type=jnp.float32
        )
        * scale
    ).astype(jnp.bfloat16)
    grad_values = jnp.einsum(
        "bgrij,bigrd->bjgd",
        probs.astype(jnp.bfloat16),
        grad_heads,
        preferred_element_type=jnp.float32,
    ).astype(jnp.bfloat16)
    return (
        grad_query.reshape(query.shape),
        grad_keys.reshape(keys.shape),
        grad_values.reshape(values.shape),
        grad_scores,
    )


def forward(tokens, memory, weights, onehot, causal):
    gains, table, self_q, self_kv, self_out, cross_q, cross_kv, cross_out, gate_up, down = weights
    gain_rows = gains.astype(jnp.float32)
    start = tokens.astype(jnp.float32)
    normed_self = rms_norm(start, gain_rows[0]).astype(jnp.bfloat16)
    query_self = jnp.dot(normed_self, self_q, preferred_element_type=jnp.float32).astype(
        jnp.bfloat16
    )
    pair_self = jnp.dot(normed_self, flatten(self_kv), preferred_element_type=jnp.float32).astype(
        jnp.bfloat16
    )
    half = pair_self.shape[-1] // 2
    keys_self = pair_self[..., :half]
    values_self = pair_self[..., half:]
    groups = half // DH
    heads = table.shape[1]
    rows = tokens.shape[1]
    bias = jnp.einsum("ijn,nh->hij", onehot, table, preferred_element_type=jnp.float32).reshape(
        groups, heads // groups, rows, rows
    )
    mixed_self, log_self = attend_forward(query_self, keys_self, values_self, bias, causal)
    after_self = start + branch_total(
        jnp.dot(mixed_self, self_out, preferred_element_type=jnp.float32)
    )
    normed_cross = rms_norm(after_self, gain_rows[1]).astype(jnp.bfloat16)
    query_cross = jnp.dot(normed_cross, cross_q, preferred_element_type=jnp.float32).astype(
        jnp.bfloat16
    )
    pair_cross = jnp.dot(memory, flatten(cross_kv), preferred_element_type=jnp.float32).astype(
        jnp.bfloat16
    )
    keys_cross = pair_cross[..., :half]
    values_cross = pair_cross[..., half:]
    mixed_cross, log_cross = attend_forward(query_cross, keys_cross, values_cross, None, None)
    after_cross = after_self + branch_total(
        jnp.dot(mixed_cross, cross_out, preferred_element_type=jnp.float32)
    )
    normed_ffn = rms_norm(after_cross, gain_rows[2]).astype(jnp.bfloat16)
    joined = jnp.dot(normed_ffn, flatten(gate_up), preferred_element_type=jnp.float32)
    hidden_width = joined.shape[-1] // 2
    gate = joined[..., :hidden_width]
    up = joined[..., hidden_width:]
    hidden = gelu_product(gate, up).astype(jnp.bfloat16)
    output = after_cross + branch_total(jnp.dot(hidden, down, preferred_element_type=jnp.float32))
    saved = (
        start,
        after_self,
        after_cross,
        normed_self,
        query_self,
        keys_self,
        values_self,
        bias,
        mixed_self,
        log_self,
        normed_cross,
        query_cross,
        keys_cross,
        values_cross,
        mixed_cross,
        log_cross,
        normed_ffn,
        gate,
        up,
        hidden,
    )
    return (output, saved)


def backward(saved, grad_out, memory, weights, onehot, causal):
    (
        start,
        after_self,
        after_cross,
        normed_self,
        query_self,
        keys_self,
        values_self,
        bias,
        mixed_self,
        log_self,
        normed_cross,
        query_cross,
        keys_cross,
        values_cross,
        mixed_cross,
        log_cross,
        normed_ffn,
        gate,
        up,
        hidden,
    ) = saved
    gains, table, self_q, self_kv, self_out, cross_q, cross_kv, cross_out, gate_up, down = weights
    gain_rows = gains.astype(jnp.float32)
    grad_ffn = grad_out.astype(jnp.float32)
    rounded = grad_ffn.astype(jnp.bfloat16)
    down_grad = jnp.einsum("blf,bld->fd", hidden, rounded, preferred_element_type=jnp.float32)
    grad_hidden = jnp.einsum("bld,fd->blf", rounded, down, preferred_element_type=jnp.float32)
    _, pull = jax.vjp(gelu_product, gate, up)
    grad_gate, grad_up = pull(grad_hidden)
    grad_joined = jnp.concatenate([grad_gate, grad_up], axis=-1).astype(jnp.bfloat16)
    gate_up_grad = jnp.einsum(
        "bld,blf->df", normed_ffn, grad_joined, preferred_element_type=jnp.float32
    ).reshape(gate_up.shape)
    grad_normed = input_total(
        jnp.einsum("blf,df->bld", grad_joined, flatten(gate_up), preferred_element_type=jnp.float32)
    )
    _, pull = jax.vjp(rms_norm, after_cross, gain_rows[2])
    grad_residual, gain_ffn = pull(grad_normed)
    grad_cross = grad_ffn + grad_residual
    rounded = grad_cross.astype(jnp.bfloat16)
    cross_out_grad = jnp.einsum(
        "blh,bld->hd", mixed_cross, rounded, preferred_element_type=jnp.float32
    )
    grad_mixed = jnp.einsum(
        "bld,hd->blh", rounded, cross_out, preferred_element_type=jnp.float32
    ).astype(jnp.bfloat16)
    grad_query, grad_keys, grad_values, _ = attend_backward(
        query_cross, keys_cross, values_cross, None, None, log_cross, grad_mixed
    )
    grad_pair_cross = jnp.concatenate([grad_keys, grad_values], axis=-1)
    cross_q_grad = jnp.einsum(
        "bld,blh->dh", normed_cross, grad_query, preferred_element_type=jnp.float32
    )
    cross_kv_grad = jnp.einsum(
        "bsd,bsw->dw", memory, grad_pair_cross, preferred_element_type=jnp.float32
    ).reshape(cross_kv.shape)
    grad_normed = input_total(
        jnp.einsum("blh,dh->bld", grad_query, cross_q, preferred_element_type=jnp.float32)
    )
    _, pull = jax.vjp(rms_norm, after_self, gain_rows[1])
    grad_residual, gain_cross = pull(grad_normed)
    grad_self = grad_cross + grad_residual
    rounded = grad_self.astype(jnp.bfloat16)
    self_out_grad = jnp.einsum(
        "blh,bld->hd", mixed_self, rounded, preferred_element_type=jnp.float32
    )
    grad_mixed = jnp.einsum(
        "bld,hd->blh", rounded, self_out, preferred_element_type=jnp.float32
    ).astype(jnp.bfloat16)
    grad_query, grad_keys, grad_values, grad_scores = attend_backward(
        query_self, keys_self, values_self, bias, causal, log_self, grad_mixed
    )
    batch = grad_scores.shape[0]
    rows = grad_scores.shape[-1]
    table_grad = jnp.einsum(
        "ijn,bhij->nh",
        onehot,
        grad_scores.reshape(batch, -1, rows, rows),
        preferred_element_type=jnp.float32,
    )
    grad_pair = jnp.concatenate([grad_keys, grad_values], axis=-1)
    self_q_grad = jnp.einsum(
        "bld,blh->dh", normed_self, grad_query, preferred_element_type=jnp.float32
    )
    self_kv_grad = jnp.einsum(
        "bld,blw->dw", normed_self, grad_pair, preferred_element_type=jnp.float32
    ).reshape(self_kv.shape)
    grad_normed = input_total(
        jnp.einsum("blh,dh->bld", grad_query, self_q, preferred_element_type=jnp.float32)
        + jnp.einsum("blw,dw->bld", grad_pair, flatten(self_kv), preferred_element_type=jnp.float32)
    )
    _, pull = jax.vjp(rms_norm, start, gain_rows[0])
    grad_residual, gain_self = pull(grad_normed)
    grad_tokens = grad_self + grad_residual
    gains_grad = jnp.stack([gain_self, gain_cross, gain_ffn])
    grads = (
        gains_grad,
        table_grad,
        self_q_grad,
        self_kv_grad,
        self_out_grad,
        cross_q_grad,
        cross_kv_grad,
        cross_out_grad,
        gate_up_grad,
        down_grad,
    )
    return (grad_tokens, grad_pair_cross, grads)


def per_device(
    decoder_in,
    memory,
    buckets,
    norm_gains,
    rel_bias,
    self_q,
    self_kv,
    self_out,
    cross_q,
    cross_kv,
    cross_out,
    gate_up,
    down,
    cotangent,
):
    local = decoder_in.shape[0]
    rows = decoder_in.shape[1]
    per_batch = local // MICRO
    positions = jnp.arange(rows, dtype=jnp.int32)
    causal = positions[:, None] >= positions[None, :]
    onehot = (buckets[:, :, None] == jnp.arange(NB, dtype=jnp.int32)[None, None, :]).astype(
        jnp.bfloat16
    )
    weights = gather_weights(
        norm_gains, rel_bias, self_q, self_kv, self_out, cross_q, cross_kv, cross_out, gate_up, down
    )
    outputs = []
    token_grads = []
    memory_grads = []
    totals = None
    for index in range(MICRO):
        lower = index * per_batch
        upper = lower + per_batch
        memory_part = memory[lower:upper]
        output, saved = forward(decoder_in[lower:upper], memory_part, weights, onehot, causal)
        grad_tokens, grad_pair_cross, grads = backward(
            saved, cotangent[lower:upper], memory_part, weights, onehot, causal
        )
        memory_term = jnp.einsum(
            "bsw,dw->bsd", grad_pair_cross, flatten(weights[6]), preferred_element_type=jnp.float32
        )
        memory_part_grad = lax.psum_scatter(
            memory_term.astype(jnp.bfloat16), "tp", scatter_dimension=2, tiled=True
        )
        memory_grads.append(memory_part_grad)
        outputs.append(output.astype(jnp.bfloat16))
        token_grads.append(grad_tokens)
        grads = (
            lax.psum_scatter(
                grads[0].astype(jnp.bfloat16), ("seq", "fsdp"), scatter_dimension=1, tiled=True
            ).astype(jnp.float32),
            lax.psum_scatter(
                grads[1].astype(jnp.bfloat16), ("seq", "fsdp"), scatter_dimension=0, tiled=True
            ).astype(jnp.float32),
            lax.psum_scatter(
                grads[2].astype(jnp.bfloat16), ("seq", "fsdp"), scatter_dimension=0, tiled=True
            ).astype(jnp.float32),
            lax.psum_scatter(
                grads[3].astype(jnp.bfloat16), ("seq", "fsdp"), scatter_dimension=0, tiled=True
            ).astype(jnp.float32),
            lax.psum_scatter(
                grads[4].astype(jnp.bfloat16), ("seq", "fsdp"), scatter_dimension=1, tiled=True
            ).astype(jnp.float32),
            lax.psum_scatter(
                grads[5].astype(jnp.bfloat16), ("seq", "fsdp"), scatter_dimension=0, tiled=True
            ).astype(jnp.float32),
            lax.psum_scatter(
                grads[6].astype(jnp.bfloat16), ("seq", "fsdp"), scatter_dimension=0, tiled=True
            ).astype(jnp.float32),
            lax.psum_scatter(
                grads[7].astype(jnp.bfloat16), ("seq", "fsdp"), scatter_dimension=1, tiled=True
            ).astype(jnp.float32),
            lax.psum_scatter(
                grads[8].astype(jnp.bfloat16), ("seq", "fsdp"), scatter_dimension=0, tiled=True
            ).astype(jnp.float32),
            lax.psum_scatter(
                grads[9].astype(jnp.bfloat16), ("seq", "fsdp"), scatter_dimension=1, tiled=True
            ).astype(jnp.float32),
        )
        totals = grads if totals is None else jax.tree.map(jnp.add, totals, grads)
    return (
        jnp.concatenate(outputs, axis=0),
        jnp.concatenate(token_grads, axis=0),
        jnp.concatenate(memory_grads, axis=0),
        totals[0],
        totals[1],
        totals[2],
        totals[3],
        totals[4],
        totals[5],
        totals[6],
        totals[7],
        totals[8],
        totals[9],
    )


def solution(mesh):
    return jax.shard_map(
        per_device,
        mesh=mesh,
        in_specs=(
            P(("seq", "fsdp"), None, None),
            P(("seq", "fsdp"), None, None),
            P(),
            P(None, ("seq", "fsdp")),
            P(("seq", "fsdp"), "tp"),
            P(("seq", "fsdp"), "tp"),
            P(("seq", "fsdp"), None, "tp"),
            P("tp", ("seq", "fsdp")),
            P(("seq", "fsdp"), "tp"),
            P(("seq", "fsdp"), None, "tp"),
            P("tp", ("seq", "fsdp")),
            P(("seq", "fsdp"), None, "tp"),
            P("tp", ("seq", "fsdp")),
            P(("seq", "fsdp"), None, None),
        ),
        out_specs=(
            P(("seq", "fsdp"), None, None),
            P(("seq", "fsdp"), None, None),
            P(("seq", "fsdp"), None, "tp"),
            P(None, ("seq", "fsdp")),
            P(("seq", "fsdp"), "tp"),
            P(("seq", "fsdp"), "tp"),
            P(("seq", "fsdp"), None, "tp"),
            P("tp", ("seq", "fsdp")),
            P(("seq", "fsdp"), "tp"),
            P(("seq", "fsdp"), None, "tp"),
            P("tp", ("seq", "fsdp")),
            P(("seq", "fsdp"), None, "tp"),
            P("tp", ("seq", "fsdp")),
        ),
        check_vma=False,
    )
```

profile of v0, /device:TPU:0, one launch (start us, length us, event | category | flops | bytes accessed | tf_op | source)
XLA Modules:
  0.0 1104.6 jit_solution(3590226312965783500)
XLA Ops:
  10.3 13.7 %all_gather.30 = bf16[3,1024]{1,0:T(4,128)(2,1)S(1)} all-gather(bf16[3,128]{1,0:T(4,128)(2,1)} %param.17), channel_id=1, replica_groups=mesh['seq'=4,'tp'=4,'fsdp'=2] {'seq','fsdp'}, dimensions={1}, use_global_device_ids=true | all-gather | bytes 6912 | tf_op jit(solution)/shard_map/all_gather | solution.py:31
  24.0 15.2 %all_gather.32 = bf16[1024,256]{1,0:T(8,128)(2,1)S(1)} all-gather(bf16[128,256]{1,0:T(8,128)(2,1)} %param.19), channel_id=1, replica_groups=mesh['seq'=4,'tp'=4,'fsdp'=2] {'seq','fsdp'}, dimensions={0}, use_global_device_ids=true | all-gather | bytes 589824 | tf_op jit(solution)/shard_map/all_gather | solution.py:33
  42.2 15.0 %all_gather.31 = bf16[1024,2,128]{2,1,0:T(2,128)(2,1)S(1)} all-gather(bf16[128,2,128]{2,1,0:T(2,128)(2,1)S(1)} %copy-done.72), channel_id=1, replica_groups=mesh['seq'=4,'tp'=4,'fsdp'=2] {'seq','fsdp'}, dimensions={0}, use_global_device_ids=true | all-gather | bytes 589824 | tf_op jit(solution)/shard_map/all_gather | solution.py:34
  58.3 8.7 all-gather
  68.0 13.9 %all_gather.34 = bf16[256,1024]{1,0:T(8,128)(2,1)S(1)} all-gather(bf16[256,128]{1,0:T(8,128)(2,1)S(1)} %copy-done.73), channel_id=1, replica_groups=mesh['seq'=4,'tp'=4,'fsdp'=2] {'seq','fsdp'}, dimensions={1}, use_global_device_ids=true | all-gather | bytes 589824 | tf_op jit(solution)/shard_map/all_gather | solution.py:35
  86.6 15.2 %all_gather.35 = bf16[1024,2,128]{2,1,0:T(2,128)(2,1)S(1)} all-gather(bf16[128,2,128]{2,1,0:T(2,128)(2,1)} %param.23), channel_id=1, replica_groups=mesh['seq'=4,'tp'=4,'fsdp'=2] {'seq','fsdp'}, dimensions={0}, use_global_device_ids=true | all-gather | bytes 589824 | tf_op jit(solution)/shard_map/all_gather | solution.py:37
  102.3 6.1 convolution_convert_fusion.2
  108.5 5.9 convolution_convert_fusion.3
  114.4 15.8 %all_gather.36 = bf16[1024,256]{1,0:T(8,128)(2,1)} all-gather(bf16[128,256]{1,0:T(8,128)(2,1)S(1)} %copy-done.74), channel_id=1, replica_groups=mesh['seq'=4,'tp'=4,'fsdp'=2] {'seq','fsdp'}, dimensions={0}, use_global_device_ids=true | all-gather | bytes 589824 | tf_op jit(solution)/shard_map/all_gather | solution.py:36
  130.2 14.4 %all_gather.37 = bf16[256,1024]{1,0:T(8,128)(2,1)S(1)} all-gather(bf16[256,128]{1,0:T(8,128)(2,1)S(1)} %copy-done.75), channel_id=1, replica_groups=mesh['seq'=4,'tp'=4,'fsdp'=2] {'seq','fsdp'}, dimensions={1}, use_global_device_ids=true | all-gather | bytes 589824 | tf_op jit(solution)/shard_map/all_gather | solution.py:38
  169.0 10.6 all-reduce.26.cloned.1.call-start
  179.6 39.7 %all-reduce.28.cloned.1.call-done = (bf16[2,128,1024]{2,1,0:T(8,128)(2,1)}, bf16[2,128,1024]{2,1,0:T(8,128)(2,1)}) async-done(((bf16[2,128,1024]{2,1,0:T(8,128)(2,1)}, bf16[2,128,1024]{2,1,0:T(8,128)(2,1)}), (bf16[2,128,1024]{2,1,0:T(8,128)(2,1)}, bf16[2,128,1024]{2,1,0:T(8,128)(2,1)})) %all-reduce.28.cloned.1.call-update) | async-done | bytes 1048592 | tf_op jit(solution)/shard_map/psum | solution.py:45
  221.9 3.9 fusion.203
  225.9 5.7 all-gather.6.cloned.1.call-done
  231.6 3.8 fusion.157
  243.6 51.4 %all-reduce.26.cloned.1.call-done = (bf16[2,128,1024]{2,1,0:T(8,128)(2,1)}, bf16[2,128,1024]{2,1,0:T(8,128)(2,1)}) async-done(((bf16[2,128,1024]{2,1,0:T(8,128)(2,1)}, bf16[2,128,1024]{2,1,0:T(8,128)(2,1)}), (bf16[2,128,1024]{2,1,0:T(8,128)(2,1)}, bf16[2,128,1024]{2,1,0:T(8,128)(2,1)})) %all-reduce.26.cloned.1.call-update) | async-done | bytes 1048592 | tf_op jit(solution)/shard_map/psum | solution.py:49
  307.3 9.1 fusion
  316.5 4.8 fusion.2
  325.2 4.4 fusion.3
  329.6 4.7 fusion.5
  339.5 2.9 fusion.82
  345.3 46.7 %all-reduce.24.cloned.1.call-done = (bf16[2,128,1024]{2,1,0:T(8,128)(2,1)}, bf16[2,128,1024]{2,1,0:T(8,128)(2,1)}) async-done(((bf16[2,128,1024]{2,1,0:T(8,128)(2,1)}, bf16[2,128,1024]{2,1,0:T(8,128)(2,1)}), (bf16[2,128,1024]{2,1,0:T(8,128)(2,1)}, bf16[2,128,1024]{2,1,0:T(8,128)(2,1)})) %all-reduce.24.cloned.1.call-update) | async-done | bytes 1048592 | tf_op jit(solution)/shard_map/psum | solution.py:49
  391.9 3.0 fusion.129
  396.4 3.7 fusion.132
  462.1 6.0 fusion.38
  470.4 4.6 fusion.37
  477.3 7.7 fusion.61
  488.3 6.0 fusion.41
  498.7 4.5 fusion.36
  510.0 7.2 fusion.64
  534.5 3.8 bitcast_convert_fusion
  538.4 3.8 bitcast_convert_fusion.1
  542.2 7.2 convolution_convert_fusion
  549.5 7.3 convolution_convert_fusion.1
  565.0 29.8 %all-reduce.6 = (bf16[32,4]{1,0:T(8,128)(2,1)S(1)}, bf16[32,4]{1,0:T(8,128)(2,1)S(1)}) all-reduce(bf16[32,4]{1,0:T(8,128)(2,1)S(1)} %fusion.118, bf16[32,4]{1,0:T(8,128)(2,1)S(1)} %fusion.117), channel_id=6, replica_groups=mesh['seq'=4,'tp'=4,'fsdp'=2] {'seq','fsdp'}, use_global_device_ids=true, to_apply=%region_47.48.clone | all-reduce | flops 256 | bytes 1024
  597.6 13.1 %reduce-scatter.67.cloned.1.call-done = bf16[128,704]{1,0:T(8,128)(2,1)} async-done(((bf16[1024,704]{1,0:T(8,128)(2,1)}), bf16[128,704]{1,0:T(8,128)(2,1)}) %reduce-scatter.67.cloned.1.call-update) | async-done | bytes 180240
  611.8 34.8 %reduce-scatter.65.cloned.1.call-done = bf16[128,704]{1,0:T(8,128)(2,1)} async-done(((bf16[1024,704]{1,0:T(8,128)(2,1)}), bf16[128,704]{1,0:T(8,128)(2,1)}) %reduce-scatter.65.cloned.1.call-update) | async-done | bytes 180240
  648.4 29.1 %reduce-scatter.53.cloned.1.call-done = bf16[128,256]{1,0:T(8,128)(2,1)} async-done(((bf16[1024,256]{1,0:T(8,128)(2,1)}), bf16[128,256]{1,0:T(8,128)(2,1)}) %reduce-scatter.53.cloned.1.call-update) | async-done | bytes 65552
  678.5 30.3 %reduce-scatter.55.cloned.1.call-done = bf16[128,256]{1,0:T(8,128)(2,1)} async-done(((bf16[1024,256]{1,0:T(8,128)(2,1)}), bf16[128,256]{1,0:T(8,128)(2,1)}) %reduce-scatter.55.cloned.1.call-update) | async-done | bytes 65552
  712.2 27.8 %reduce-scatter.41.cloned.1.call-done = bf16[128,256]{1,0:T(8,128)(2,1)} async-done(((bf16[1024,256]{1,0:T(8,128)(2,1)}), bf16[128,256]{1,0:T(8,128)(2,1)}) %reduce-scatter.41.cloned.1.call-update) | async-done | bytes 65552 | tf_op jit(solution)/shard_map/reduce_scatter | solution.py:356
  740.0 31.8 %reduce-scatter.43.cloned.1.call-done = bf16[128,256]{1,0:T(8,128)(2,1)} async-done(((bf16[1024,256]{1,0:T(8,128)(2,1)}), bf16[128,256]{1,0:T(8,128)(2,1)}) %reduce-scatter.43.cloned.1.call-update) | async-done | bytes 65552 | tf_op jit(solution)/shard_map/reduce_scatter | solution.py:356
  778.4 24.1 %reduce-scatter.49.cloned.1.call-done = bf16[128,3]{1,0:T(8,128)(2,1)} async-done(((bf16[1024,3]{1,0:T(8,128)(2,1)}), bf16[128,3]{1,0:T(8,128)(2,1)}) %reduce-scatter.49.cloned.1.call-update) | async-done | bytes 784
  803.3 30.5 %reduce-scatter.51.cloned.1.call-done = bf16[128,3]{1,0:T(8,128)(2,1)} async-done(((bf16[1024,3]{1,0:T(8,128)(2,1)}), bf16[128,3]{1,0:T(8,128)(2,1)}) %reduce-scatter.51.cloned.1.call-update) | async-done | bytes 784
  835.3 38.5 %reduce-scatter.63.cloned.1.call-done = bf16[128,1408]{1,0:T(8,128)(2,1)} async-done(((bf16[1024,1408]{1,0:T(8,128)(2,1)}), bf16[128,1408]{1,0:T(8,128)(2,1)}) %reduce-scatter.63.cloned.1.call-update) | async-done | bytes 360464
  874.9 38.9 %reduce-scatter.61.cloned.1.call-done = bf16[128,1408]{1,0:T(8,128)(2,1)} async-done(((bf16[1024,1408]{1,0:T(8,128)(2,1)}), bf16[128,1408]{1,0:T(8,128)(2,1)}) %reduce-scatter.61.cloned.1.call-update) | async-done | bytes 360464
  916.0 86.8 %reduce-scatter.39.cloned.1.call-done = bf16[2,2048,256]{2,1,0:T(8,128)(2,1)} async-done(((bf16[2,2048,1024]{2,1,0:T(8,128)(2,1)}), bf16[2,2048,256]{2,1,0:T(8,128)(2,1)}) %reduce-scatter.39.cloned.1.call-update) | async-done | bytes 2097168 | tf_op jit(solution)/shard_map/reduce_scatter | solution.py:343
  1002.8 89.3 %reduce-scatter.37.cloned.1.call-done = bf16[2,2048,256]{2,1,0:T(8,128)(2,1)} async-done(((bf16[2,2048,1024]{2,1,0:T(8,128)(2,1)}), bf16[2,2048,256]{2,1,0:T(8,128)(2,1)}) %reduce-scatter.37.cloned.1.call-update) | async-done | bytes 2097168 | tf_op jit(solution)/shard_map/reduce_scatter | solution.py:343
  1092.1 4.6 pad_maximum_fusion
  (435 shorter events, 199.5 us)
Async XLA Ops:
  8.0 49.5 %copy-start.2 = (bf16[4,128,1024]{2,1,0:T(8,128)(2,1)S(1)}, bf16[4,128,1024]{2,1,0:T(8,128)(2,1)}, u32[]{:S(2)}) copy-start(bf16[4,128,1024]{2,1,0:T(8,128)(2,1)} %param.14) | copy-start | bytes 3145732
  8.0 34.2 %copy-start.72 = (bf16[128,2,128]{2,1,0:T(2,128)(2,1)S(1)}, bf16[128,2,128]{2,1,0:T(2,128)(2,1)}, u32[]{:S(2)}) copy-start(bf16[128,2,128]{2,1,0:T(2,128)(2,1)} %param.20) | copy-start | bytes 196612
  8.0 139.4 %all-reduce.30.cloned.1.call-start = ((), (), s32[]{:S(2)}) async-start(), calls=%async_computation.39 | async-start | bytes 2097152 | tf_op jit(solution)/shard_map/psum | solution.py:45
  9.7 48.6 %copy-start.82 = (f32[2,128]{1,0:T(2,128)}, f32[2,128]{1,0:T(2,128)S(1)}, u32[]{:S(2)}) copy-start(f32[2,128]{1,0:T(2,128)S(1)} %fusion.204) | copy-start | bytes 3076
  10.3 48.1 %copy-start.84 = (f32[2,128]{1,0:T(2,128)}, f32[2,128]{1,0:T(2,128)S(1)}, u32[]{:S(2)}) copy-start(f32[2,128]{1,0:T(2,128)S(1)} %fusion.207) | copy-start | bytes 3076
  39.1 19.2 %copy-start.102 = (bf16[4,4]{1,0:T(4,128)(2,1)S(1)}, bf16[4,4]{1,0:T(4,128)(2,1)}, u32[]{:S(2)}) copy-start(bf16[4,4]{1,0:T(4,128)(2,1)} %param.18) | copy-start | bytes 100
  39.1 27.9 %copy-start.103 = (s32[128,128]{1,0:T(8,128)S(1)}, s32[128,128]{1,0:T(8,128)}, u32[]{:S(2)}) copy-start(s32[128,128]{1,0:T(8,128)} %param.16) | copy-start | bytes 196612
  40.8 27.3 %copy-start.73 = (bf16[256,128]{1,0:T(8,128)(2,1)S(1)}, bf16[256,128]{1,0:T(8,128)(2,1)}, u32[]{:S(2)}) copy-start(bf16[256,128]{1,0:T(8,128)(2,1)} %param.21) | copy-start | bytes 196612
  67.9 16.4 %copy-start.45 = (bf16[2,128,256]{1,2,0:T(8,128)(2,1)}, bf16[2,128,256]{1,2,0:T(8,128)(2,1)S(1)}, u32[]{:S(2)}) copy-start(bf16[2,128,256]{1,2,0:T(8,128)(2,1)S(1)} %copy.297) | copy-start | bytes 393220
  68.0 16.3 %copy-start.44 = (bf16[2,128,256]{1,2,0:T(8,128)(2,1)}, bf16[2,128,256]{1,2,0:T(8,128)(2,1)S(1)}, u32[]{:S(2)}) copy-start(bf16[2,128,256]{1,2,0:T(8,128)(2,1)S(1)} %copy.283) | copy-start | bytes 393220
  83.9 24.5 %copy-start.19 = (f32[2,2,2,128,128]{3,4,2,1,0:T(8,128)}, f32[2,2,2,128,128]{3,4,2,1,0:T(8,128)S(1)}, u32[]{:S(2)}) copy-start(f32[2,2,2,128,128]{3,4,2,1,0:T(8,128)S(1)} %get-tuple-element.87) | copy-start | bytes 1572868
  84.0 24.4 %copy-start.78 = (f32[2,2,2,128]{3,2,1,0:T(2,128)}, f32[2,2,2,128]{3,2,1,0:T(2,128)S(1)}, u32[]{:S(2)}) copy-start(f32[2,2,2,128]{3,2,1,0:T(2,128)S(1)} %fusion.177) | copy-start | bytes 12292
  84.3 24.1 %copy-start.48 = (bf16[2,2,64,2,128]{4,2,3,1,0:T(8,128)(2,1)}, bf16[2,2,64,2,128]{4,2,3,1,0:T(8,128)(2,1)S(1)}, u32[]{:S(2)}) copy-start(bf16[2,2,64,2,128]{4,2,3,1,0:T(8,128)(2,1)S(1)} %convolution_convert_fusion.22) | copy-start | bytes 393220
  86.6 132.7 %all-reduce.28.cloned.1.call-start = ((), (), s32[]{:S(2)}) async-start(), calls=%async_computation.38 | async-start | bytes 2097152 | tf_op jit(solution)/shard_map/psum | solution.py:45
  108.5 21.7 %copy-start.75 = (bf16[256,128]{1,0:T(8,128)(2,1)S(1)}, bf16[256,128]{1,0:T(8,128)(2,1)}, u32[]{:S(2)}) copy-start(bf16[256,128]{1,0:T(8,128)(2,1)} %param.24) | copy-start | bytes 196612
  144.6 22.1 %copy-start.16 = (bf16[256,1024]{1,0:T(8,128)(2,1)}, bf16[256,1024]{1,0:T(8,128)(2,1)S(1)}, u32[]{:S(2)}) copy-start(bf16[256,1024]{1,0:T(8,128)(2,1)S(1)} %all_gather.37) | copy-start | bytes 1572868
  166.7 52.6 %copy-start.52 = (bf16[2,2,64,2,128]{4,2,3,1,0:T(8,128)(2,1)}, bf16[2,2,64,2,128]{4,2,3,1,0:T(8,128)(2,1)S(1)}, u32[]{:S(2)}) copy-start(bf16[2,2,64,2,128]{4,2,3,1,0:T(8,128)(2,1)S(1)} %fusion.107) | copy-start | bytes 393220
  167.9 54.1 %all-gather.4.cloned.1.call-start = ((), (), s32[]{:S(2)}) async-start(), calls=%async_computation.16 | async-start | bytes 3244032 | tf_op jit(solution)/shard_map/all_gather | solution.py:39
  168.4 63.2 %all-gather.6.cloned.1.call-start = ((), (), s32[]{:S(2)}) async-start(), calls=%async_computation.17 | async-start | bytes 1622016 | tf_op jit(solution)/shard_map/all_gather | solution.py:40
  169.0 125.9 %all-reduce.26.cloned.1.call-start = ((), (), s32[]{:S(2)}) async-start(), calls=%async_computation.37 | async-start | bytes 2097152 | tf_op jit(solution)/shard_map/psum | solution.py:49
  221.4 14.1 %copy-start.91 = (f32[2,128]{1,0:T(2,128)}, f32[2,128]{1,0:T(2,128)S(1)}, u32[]{:S(2)}) copy-start(f32[2,128]{1,0:T(2,128)S(1)} %get-tuple-element.55) | copy-start | bytes 3076
  243.5 148.4 %all-reduce.24.cloned.1.call-start = ((), (), s32[]{:S(2)}) async-start(), calls=%async_computation.36 | async-start | bytes 2097152 | tf_op jit(solution)/shard_map/psum | solution.py:49
  339.0 190.7 %all-reduce.22.cloned.1.call-start = ((), (), s32[]{:S(2)}) async-start(), calls=%async_computation.35 | async-start | bytes 4194304 | tf_op jit(solution)/shard_map/psum | solution.py:45
  436.7 11.8 %copy-start.88 = (f32[2,128]{1,0:T(2,128)S(1)}, f32[2,128]{1,0:T(2,128)}, u32[]{:S(2)}) copy-start(f32[2,128]{1,0:T(2,128)} %copy-done.87) | copy-start | bytes 3076
  436.7 122.7 %reduce-scatter.57.cloned.1.call-start = ((), (), s32[]{:S(2)}) async-start(), calls=%async_computation.28 | async-start | bytes 589824
  441.2 119.2 %reduce-scatter.59.cloned.1.call-start = ((), (), s32[]{:S(2)}) async-start(), calls=%async_computation.29 | async-start | bytes 589824
  446.1 149.9 %reduce-scatter.47.cloned.1.call-start = ((), (), s32[]{:S(2)}) async-start(), calls=%async_computation.23 | async-start | bytes 589824 | tf_op jit(solution)/shard_map/reduce_scatter | solution.py:365
  448.5 147.5 %reduce-scatter.45.cloned.1.call-start = ((), (), s32[]{:S(2)}) async-start(), calls=%async_computation.22 | async-start | bytes 589824 | tf_op jit(solution)/shard_map/reduce_scatter | solution.py:365
  450.9 159.8 %reduce-scatter.67.cloned.1.call-start = ((), (), s32[]{:S(2)}) async-start(), calls=%async_computation.33 | async-start | bytes 1769472
  456.4 190.1 %reduce-scatter.65.cloned.1.call-start = ((), (), s32[]{:S(2)}) async-start(), calls=%async_computation.32 | async-start | bytes 1769472
  461.9 215.6 %reduce-scatter.53.cloned.1.call-start = ((), (), s32[]{:S(2)}) async-start(), calls=%async_computation.26 | async-start | bytes 589824
  488.3 220.5 %reduce-scatter.55.cloned.1.call-start = ((), (), s32[]{:S(2)}) async-start(), calls=%async_computation.27 | async-start | bytes 589824
  510.0 12.6 %copy-start.67 = (bf16[2,128,128]{2,1,0:T(8,128)(2,1)S(1)}, bf16[2,128,128]{2,1,0:T(8,128)(2,1)}, u32[]{:S(2)}) copy-start(bf16[2,128,128]{2,1,0:T(8,128)(2,1)} %copy.329) | copy-start | bytes 196612
  510.0 12.6 %copy-start.85 = (f32[2,128]{1,0:T(2,128)S(1)}, f32[2,128]{1,0:T(2,128)}, u32[]{:S(2)}) copy-start(f32[2,128]{1,0:T(2,128)} %copy-done.84) | copy-start | bytes 3076
  510.0 199.7 %all-reduce.20.cloned.1.call-start = ((), (), s32[]{:S(2)}) async-start(), calls=%async_computation.34 | async-start | bytes 4194304
  526.7 213.3 %reduce-scatter.41.cloned.1.call-start = ((), (), s32[]{:S(2)}) async-start(), calls=%async_computation.20 | async-start | bytes 589824 | tf_op jit(solution)/shard_map/reduce_scatter | solution.py:356
  528.0 243.8 %reduce-scatter.43.cloned.1.call-start = ((), (), s32[]{:S(2)}) async-start(), calls=%async_computation.21 | async-start | bytes 589824 | tf_op jit(solution)/shard_map/reduce_scatter | solution.py:356
  529.4 273.1 %reduce-scatter.49.cloned.1.call-start = ((), (), s32[]{:S(2)}) async-start(), calls=%async_computation.24 | async-start | bytes 294912
  533.4 300.4 %reduce-scatter.51.cloned.1.call-start = ((), (), s32[]{:S(2)}) async-start(), calls=%async_computation.25 | async-start | bytes 294912
  534.4 339.3 %reduce-scatter.63.cloned.1.call-start = ((), (), s32[]{:S(2)}) async-start(), calls=%async_computation.31 | async-start | bytes 3244032
  538.3 375.5 %reduce-scatter.61.cloned.1.call-start = ((), (), s32[]{:S(2)}) async-start(), calls=%async_computation.30 | async-start | bytes 3244032
  542.2 460.6 %reduce-scatter.39.cloned.1.call-start = ((), (), s32[]{:S(2)}) async-start(), calls=%async_computation.19 | async-start | bytes 10485760 | tf_op jit(solution)/shard_map/reduce_scatter | solution.py:343
  549.5 542.6 %reduce-scatter.37.cloned.1.call-start = ((), (), s32[]{:S(2)}) async-start(), calls=%async_computation.18 | async-start | bytes 10485760 | tf_op jit(solution)/shard_map/reduce_scatter | solution.py:343
  647.6 128.5 %copy-start.94 = (f32[2,128]{1,0:T(2,128)S(1)}, f32[2,128]{1,0:T(2,128)}, u32[]{:S(2)}) copy-start(f32[2,128]{1,0:T(2,128)} %copy-done.93) | copy-start | bytes 3076
  647.6 128.5 %copy-start.96 = (f32[2,128]{1,0:T(2,128)S(1)}, f32[2,128]{1,0:T(2,128)}, u32[]{:S(2)}) copy-start(f32[2,128]{1,0:T(2,128)} %copy-done.95) | copy-start | bytes 3076
  647.6 128.5 %copy-start.100 = (f32[2,128]{1,0:T(2,128)S(1)}, f32[2,128]{1,0:T(2,128)}, u32[]{:S(2)}) copy-start(f32[2,128]{1,0:T(2,128)} %get-tuple-element.22) | copy-start | bytes 3076
  647.6 128.5 %copy-start.101 = (f32[2,128]{1,0:T(2,128)S(1)}, f32[2,128]{1,0:T(2,128)}, u32[]{:S(2)}) copy-start(f32[2,128]{1,0:T(2,128)} %get-tuple-element.25) | copy-start | bytes 3076
  647.7 128.5 %copy-start.86 = (f32[2,128]{1,0:T(2,128)S(1)}, f32[2,128]{1,0:T(2,128)}, u32[]{:S(2)}) copy-start(f32[2,128]{1,0:T(2,128)} %copy-done.84) | copy-start | bytes 3076
  (85 other events, 415.4 us)
Sparse Core Ops, SparseCore 0:
  86.7 51.2 all-reduce.29
  168.0 51.2 all-reduce.27
  243.7 51.2 all-reduce.25
  339.2 52.7 all-reduce.23
  436.8 70.1 all-reduce.21
  526.8 75.9 all-reduce.19
Sparse Core Ops, SparseCore 1:
  169.9 35.4 all-gather.3
  206.8 24.7 all-gather.5
  441.3 30.8 reduce-scatter.56
  474.5 28.9 reduce-scatter.58
  505.9 28.9 reduce-scatter.46
  537.1 31.4 reduce-scatter.44
  571.5 39.1 reduce-scatter.66
  613.0 33.5 reduce-scatter.64
  648.8 28.7 reduce-scatter.52
  679.8 28.9 reduce-scatter.54
  711.0 29.0 reduce-scatter.40
  742.9 28.9 reduce-scatter.42
  774.0 28.4 reduce-scatter.48
  805.3 28.4 reduce-scatter.50
  836.8 36.8 reduce-scatter.62
  876.2 37.6 reduce-scatter.60
  917.2 85.5 reduce-scatter.38
  1005.9 86.2 reduce-scatter.36
where the time goes:
time: 1120 us; the launch traced here: 1100 us
  waiting for transfers between devices  620 us (55%)
  matrix products  177 us (16%)
  blocking collectives  142 us (13%)
  local copies, waits for them, and re-layouts  77 us (7%)
  other arithmetic  57.6 us (5%)
  between operations  19.1 us (2%)
  starting transfers between devices  12.4 us (1%)
    unnamed x35, waiting for transfers between devices  241 us
    reduce_scatter x2, waiting for transfers between devices, per_device(): lax.psum_scatter(memory_term.astype(jnp.bfloat16), 'tp', scatter_dimensio...  176 us
    psum x2, waiting for transfers between devices, input_total(): lax.psum(partial_value.astype(jnp.bfloat16), 'tp').astype(jnp.float32)  98 us
    reduce_scatter x2, waiting for transfers between devices, per_device(): lax.psum_scatter(grads[2].astype(jnp.bfloat16), ('seq', 'fsdp'), scatter_...  59.6 us
    unnamed x237, local copies, waits for them, and re-layouts  41 us
    psum x3, waiting for transfers between devices, branch_total(): lax.psum(partial_value.astype(jnp.bfloat16), 'tp').astype(jnp.float32)  39.7 us
    unnamed x1, blocking collectives  29.8 us
  transfers between devices with their start and end apart: 24, of which 16 were waited for; matrix products, arithmetic and copies ran while one was open for 16% of the time, Pallas kernels for 0%

commit v1 on v0

--- a/solution.py
+++ b/solution.py
@@ -1,6 +1,8 @@
 import jax
 import jax.numpy as jnp
 from jax import lax
+from jax.experimental import pallas as pl
+from jax.experimental.pallas import tpu as pltpu
 from jax.sharding import PartitionSpec as P
 
 DH = 64
@@ -396,9 +398,878 @@
     )
 
 
+GROUP = 128
+
+
+def lane_blocks(value):
+    count = value.shape[1] // GROUP
+    return jnp.concatenate(
+        [value[:, b * GROUP : (b + 1) * GROUP] for b in range(count)], axis=0
+    )
+
+
+def dot(left, right):
+    return jnp.dot(left, right, preferred_element_type=jnp.float32)
+
+
+def dot_t(left, right):
+    return lax.dot_general(left, right, (((1,), (1,)), ((), ())), preferred_element_type=jnp.float32)
+
+
+def t_dot(left, right):
+    return lax.dot_general(left, right, (((0,), (0,)), ((), ())), preferred_element_type=jnp.float32)
+
+
+def low(value):
+    return value.astype(jnp.bfloat16)
+
+
+def high(value):
+    return value.astype(jnp.float32)
+
+
+def norm_backward(values, gain, cotangent):
+    _, pull = jax.vjp(rms_norm, values, gain)
+    return pull(cotangent)
+
+
+def stacked(block, pair, lanes):
+    block = high(block[:, pair * GROUP : (pair + 1) * GROUP])
+    other = pltpu.roll(block, DH, 1)
+    if pair == 0:
+        rows = jnp.concatenate([block, other], axis=0)
+        keep = lanes < DH
+    else:
+        rows = jnp.concatenate([other, block], axis=0)
+        keep = lanes >= DH
+    return low(jnp.where(keep, rows, 0.0))
+
+
+def unstacked(parts):
+    heads = []
+    for pair, value in enumerate(parts):
+        half = value[:, pair * DH : (pair + 1) * DH]
+        heads += [half[0:GROUP], half[GROUP : 2 * GROUP]]
+    return jnp.concatenate(heads, axis=1)
+
+
+def cross_forward_kernel(q_ref, kv_ref, o_ref, lse_ref, scores, probs):
+    span = kv_ref.shape[0]
+    chunk = 256
+    lanes = lax.broadcasted_iota(jnp.int32, (1, GROUP), 1)
+    outs = []
+    for pair in range(2):
+        query = stacked(q_ref[...], pair, lanes)
+
+        def first(index, best):
+            rows = pl.ds(index * chunk, chunk)
+            part = dot_t(kv_ref[rows, 0:GROUP], query)
+            scores[rows, :] = part
+            return jnp.maximum(best, jnp.max(part, axis=0, keepdims=True))
+
+        best = lax.fori_loop(
+            0, span // chunk, first, jnp.full((1, 2 * GROUP), MASKED, jnp.float32), unroll=2
+        )
+
+        def second(index, total):
+            rows = pl.ds(index * chunk, chunk)
+            part = jnp.exp(scores[rows, :] - best)
+            probs[rows, :] = low(part)
+            return total + jnp.sum(part, axis=0, keepdims=True)
+
+        total = lax.fori_loop(
+            0, span // chunk, second, jnp.zeros((1, 2 * GROUP), jnp.float32), unroll=2
+        )
+        mixed = t_dot(kv_ref[:, GROUP : 2 * GROUP], probs[...])
+        outs.append((mixed / total).T)
+        lse_ref[0, pair : pair + 1, :] = best + jnp.log(total)
+    o_ref[...] = low(unstacked(outs))
+
+
+def inner_of(dout, out):
+    return jnp.sum((high(dout) * high(out)).T, axis=0, keepdims=True)
+
+
+def cross_backward_kernel(q_ref, do_ref, o_ref, kv_ref, lse_ref, dq_ref, dkv_ref, probs, grads):
+    span = kv_ref.shape[0]
+    chunk = 256
+    lanes = lax.broadcasted_iota(jnp.int32, (1, GROUP), 1)
+    queries = []
+    douts = []
+    for pair in range(2):
+        query = stacked(q_ref[...], pair, lanes)
+        dout = stacked(do_ref[...], pair, lanes)
+        inner = inner_of(dout, stacked(o_ref[...], pair, lanes))
+        lse = lse_ref[0, pair : pair + 1, :]
+        columns = slice(pair * 2 * GROUP, (pair + 1) * 2 * GROUP)
+
+        def step(index, carry):
+            rows = pl.ds(index * chunk, chunk)
+            prob = jnp.exp(dot_t(kv_ref[rows, 0:GROUP], query) - lse)
+            grad = prob * (dot_t(kv_ref[rows, GROUP : 2 * GROUP], dout) - inner)
+            probs[rows, columns] = low(prob)
+            grads[rows, columns] = low(grad)
+            return carry
+
+        lax.fori_loop(0, span // chunk, step, 0, unroll=2)
+        queries.append(query)
+        douts.append(dout)
+    query = jnp.concatenate(queries, axis=0)
+    dout = jnp.concatenate(douts, axis=0)
+    dkv_ref[:, 0:GROUP] = low(dot(grads[...], query))
+    dkv_ref[:, GROUP : 2 * GROUP] = low(dot(probs[...], dout))
+    dq = (t_dot(kv_ref[:, 0:GROUP], grads[...]) * DH ** (-0.5)).T
+    dq_ref[...] = low(unstacked([dq[0 : 2 * GROUP], dq[2 * GROUP :]]))
+
+
+def self_scores(kv_ref, query, bias_ref, pair):
+    rows = kv_ref.shape[0]
+    scores = dot_t(kv_ref[:, 0:GROUP], query)
+    scores = scores + jnp.concatenate([bias_ref[2 * pair], bias_ref[2 * pair + 1]], axis=1)
+    key_at = lax.broadcasted_iota(jnp.int32, scores.shape, 0)
+    query_at = lax.broadcasted_iota(jnp.int32, scores.shape, 1) % rows
+    return scores, key_at <= query_at
+
+
+def self_forward_kernel(q_ref, kv_ref, bias_ref, o_ref, lse_ref):
+    lanes = lax.broadcasted_iota(jnp.int32, (1, GROUP), 1)
+    outs = []
+    for pair in range(2):
+        query = stacked(q_ref[...], pair, lanes)
+        scores, seen = self_scores(kv_ref, query, bias_ref, pair)
+        scores = jnp.where(seen, scores, MASKED)
+        best = jnp.max(scores, axis=0, keepdims=True)
+        part = jnp.exp(scores - best)
+        total = jnp.sum(part, axis=0, keepdims=True)
+        mixed = t_dot(kv_ref[:, GROUP : 2 * GROUP], low(part / total))
+        outs.append(mixed.T)
+        lse_ref[0, pair : pair + 1, :] = best + jnp.log(total)
+    o_ref[...] = low(unstacked(outs))
+
+
+def self_backward_kernel(
+    q_ref, do_ref, o_ref, kv_ref, lse_ref, bias_ref, dq_ref, dkv_ref, ds_ref
+):
+    lanes = lax.broadcasted_iota(jnp.int32, (1, GROUP), 1)
+    dqs = []
+    dk = 0.0
+    dv = 0.0
+    for pair in range(2):
+        query = stacked(q_ref[...], pair, lanes)
+        dout = stacked(do_ref[...], pair, lanes)
+        inner = inner_of(dout, stacked(o_ref[...], pair, lanes))
+        scores, seen = self_scores(kv_ref, query, bias_ref, pair)
+        prob = jnp.exp(jnp.where(seen, scores - lse_ref[0, pair : pair + 1, :], MASKED))
+        grad = low(prob * (dot_t(kv_ref[:, GROUP : 2 * GROUP], dout) - inner))
+        ds_ref[2 * pair] = grad[:, 0:GROUP]
+        ds_ref[2 * pair + 1] = grad[:, GROUP : 2 * GROUP]
+        dk = dk + dot(grad, query)
+        dv = dv + dot(low(prob), dout)
+        dqs.append((t_dot(kv_ref[:, 0:GROUP], grad) * DH ** (-0.5)).T)
+    dkv_ref[:, 0:GROUP] = low(dk)
+    dkv_ref[:, GROUP : 2 * GROUP] = low(dv)
+    dq_ref[...] = low(unstacked(dqs))
+
+
+def attention_specs(rows, span):
+    narrow = pl.BlockSpec((rows, 2 * GROUP), lambda k: (0, k))
+    tall = pl.BlockSpec((span, 2 * GROUP), lambda k: (0, k))
+    lse = pl.BlockSpec((1, 2, 2 * GROUP), lambda k: (k, 0, 0))
+    square = pl.BlockSpec((4, rows, rows), lambda k: (k, 0, 0))
+    return narrow, tall, lse, square
+
+
+def kernel_call(kernel, name, blocks, specs, outs, scratch, cost, arguments, limit=32):
+    return pl.pallas_call(
+        kernel,
+        grid=(blocks,),
+        in_specs=specs,
+        out_specs=[spec for spec, _, _ in outs],
+        out_shape=[jax.ShapeDtypeStruct(shape, kind) for _, shape, kind in outs],
+        scratch_shapes=scratch,
+        compiler_params=pltpu.CompilerParams(vmem_limit_bytes=limit * 2**20),
+        cost_estimate=pl.CostEstimate(flops=cost[0], bytes_accessed=cost[1], transcendentals=cost[2]),
+        name=name,
+    )(*arguments)
+
+
+def attention_forward(query, pairs, bias):
+    rows, span = query.shape[0], pairs.shape[0]
+    blocks = query.shape[1] // (2 * GROUP)
+    narrow, tall, lse, square = attention_specs(rows, span)
+    cost = (
+        16 * rows * span * DH * blocks,
+        2 * (2 * query.size + pairs.size),
+        4 * rows * span * blocks,
+    )
+    outs = [
+        (narrow, query.shape, jnp.bfloat16),
+        (lse, (blocks, 2, 2 * GROUP), jnp.float32),
+    ]
+    if bias is not None:
+        return kernel_call(
+            self_forward_kernel,
+            "self_forward",
+            blocks,
+            [narrow, tall, square],
+            outs,
+            [],
+            cost,
+            (query, pairs, bias),
+        )
+    return kernel_call(
+        cross_forward_kernel,
+        "cross_forward",
+        blocks,
+        [narrow, tall],
+        outs,
+        [
+            pltpu.VMEM((span, 2 * GROUP), jnp.float32),
+            pltpu.VMEM((span, 2 * GROUP), jnp.bfloat16),
+        ],
+        cost,
+        (query, pairs),
+    )
+
+
+def attention_backward(query, dout, out, pairs, lse_value, bias):
+    rows, span = query.shape[0], pairs.shape[0]
+    blocks = query.shape[1] // (2 * GROUP)
+    narrow, tall, lse, square = attention_specs(rows, span)
+    cost = (
+        40 * rows * span * DH * blocks,
+        2 * (4 * query.size + 2 * pairs.size),
+        4 * rows * span * blocks,
+    )
+    outs = [(narrow, query.shape, jnp.bfloat16), (tall, pairs.shape, jnp.bfloat16)]
+    if bias is not None:
+        return kernel_call(
+            self_backward_kernel,
+            "self_backward",
+            blocks,
+            [narrow, narrow, narrow, tall, lse, square],
+            outs + [(square, (4 * blocks, rows, rows), jnp.bfloat16)],
+            [],
+            cost,
+            (query, dout, out, pairs, lse_value, bias),
+        )
+    return kernel_call(
+        cross_backward_kernel,
+        "cross_backward",
+        blocks,
+        [narrow, narrow, narrow, tall, lse],
+        outs,
+        [pltpu.VMEM((span, 4 * GROUP), jnp.bfloat16)] * 2,
+        cost,
+        (query, dout, out, pairs, lse_value),
+    )
+
+
+def with_index(kernel, name, grid, specs, outs, scratch, cost, index, arguments, limit=32):
+    return pl.pallas_call(
+        kernel,
+        grid_spec=pltpu.PrefetchScalarGridSpec(
+            num_scalar_prefetch=1,
+            grid=grid,
+            in_specs=specs,
+            out_specs=[spec for spec, _, _ in outs],
+            scratch_shapes=scratch,
+        ),
+        out_shape=[jax.ShapeDtypeStruct(shape, kind) for _, shape, kind in outs],
+        compiler_params=pltpu.CompilerParams(vmem_limit_bytes=limit * 2**20),
+        cost_estimate=pl.CostEstimate(flops=cost[0], bytes_accessed=cost[1], transcendentals=0),
+        name=name,
+    )(index, *arguments)
+
+
+def unpack_heads(index, near, far, depth, top, rows_first, width, extra):
+    tp = near[0].shape[0]
+    listed = isinstance(far[0], list)
+    seq = (far[0][0].shape[0] if listed else far[0].shape[1]) + 1
+    shard = width // (2 * seq)
+    sides = tuple(far[0]) + tuple(far[1]) if listed else tuple(far)
+
+    def kernel(index_ref, *refs):
+        near_refs, far_refs = refs[0:2], refs[2 : 2 + len(sides)]
+        outs = refs[2 + len(sides) :]
+
+        def place(q, side, read):
+            row = 2 * (index_ref[0] ^ q) + (index_ref[2] ^ side)
+            at = pl.ds(pl.multiple_of(row * shard, shard), shard)
+            for entry, (out, down) in enumerate(zip(outs, rows_first)):
+                start = entry * 2 * shard
+                if down:
+                    out[:, at] = read(start, 2 * shard)
+                else:
+                    for b in range(2):
+                        out[at, b * GROUP : (b + 1) * GROUP] = read(start + b * shard, shard)
+            if extra:
+                outs[-1][0, row] = read(depth - extra, extra)
+
+        for side in range(2):
+            place(0, side, lambda start, size: near_refs[side][0, top + start : top + start + size, :])
+            for q in range(1, seq):
+                if listed:
+                    for k in range(tp):
+
+                        @pl.when(pl.program_id(0) == k)
+                        def _():
+                            ref = far_refs[side * tp + k]
+                            place(q, side, lambda start, size: ref[q - 1, start : start + size, :])
+
+                else:
+                    place(
+                        q,
+                        side,
+                        lambda start, size: far_refs[side][0, q - 1, start : start + size, :],
+                    )
+
+    specs = [pl.BlockSpec((1,) + near[0].shape[1:], lambda k, index: (k ^ index[1], 0, 0))] * 2
+    for value in sides:
+        if listed:
+            specs.append(pl.BlockSpec(value.shape, lambda k, index: (0, 0, 0)))
+        else:
+            specs.append(
+                pl.BlockSpec((1,) + value.shape[1:], lambda k, index: (k ^ index[1], 0, 0, 0))
+            )
+    outs = []
+    for down in rows_first:
+        if down:
+            spec = pl.BlockSpec((2 * GROUP, width), lambda k, index: (k, 0))
+            outs.append((spec, (tp * 2 * GROUP, width), jnp.bfloat16))
+        else:
+            spec = pl.BlockSpec((width, 2 * GROUP), lambda k, index: (0, k))
+            outs.append((spec, (width, tp * 2 * GROUP), jnp.bfloat16))
+    if extra:
+        spec = pl.BlockSpec((1, 2 * seq, extra, GROUP), lambda k, index: (k, 0, 0, 0))
+        outs.append((spec, (tp, 2 * seq, extra, GROUP), jnp.bfloat16))
+    return with_index(
+        kernel,
+        "unpack_heads",
+        (tp,),
+        specs,
+        outs,
+        [],
+        (0, 8 * tp * seq * depth * GROUP),
+        index,
+        (*near, *sides),
+    )
+
+
+def unpack_hidden(value, width, hidden_width):
+    count = value.shape[0]
+    shard = width // count
+    columns = 2 * hidden_width // GROUP
+
+    def kernel(in_ref, gate_up_ref, down_ref):
+        for b in range(columns):
+            gate_up_ref[:, b * GROUP : (b + 1) * GROUP] = in_ref[0, b * shard : (b + 1) * shard, :]
+        down_ref[...] = in_ref[0, columns * shard :, :]
+
+    return kernel_call(
+        kernel,
+        "unpack_hidden",
+        count,
+        [pl.BlockSpec((1, value.shape[1], GROUP), lambda k: (k, 0, 0))],
+        [
+            (
+                pl.BlockSpec((shard, 2 * hidden_width), lambda k: (k, 0)),
+                (width, 2 * hidden_width),
+                jnp.bfloat16,
+            ),
+            (
+                pl.BlockSpec((hidden_width, shard), lambda k: (0, k)),
+                (hidden_width, width),
+                jnp.bfloat16,
+            ),
+        ],
+        [],
+        (0, 4 * value.size, 0),
+        (value,),
+    )
+
+
+def memory_terms(index, pairs, weight, tp):
+    rows, width = pairs.shape
+    features = weight.shape[0] // tp
+    steps = 4
+    block = rows // steps
+
+    def kernel(index_ref, pairs_ref, weight_ref, *outs):
+        for k, out in enumerate(outs):
+            at = pl.multiple_of((index_ref[1] ^ k) * features, features)
+            out[...] = low(dot_t(pairs_ref[...], weight_ref[pl.ds(at, features), :]))
+
+    spec = pl.BlockSpec((block, features), lambda k, index: (k, 0))
+    return with_index(
+        kernel,
+        "memory_terms",
+        (steps,),
+        [
+            pl.BlockSpec((block, width), lambda k, index: (k, 0)),
+            pl.BlockSpec(weight.shape, lambda k, index: (0, 0)),
+        ],
+        [(spec, (rows, features), jnp.bfloat16)] * tp,
+        [],
+        (2 * rows * width * weight.shape[0], 2 * (2 * pairs.size + weight.size)),
+        index,
+        (pairs, weight),
+    )
+
+
+def hidden_out(index, hidden, weight, values, tp):
+    rows = hidden.shape[0] // tp
+    width = weight.shape[1]
+
+    def kernel(index_ref, hidden_ref, weight_ref, values_ref, out_ref):
+        part = dot(hidden_ref[...], weight_ref[...])
+
+        @pl.when(pl.program_id(0) == 0)
+        def _():
+            out_ref[0] = low(part + values_ref[...])
+
+        @pl.when(pl.program_id(0) != 0)
+        def _():
+            out_ref[0] = low(part)
+
+    return with_index(
+        kernel,
+        "hidden_out",
+        (tp,),
+        [
+            pl.BlockSpec((rows, hidden.shape[1]), lambda k, index: (k, 0)),
+            pl.BlockSpec(weight.shape, lambda k, index: (0, 0)),
+            pl.BlockSpec(values.shape, lambda k, index: (0, 0)),
+        ],
+        [
+            (
+                pl.BlockSpec((1, rows, width), lambda k, index: (k ^ index[1], 0, 0)),
+                (tp, rows, width),
+                jnp.bfloat16,
+            )
+        ],
+        [],
+        (2 * hidden.size * width, 2 * (hidden.size + weight.size + tp * rows * width)),
+        index,
+        (hidden, weight, values),
+    )[0]
+
+
+def row_terms(index, seq, name, pairs):
+    rows = pairs[0][0].shape[-2]
+    width = pairs[0][0].shape[-1]
+    shard = width // (2 * seq)
+    columns = sum(right.shape[1] for _, right in pairs)
+
+    def row_of(step, index):
+        return 2 * (index[0] ^ (step % seq)) + (index[2] ^ (1 - step // seq))
+
+    def kernel(index_ref, *refs):
+        sent_ref, kept_ref = refs[-2:]
+        parts = []
+        for entry in range(len(pairs)):
+            left, right = refs[2 * entry], refs[2 * entry + 1]
+            left = left[0] if len(left.shape) == 3 else left[...]
+            parts.append(t_dot(left, right[...]))
+
+        def put(ref, kind):
+            at = 0
+            for part in parts:
+                ref[0, :, at : at + part.shape[1]] = part.astype(kind)
+                at += part.shape[1]
+
+        @pl.when(pl.program_id(0) < seq)
+        def _():
+            put(sent_ref, jnp.bfloat16)
+
+        @pl.when(pl.program_id(0) >= seq)
+        def _():
+            put(kept_ref, jnp.float32)
+
+    specs = []
+    arguments = []
+    for left, right in pairs:
+        if left.ndim == 3:
+            specs.append(
+                pl.BlockSpec((1, rows, shard), lambda s, index: (index[1], 0, row_of(s, index)))
+            )
+        else:
+            specs.append(pl.BlockSpec((rows, shard), lambda s, index: (0, row_of(s, index))))
+        specs.append(pl.BlockSpec(right.shape, lambda s, index: (0, 0)))
+        arguments += [left, right]
+    shape = (seq, shard, columns)
+    block = (1, shard, columns)
+    return with_index(
+        kernel,
+        name,
+        (2 * seq,),
+        specs,
+        [
+            (
+                pl.BlockSpec(block, lambda s, index: (jnp.minimum(s, seq - 1), 0, 0)),
+                shape,
+                jnp.bfloat16,
+            ),
+            (
+                pl.BlockSpec(block, lambda s, index: (jnp.maximum(s - seq, 0), 0, 0)),
+                shape,
+                jnp.float32,
+            ),
+        ],
+        [],
+        (2 * rows * width * columns, 2 * rows * (width + columns) + 3 * width * columns),
+        index,
+        tuple(arguments),
+    )
+
+
+def hidden_terms(normed, grad_joined, rounded, hidden):
+    rows, width = normed.shape
+    columns = grad_joined.shape[1] + hidden.shape[1]
+    split = grad_joined.shape[1]
+    steps = width // GROUP
+
+    def kernel(normed_ref, joined_ref, rounded_ref, hidden_ref, out_ref):
+        out_ref[:, :split] = low(t_dot(normed_ref[...], joined_ref[...]))
+        out_ref[:, split:] = low(t_dot(rounded_ref[...], hidden_ref[...]))
+
+    left = pl.BlockSpec((rows, GROUP), lambda k: (0, k))
+    return kernel_call(
+        kernel,
+        "hidden_terms",
+        steps,
+        [
+            left,
+            pl.BlockSpec(grad_joined.shape, lambda k: (0, 0)),
+            left,
+            pl.BlockSpec(hidden.shape, lambda k: (0, 0)),
+        ],
+        [(pl.BlockSpec((GROUP, columns), lambda k: (k, 0)), (width, columns), jnp.bfloat16)],
+        [],
+        (2 * rows * width * columns, 4 * rows * (width + columns) + 2 * width * columns, 0),
+        (normed, grad_joined, rounded, hidden),
+    )[0]
+
+
+def one_each(seq, tp):
+    everyone = ("seq", "tp", "fsdp")
+
+    def after(value, *earlier):
+        return lax.optimization_barrier((value, earlier))[0]
+
+    def swap(value, axis, flip):
+        size = {"seq": seq, "tp": tp, "fsdp": 2}[axis]
+        return lax.ppermute(value, axis, [(place, place ^ flip) for place in range(size)])
+
+    def gather(value, axis, size):
+        return [value] + [swap(value, axis, flip) for flip in range(1, size)]
+
+    def exchange(parts, axis):
+        return [parts[0]] + [swap(parts[k], axis, k) for k in range(1, len(parts))]
+
+    def exchange_all(value):
+        return lax.all_to_all(value, "tp", 0, 0, tiled=True)
+
+    def to_everyone(value):
+        return exchange_all(jnp.broadcast_to(value[None], (tp,) + value.shape))
+
+    def total(parts):
+        result = high(parts[0])
+        for part in parts[1:]:
+            result = result + high(part)
+        return result
+
+    def run(
+        decoder_in,
+        memory,
+        buckets,
+        norm_gains,
+        rel_bias,
+        self_q,
+        self_kv,
+        self_out,
+        cross_q,
+        cross_kv,
+        cross_out,
+        gate_up,
+        down,
+        cotangent,
+    ):
+        count, rows, width = decoder_in.shape
+        z = lax.axis_index("seq")
+        t = lax.axis_index("tp")
+        c = lax.axis_index("fsdp")
+        index = jnp.stack([z, t, c]).astype(jnp.int32)
+        cores = 2
+        shard = self_q.shape[0]
+        tables = rel_bias.shape[0]
+        heads = rel_bias.shape[1]
+        hidden_width = down.shape[0]
+        extra = 16
+
+        def own(value):
+            return lax.dynamic_index_in_dim(value, t, 0, keepdims=False)
+
+        def from_here(value):
+            return [
+                lax.dynamic_index_in_dim(value, t ^ k, 0, keepdims=False) for k in range(tp)
+            ]
+
+        def in_order(parts, kind):
+            result = jnp.zeros((count,) + parts[0].shape, kind)
+            for k, part in enumerate(parts):
+                result = lax.dynamic_update_index_in_dim(result, part.astype(kind), t ^ k, 0)
+            return result
+
+        def head_blocks(value):
+            size = value.shape[1] // tp
+            return [value[:, k * size : (k + 1) * size] for k in range(tp)]
+
+        small = jnp.concatenate(
+            [
+                norm_gains,
+                jnp.pad(rel_bias.reshape(1, -1), ((0, 0), (0, GROUP - rel_bias.size))),
+                jnp.zeros((extra - 4, GROUP), jnp.bfloat16),
+            ],
+            axis=0,
+        )
+        pack_a = jnp.concatenate(
+            [lane_blocks(flatten(cross_kv)), lane_blocks(self_q), lane_blocks(flatten(self_kv)), small],
+            axis=0,
+        )
+        pack_b = jnp.concatenate([self_out, lane_blocks(cross_q), cross_out], axis=0)
+        pack_f = jnp.concatenate([lane_blocks(flatten(gate_up)), down], axis=0)
+
+        depth_a, depth_b = pack_a.shape[0], pack_b.shape[0]
+        near = to_everyone(jnp.concatenate([pack_a, pack_b], axis=0))
+        ring_a = gather(pack_a, "seq", seq)
+        ring_b = gather(after(pack_b, *ring_a), "seq", seq)
+        far_a = to_everyone(after(jnp.stack(ring_a[1:]), near))
+        far_b = gather(after(jnp.stack(ring_b[1:]), far_a), "tp", tp)
+        full_f = lax.all_gather(after(pack_f, *ring_b), ("seq", "fsdp"), axis=0, tiled=True)
+        near = [near, swap(near, "fsdp", 1)]
+        far_a = [far_a, swap(far_a, "fsdp", 1)]
+
+        cross_pairs, weight_self_q, weight_self_kv, smalls = unpack_heads(
+            index, near, far_a, depth_a, 0, (False, False, False), width, extra
+        )
+        weight_gate_up, weight_down = unpack_hidden(
+            full_f.reshape(seq * cores, -1, GROUP), width, hidden_width
+        )
+        gain_rows = high(smalls[0, :, 0:3].transpose(1, 0, 2).reshape(3, width))
+        table = smalls[:, :, 3, 0 : tables * heads].reshape(tp, seq * cores, tables, heads)
+        table = table.transpose(1, 2, 0, 3).reshape(NB, tp * heads)
+        onehot = (
+            buckets.T[:, :, None] == jnp.arange(NB, dtype=jnp.int32)[None, None, :]
+        ).astype(jnp.bfloat16)
+        bias = jnp.einsum("jin,nh->hji", onehot, table, preferred_element_type=jnp.float32)
+
+        pairs = low(dot(own(memory), cross_pairs))
+        start = high(own(decoder_in))
+        scale = DH ** (-0.5)
+
+        normed_self = low(rms_norm(start, gain_rows[0]))
+        query_self = low(dot(normed_self, weight_self_q) * scale)
+        pair_self = low(dot(normed_self, weight_self_kv))
+        mixed_self, log_self = attention_forward(query_self, pair_self, bias)
+        far_b = [after(part, mixed_self, pairs) for part in far_b]
+        far_b = [far_b, [swap(part, "fsdp", 1) for part in far_b]]
+        weight_self_out, weight_cross_q, weight_cross_out = unpack_heads(
+            index, near, far_b, depth_b, depth_a, (True, False, True), width, 0
+        )
+        after_self = start + dot(mixed_self, weight_self_out)
+
+        normed_cross = low(rms_norm(after_self, gain_rows[1]))
+        query_cross = low(dot(normed_cross, weight_cross_q) * scale)
+        mixed_cross, log_cross = attention_forward(query_cross, pairs, None)
+        after_cross = after_self + dot(mixed_cross, weight_cross_out)
+        normed_ffn = low(rms_norm(after_cross, gain_rows[2]))
+
+        all_cross = lax.all_gather(normed_cross, "tp", axis=0, tiled=True)
+        all_normed = jnp.concatenate(gather(normed_ffn, "tp", tp), axis=0)
+        rounded = jnp.concatenate(from_here(cotangent), axis=0)
+        joined = dot(all_normed, weight_gate_up)
+        gate = joined[:, :hidden_width]
+        up = joined[:, hidden_width:]
+        grad_hidden = dot_t(rounded, weight_down)
+        hidden = low(gelu_product(gate, up))
+        _, pull = jax.vjp(gelu_product, gate, up)
+        grad_gate, grad_up = pull(grad_hidden)
+        grad_joined = low(jnp.concatenate([grad_gate, grad_up], axis=-1))
+
+        def row_parts(value):
+            return [value[k * rows : (k + 1) * rows] for k in range(tp)]
+
+        grad_parts = exchange(row_parts(low(dot_t(grad_joined, weight_gate_up))), "tp")
+        hidden_grads = hidden_terms(all_normed, grad_joined, rounded, hidden)
+        partial_out = hidden_out(index, hidden, weight_down, after_cross, tp)
+        grad_normed = total([after(grad_parts[0], hidden_grads, partial_out)] + grad_parts[1:])
+        decoder_out = lax.psum(after(partial_out, *grad_parts), "tp")
+        hidden_grads = high(
+            lax.psum_scatter(hidden_grads, ("seq", "fsdp"), scatter_dimension=0, tiled=True)
+        )
+
+        grad_residual, gain_ffn = norm_backward(after_cross, gain_rows[2], grad_normed)
+        grad_cross = high(rounded[:rows]) + grad_residual
+        rounded_cross = low(grad_cross)
+        grad_mixed = low(dot_t(rounded_cross, weight_cross_out))
+        cross_parts = exchange(
+            [
+                jnp.concatenate([rounded_cross, o_self, o_cross], axis=1)
+                for o_self, o_cross in zip(head_blocks(mixed_self), head_blocks(mixed_cross))
+            ],
+            "tp",
+        )
+        grad_query, grad_pairs = attention_backward(
+            query_cross, grad_mixed, mixed_cross, pairs, log_cross, None
+        )
+        grad_normed = dot_t(grad_query, weight_cross_q)
+        grad_residual, gain_cross = norm_backward(after_self, gain_rows[1], grad_normed)
+        grad_self = grad_cross + grad_residual
+        rounded_self = low(grad_self)
+        self_parts = exchange(
+            after(
+                [
+                    jnp.concatenate([rounded_self, block], axis=1)
+                    for block in head_blocks(grad_query)
+                ],
+                *cross_parts,
+            ),
+            "tp",
+        )
+
+        grad_mixed_self = low(dot_t(rounded_self, weight_self_out))
+        grad_query_self, grad_pair_self, grad_scores = attention_backward(
+            query_self, after(grad_mixed_self, *cross_parts), mixed_self, pair_self, log_self, bias
+        )
+        grad_normed = dot_t(grad_query_self, weight_self_q) + dot_t(grad_pair_self, weight_self_kv)
+        grad_residual, gain_self = norm_backward(start, gain_rows[0], grad_normed)
+        grad_tokens = low(grad_self + grad_residual)
+        last_parts = [
+            jnp.concatenate([grad_tokens, q_block, kv_block], axis=1)
+            for q_block, kv_block in zip(head_blocks(grad_query_self), head_blocks(grad_pair_self))
+        ]
+        grad_pairs = after(grad_pairs, *last_parts, *self_parts)
+        last_parts = exchange(after(last_parts, *self_parts), "tp")
+        decoder_grad = in_order([part[:, :width] for part in last_parts], jnp.float32)
+
+        memory_grad = in_order(
+            exchange(after(memory_terms(index, grad_pairs, cross_pairs, tp), *last_parts), "tp"),
+            jnp.bfloat16,
+        )
+
+        def core_sum(name, *terms):
+            sent, kept = row_terms(index, seq, name, terms)
+            return kept + high(swap(sent, "fsdp", 1))
+
+        kv_rows = core_sum("memory_weights", (memory, grad_pairs))
+        step = seq // 2
+        while step:
+            kv_rows = kv_rows[:step] + high(swap(low(kv_rows[step:]), "seq", step))
+            step //= 2
+        kv_rows = kv_rows[0]
+        cross_kv_grad = total(
+            exchange([kv_rows[:, : 2 * GROUP]] + head_blocks(low(kv_rows))[1:], "tp")
+        )
+        all_back = jnp.concatenate(cross_parts, axis=0)
+        all_self = jnp.concatenate(self_parts, axis=0)
+        all_last = jnp.concatenate([part[:, width:] for part in last_parts], axis=0)
+        cross_grads = core_sum(
+            "cross_weights",
+            (jnp.concatenate(from_here(all_cross.reshape(tp, rows, width)), axis=0), all_self[:, width:]),
+            (all_back[:, :width], all_back[:, width + 2 * GROUP :]),
+        )
+        all_start = low(
+            rms_norm(high(jnp.concatenate(from_here(decoder_in), axis=0)), gain_rows[0])
+        )
+        self_grads = core_sum(
+            "self_weights",
+            (all_start, all_last),
+            (all_self[:, :width], all_back[:, width : width + 2 * GROUP]),
+        )
+
+        both_grads = low(jnp.concatenate([cross_grads, self_grads], axis=2))
+        both_grads = jnp.concatenate(
+            [
+                lax.dynamic_index_in_dim(both_grads, z ^ k, 0, keepdims=True) for k in range(seq)
+            ],
+            axis=0,
+        )
+        both_grads = jnp.sum(
+            high(lax.all_to_all(both_grads, "seq", 0, 0, tiled=True)), axis=0
+        )
+        cross_grads = both_grads[:, : 4 * GROUP]
+        self_grads = both_grads[:, 4 * GROUP :]
+
+        table_grad = jnp.einsum(
+            "jin,hji->nh", onehot, grad_scores, preferred_element_type=jnp.float32
+        )
+        gains = jnp.stack([gain_self, gain_cross, gain_ffn])
+        gain_parts = gains.reshape(3, seq, 1, cores, GROUP).transpose(1, 2, 3, 0, 4)
+        gain_parts = jnp.broadcast_to(gain_parts, (seq, tp, cores, 3, GROUP))
+        table_parts = table_grad.reshape(seq, cores, tables, tp, heads)
+        table_parts = jnp.stack(
+            [
+                lax.dynamic_index_in_dim(table_parts, t ^ k, 3, keepdims=False)
+                for k in range(tp)
+            ],
+            axis=1,
+        )
+        table_parts = jnp.pad(
+            table_parts.reshape(seq, tp, cores, 1, -1),
+            ((0, 0),) * 4 + ((0, GROUP - tables * heads),),
+        )
+        little = jnp.concatenate([gain_parts, table_parts], axis=3)
+        little = jnp.pad(low(little), ((0, 0),) * 3 + ((0, 4), (0, 0)))
+        little = lax.all_to_all(
+            after(little.reshape(-1, 8, GROUP), both_grads), everyone, 0, 0, tiled=True
+        )
+        little = jnp.sum(high(little), axis=0)
+
+        return (
+            decoder_out,
+            decoder_grad,
+            memory_grad,
+            little[0:3],
+            little[3, 0 : tables * heads].reshape(tables, heads),
+            self_grads[:, 0 : 2 * GROUP],
+            self_grads[:, 2 * GROUP : 4 * GROUP].reshape(self_kv.shape),
+            self_grads[:, 4 * GROUP :].T,
+            cross_grads[:, 0 : 2 * GROUP],
+            cross_kv_grad.reshape(cross_kv.shape),
+            cross_grads[:, 2 * GROUP :].T,
+            hidden_grads[:, : 2 * hidden_width].reshape(gate_up.shape),
+            hidden_grads[:, 2 * hidden_width :].T,
+        )
+
+    return run
+
+
+def plan_of(mesh):
+    seq, tp, cores = (mesh.shape[axis] for axis in ("seq", "tp", "fsdp"))
+
+    def chosen(*arrays):
+        count, rows, width = arrays[0].shape
+        fits = (
+            cores == 2
+            and seq & (seq - 1) == 0
+            and tp & (tp - 1) == 0
+            and count == tp
+            and rows == GROUP
+            and width == 2 * seq * GROUP
+            and arrays[5].shape[1] == 4 * DH
+            and arrays[6].shape[2] == 2 * DH
+            and arrays[4].size <= GROUP
+            and 2 * arrays[12].shape[0] % GROUP == 0
+        )
+        return (one_each(seq, tp) if fits else per_device)(*arrays)
+
+    return chosen
+
+
 def solution(mesh):
     return jax.shard_map(
-        per_device,
+        plan_of(mesh),
         mesh=mesh,
         in_specs=(
             P(("seq", "fsdp"), None, None),

time: 1120 us -> 404 us (0.36)
  waiting for transfers between devices: 620 us -> 110 us
  matrix products: 177 us -> 28.2 us
  blocking collectives: 142 us -> 0 us
  Pallas kernels: 0 us -> 84.7 us
  starting transfers between devices: 12.4 us -> 63.4 us
  other arithmetic: 57.6 us -> 27.4 us
    unnamed x35 -> x4, waiting for transfers between devices: 241 us -> 0.07 us
    reduce_scatter x6 -> x1, waiting for transfers between devices: 236 us -> 0.01 us  [run(): lax.psum_scatter(hidden_grads, ('seq', 'fsdp'), scatter_dimension=0, tile...]
    dot_general x75 -> x16, matrix products: 177 us -> 28.2 us  [the longest x7 16.4 us: dot(): return jnp.dot(left, right, preferred_element_type=jnp.float32)]
    psum x5 -> x1, waiting for transfers between devices: 138 us -> 0.01 us  [run(): decoder_out = lax.psum(after(partial_out, *grad_parts), 'tp')]
    all_gather x8 -> x0, blocking collectives: 112 us -> none  [the longest x1 15.8 us: gather_weights(): lax.all_gather(cross_q, ('seq', 'fsdp'), axis=0, tiled=True)]
    ppermute x0 -> x41, waiting for transfers between devices: none -> 99.9 us  [swap(): lax.ppermute(value, axis, [(place, place ^ flip) for place in range(size)])]
    pallas_call x0 -> x13, Pallas kernels: none -> 84.7 us  [the longest x6 48.5 us: kernel_call(): pl.pallas_call(kernel, grid=(blocks,), in_specs=specs, out_specs=[spec fo...]
    ppermute x0 -> x41, starting transfers between devices: none -> 44.4 us  [swap(): lax.ppermute(value, axis, [(place, place ^ flip) for place in range(size)])]
  transfers between devices with their start and end apart: 24 -> 49, of which waited for: 16 -> 20; matrix products, arithmetic and copies ran while one was open for 16% -> 23% of each run, Pallas kernels for 0% -> 21%
where the time goes in v1:
time: 404 us; the launch traced here: 398 us
  waiting for transfers between devices  110 us (27%)
  Pallas kernels  84.7 us (21%)
  local copies, waits for them, and re-layouts  68 us (17%)
  starting transfers between devices  63.4 us (16%)
  matrix products  28.2 us (7%)
  other arithmetic  27.4 us (7%)
  between operations  15.9 us (4%)
    ppermute x41, waiting for transfers between devices, swap(): lax.ppermute(value, axis, [(place, place ^ flip) for place in range(size)])  99.9 us
    pallas_call x6, Pallas kernels, kernel_call(): pl.pallas_call(kernel, grid=(blocks,), in_specs=specs, out_specs=[spec fo...  48.5 us
    ppermute x41, starting transfers between devices, swap(): lax.ppermute(value, axis, [(place, place ^ flip) for place in range(size)])  44.4 us
    pallas_call x7, Pallas kernels, with_index(): pl.pallas_call(kernel, grid_spec=pltpu.PrefetchScalarGridSpec(num_scalar_...  36.2 us
    unnamed x220, local copies, waits for them, and re-layouts  30.7 us
    dot_general x7, matrix products, dot(): return jnp.dot(left, right, preferred_element_type=jnp.float32)  16.4 us
    dot_general x7, matrix products, dot_t(): lax.dot_general(left, right, (((1,), (1,)), ((), ())), preferred_element_...  9.99 us
    all_to_all x2, starting transfers between devices, exchange_all(): return lax.all_to_all(value, 'tp', 0, 0, tiled=True)  9.81 us
  transfers between devices with their start and end apart: 49, of which 20 were waited for; matrix products, arithmetic and copies ran while one was open for 23% of the time, Pallas kernels for 21%

profile of v1, /device:TPU:0, one launch (start us, length us, event | category | flops | bytes accessed | tf_op | source)
XLA Modules:
  0.0 398.0 jit_solution(5465338911328004763)
XLA Ops:
  11.3 2.6 concatenate.88
  15.2 5.2 %all-to-all-start = ((bf16[4,1552,128]{2,1,0:T(8,128)(2,1)}), bf16[4,1552,128]{2,1,0:T(8,128)(2,1)S(1)}, u32[]{:S(2)}, u32[]{:S(2)}) async-start(bf16[4,1552,128]{2,1,0:T(8,128)(2,1)} %broadcast_in_dim.85), calls=%async_computation | async-start | bytes 3178496 | tf_op jit(solution)/shard_map/all_to_all | solution.py:971
  22.3 2.6 collective-permute-start.2
  25.1 5.4 %collective-permute-done.1 = bf16[784,128]{1,0:T(8,128)(2,1)S(1)} collective-permute-done((bf16[784,128]{1,0:T(8,128)(2,1)S(1)}, bf16[784,128]{1,0:T(8,128)(2,1)S(1)}, u32[]{:S(2)}, u32[]{:S(2)}) %collective-permute-start.1) | collective-permute-done | bytes 200736 | tf_op jit(solution)/shard_map/ppermute | solution.py:962
  30.5 9.2 %collective-permute-done.2 = bf16[784,128]{1,0:T(8,128)(2,1)S(1)} collective-permute-done((bf16[784,128]{1,0:T(8,128)(2,1)S(1)}, bf16[784,128]{1,0:T(8,128)(2,1)S(1)}, u32[]{:S(2)}, u32[]{:S(2)}) %collective-permute-start.2) | collective-permute-done | bytes 200736 | tf_op jit(solution)/shard_map/ppermute | solution.py:962
  41.6 4.6 %all-to-all-start.1 = ((bf16[4,3,784,128]{3,2,1,0:T(8,128)(2,1)}), bf16[4,3,784,128]{3,2,1,0:T(8,128)(2,1)}, u32[]{:S(2)}, u32[]{:S(2)}) async-start(bf16[4,3,784,128]{3,2,1,0:T(8,128)(2,1)} %broadcast_in_dim.86), calls=%async_computation.1 | async-start | bytes 4816896 | tf_op jit(solution)/shard_map/all_to_all | solution.py:971
  47.9 3.3 collective-permute-start.5
  53.8 3.6 collective-permute-done.5
  57.4 10.4 %collective-permute-done.6 = bf16[768,128]{1,0:T(8,128)(2,1)S(1)} collective-permute-done((bf16[768,128]{1,0:T(8,128)(2,1)S(1)}, bf16[768,128]{1,0:T(8,128)(2,1)S(1)}, u32[]{:S(2)}, u32[]{:S(2)}) %collective-permute-start.6) | collective-permute-done | bytes 196640 | tf_op jit(solution)/shard_map/ppermute | solution.py:962
  67.9 6.1 %all-to-all-done.1.refs_2_ = bf16[4,3,784,128]{3,2,1,0:T(8,128)(2,1)} async-done(((bf16[4,3,784,128]{3,2,1,0:T(8,128)(2,1)}), bf16[4,3,784,128]{3,2,1,0:T(8,128)(2,1)}, u32[]{:S(2)}, u32[]{:S(2)}) %all-to-all-start.1) | async-done | bytes 2408480 | tf_op jit(solution)/shard_map/all_to_all | solution.py:971
  74.8 2.4 copy.108
  83.7 5.5 %unpack_heads.2 = (bf16[1024,1024]{1,0:T(8,128)(2,1)S(1)}, bf16[1024,1024]{1,0:T(8,128)(2,1)S(1)}, bf16[1024,1024]{1,0:T(8,128)(2,1)S(1)}, bf16[4,8,16,128]{3,2,1,0:T(8,128)(2,1)S(1)}) custom-call(s32[3]{0:T(128)S(1)} %pad_add_fusion.index_ref, bf16[4,1552,128]{2,1,0:T(8,128)(2,1)S(1)} %all-to-all-done.refs_0_, ...), custom_call_target="tpu_custom_call" | custom-call | bytes 12845056 | tf_op jit(solution)/shard_map/unpack_heads/pallas_call | solution.py:669
  97.4 3.7 self_forward.1
  101.1 8.4 %fusion.3.kv_ref = bf16[2048,1024]{1,0:T(8,128)(2,1)} fusion(bf16[1024,1024]{1,0:T(8,128)(2,1)S(1)} %copy-done.39, bf16[4,2048,1024]{2,1,0:T(8,128)(2,1)} %refs_0_.1, s32[]{:T(128)S(6)} %select_n.52), kind=kOutput, calls=%fused_computation.3 | convolution fusion | flops 4297064448 | bytes 10485764 | tf_op jit(solution)/shard_map/dot_general | solution.py:412
  114.6 5.3 %unpack_heads.3 = (bf16[1024,1024]{1,0:T(8,128)(2,1)S(1)}, bf16[1024,1024]{1,0:T(8,128)(2,1)S(1)}, bf16[1024,1024]{1,0:T(8,128)(2,1)S(1)}) custom-call(s32[3]{0:T(128)S(1)} %pad_add_fusion.index_ref, bf16[4,1552,128]{2,1,0:T(8,128)(2,1)S(1)} %all-to-all-done.refs_0_, bf16[4,1552,128]{2,1,0:T(8,128)(2,1)} %collective-permute-done.refs_1_, ...), custom_call_target="tpu_custom_call" | custom-call | bytes 12582912 | tf_op jit(solution)/shard_map/unpack_heads/pallas_call | solution.py:669
  126.3 2.2 copy-done.41
  128.5 15.9 %cross_forward.1 = (bf16[128,1024]{1,0:T(8,128)(2,1)S(1)}, f32[4,2,256]{2,1,0:T(2,128)S(1)}) custom-call(bf16[128,1024]{1,0:T(8,128)(2,1)S(1)} %fusion.17.q_ref, bf16[2048,1024]{1,0:T(8,128)(2,1)S(1)} %copy-done.41), custom_call_target="tpu_custom_call" | custom-call | flops 1073741824 | bytes 4718592 | tf_op jit(solution)/shard_map/cross_forward/pallas_call | solution.py:583
  150.1 5.3 %collective-permute-done.17 = bf16[128,1024]{1,0:T(8,128)(2,1)} collective-permute-done((bf16[128,1024]{1,0:T(8,128)(2,1)S(1)}, bf16[128,1024]{1,0:T(8,128)(2,1)}, u32[]{:S(2)}, u32[]{:S(2)}) %collective-permute-start.17) | collective-permute-done | bytes 262176 | tf_op jit(solution)/shard_map/ppermute | solution.py:962
  155.4 4.8 %collective-permute-done.16 = bf16[128,1024]{1,0:T(8,128)(2,1)} collective-permute-done((bf16[128,1024]{1,0:T(8,128)(2,1)S(1)}, bf16[128,1024]{1,0:T(8,128)(2,1)}, u32[]{:S(2)}, u32[]{:S(2)}) %collective-permute-start.16) | collective-permute-done | bytes 262176 | tf_op jit(solution)/shard_map/ppermute | solution.py:962
  162.5 2.2 copy-done.15
  166.0 3.7 fusion.53
  169.7 3.0 fusion.15
  174.5 4.8 %hidden_terms.1 = bf16[1024,2112]{1,0:T(8,128)(2,1)S(1)} custom-call(bf16[512,1024]{1,0:T(8,128)(2,1)S(1)} %copy-done.17, bf16[512,1408]{1,0:T(8,128)(2,1)S(1)} %pad_maximum_fusion.1.joined_ref, bf16[512,1024]{1,0:T(8,128)(2,1)S(1)} %copy-done.16, bf16[512,704]{1,0:T(8,128)(2,1)S(1)} %get-tuple-element.187.hidden_ref), custom_call_target="tpu_custom_call" | custom-call | flops 2214592512 | bytes 10747904 | tf_op jit(solution)/shard_map/hidden_terms/pallas_call | solution.py:583
  196.0 2.5 hidden_out.1
  201.3 4.4 %collective-permute-done.20 = bf16[128,1024]{1,0:T(8,128)(2,1)} collective-permute-done((bf16[128,1024]{1,0:T(8,128)(2,1)}, bf16[128,1024]{1,0:T(8,128)(2,1)}, u32[]{:S(2)}, u32[]{:S(2)}) %collective-permute-start.20) | collective-permute-done | bytes 262176 | tf_op jit(solution)/shard_map/ppermute | solution.py:962
  207.2 2.5 fusion.58
  215.2 19.4 %cross_backward.1 = (bf16[128,1024]{1,0:T(8,128)(2,1)S(1)}, bf16[2048,1024]{1,0:T(8,128)(2,1)S(1)}) custom-call(bf16[128,1024]{1,0:T(8,128)(2,1)S(1)} %copy-done.35, bf16[128,1024]{1,0:T(8,128)(2,1)S(1)} %convolution_convert_fusion.2.do_ref, bf16[128,1024]{1,0:T(8,128)(2,1)S(1)} %copy-done.33, bf16[2048,1024]{1,0:T(8,128)(2,1)S(1)} %copy-done.42, ...), custom_call_target="tpu_custom_call" | custom-call | flops 2684354560 | bytes 9437184 | tf_op jit(solution)/shard_map/cross_backward/pallas_call | solution.py:583
  238.4 2.3 fusion.56
  242.8 3.5 self_backward.1
  263.5 7.7 %collective-permute-done.26 = bf16[128,1280]{1,0:T(8,128)(2,1)} collective-permute-done((bf16[128,1280]{1,0:T(8,128)(2,1)}, bf16[128,1280]{1,0:T(8,128)(2,1)}, u32[]{:S(2)}, u32[]{:S(2)}) %collective-permute-start.26) | collective-permute-done | bytes 327712 | tf_op jit(solution)/shard_map/ppermute | solution.py:962
  273.8 2.5 collective-permute-start.29
  276.3 3.7 cross_weights.1
  280.2 8.9 %memory_weights.1 = (bf16[4,128,1024]{2,1,0:T(8,128)(2,1)S(1)}, f32[4,128,1024]{2,1,0:T(8,128)S(1)}) custom-call(s32[3]{0:T(128)S(1)} %pad_add_fusion.index_ref, bf16[4,2048,1024]{2,1,0:T(8,128)(2,1)} %refs_0_.1, bf16[2048,1024]{1,0:T(8,128)(2,1)S(1)} %copy-done.20), custom_call_target="tpu_custom_call" | custom-call | flops 4294967296 | bytes 11534336 | tf_op jit(solution)/shard_map/memory_weights/pallas_call | solution.py:669
  289.7 6.1 %memory_terms.1 = (bf16[2048,256]{1,0:T(8,128)(2,1)S(1)}, bf16[2048,256]{1,0:T(8,128)(2,1)S(1)}, bf16[2048,256]{1,0:T(8,128)(2,1)S(1)}, bf16[2048,256]{1,0:T(8,128)(2,1)S(1)}) custom-call(s32[3]{0:T(128)S(1)} %pad_add_fusion.index_ref, bf16[2048,1024]{1,0:T(8,128)(2,1)S(1)} %copy-done.20, bf16[1024,1024]{1,0:T(8,128)(2,1)S(1)} %copy-done.40), custom_call_target="tpu_custom_call" | custom-call | flops 4294967296 | bytes 10485760 | tf_op jit(solution)/shard_map/memory_terms/pallas_call | solution.py:669
  297.0 4.1 %self_weights.1 = (bf16[4,128,768]{2,1,0:T(8,128)(2,1)S(1)}, f32[4,128,768]{2,1,0:T(8,128)S(1)}) custom-call(s32[3]{0:T(128)S(1)} %pad_add_fusion.index_ref, bf16[512,1024]{1,0:T(8,128)(2,1)S(1)} %copy-done.30, bf16[512,512]{1,0:T(8,128)(2,1)S(1)} %pad_maximum_fusion.9.refs_1_, bf16[512,1024]{1,0:T(8,128)(2,1)S(1)} %slice.368.refs_2_, ...), custom_call_target="tpu_custom_call" | custom-call | flops 805306368 | bytes 4194304 | tf_op jit(solution)/shard_map/self_weights/pallas_call | solution.py:669
  301.8 2.6 collective-permute-start.32
  305.9 3.0 collective-permute-start.36
  310.4 4.3 %all-to-all-start.2 = ((bf16[4,128,1280]{2,1,0:T(8,128)(2,1)}), bf16[4,128,1280]{2,1,0:T(8,128)(2,1)}, u32[]{:S(2)}, u32[]{:S(2)}) async-start(bf16[4,128,1280]{2,1,0:T(8,128)(2,1)} %pad_maximum_fusion.2), calls=%async_computation.2 | async-start | bytes 2621440 | tf_op jit(solution)/shard_map/all_to_all | solution.py:1199
  314.8 8.7 %collective-permute-done.30 = bf16[2048,256]{1,0:T(8,128)(2,1)} collective-permute-done((bf16[2048,256]{1,0:T(8,128)(2,1)S(1)}, bf16[2048,256]{1,0:T(8,128)(2,1)}, u32[]{:S(2)}, u32[]{:S(2)}) %collective-permute-start.30) | collective-permute-done | bytes 1048608 | tf_op jit(solution)/shard_map/ppermute | solution.py:962
  323.5 2.3 bitcast_dynamic-update-slice_fusion.2
  325.8 21.5 %collective-permute-done.36 = bf16[2,128,1024]{2,1,0:T(8,128)(2,1)} collective-permute-done((bf16[2,128,1024]{2,1,0:T(8,128)(2,1)}, bf16[2,128,1024]{2,1,0:T(8,128)(2,1)}, u32[]{:S(2)}, u32[]{:S(2)}) %collective-permute-start.36) | collective-permute-done | bytes 524320 | tf_op jit(solution)/shard_map/ppermute | solution.py:962
  349.0 2.3 bitcast_dynamic-update-slice_fusion.1
  351.2 11.9 %collective-permute-done.37 = bf16[1,128,1024]{2,1,0:T(8,128)(2,1)S(1)} collective-permute-done((bf16[1,128,1024]{2,1,0:T(8,128)(2,1)S(1)}, bf16[1,128,1024]{2,1,0:T(8,128)(2,1)S(1)}, u32[]{:S(2)}, u32[]{:S(2)}) %collective-permute-start.37) | collective-permute-done | bytes 262176 | tf_op jit(solution)/shard_map/ppermute | solution.py:962
  363.2 2.4 collective-permute-start.40
  366.8 2.3 bitcast_dynamic-update-slice_fusion
  372.2 4.8 %all-to-all-start.3 = ((bf16[32,8,128]{2,1,0:T(8,128)(2,1)}), bf16[32,8,128]{2,1,0:T(8,128)(2,1)S(1)}, u32[]{:S(2)}, u32[]{:S(2)}) async-start(bf16[32,8,128]{2,1,0:T(8,128)(2,1)} %bitcast.40), calls=%async_computation.3 | async-start | bytes 131072 | tf_op jit(solution)/shard_map/all_to_all | solution.py:1224
  380.1 4.3 %all-to-all-done.3 = bf16[32,8,128]{2,1,0:T(8,128)(2,1)S(1)} async-done(((bf16[32,8,128]{2,1,0:T(8,128)(2,1)}), bf16[32,8,128]{2,1,0:T(8,128)(2,1)S(1)}, u32[]{:S(2)}, u32[]{:S(2)}) %all-to-all-start.3) | async-done | bytes 65568 | tf_op jit(solution)/shard_map/all_to_all | solution.py:1224
  389.0 2.3 copy.173
  (426 shorter events, 121.7 us)
Async XLA Ops:
  15.2 24.6 %all-to-all-start = ((bf16[4,1552,128]{2,1,0:T(8,128)(2,1)}), bf16[4,1552,128]{2,1,0:T(8,128)(2,1)S(1)}, u32[]{:S(2)}, u32[]{:S(2)}) async-start(bf16[4,1552,128]{2,1,0:T(8,128)(2,1)} %broadcast_in_dim.85), calls=%async_computation | async-start | bytes 3178496 | tf_op jit(solution)/shard_map/all_to_all | solution.py:971
  20.6 9.9 %collective-permute-start.1 = (bf16[784,128]{1,0:T(8,128)(2,1)S(1)}, bf16[784,128]{1,0:T(8,128)(2,1)S(1)}, u32[]{:S(2)}, u32[]{:S(2)}) collective-permute-start(bf16[784,128]{1,0:T(8,128)(2,1)S(1)} %concatenate.89), channel_id=1, source_target_pairs={{0,8},{8,0},{16,24},{24,16},{1,9},{9,1},{17,25},{25,17},{2,10},{10... | collective-permute-start | bytes 602120 | tf_op jit(solution)/shard_map/ppermute | solution.py:962
  22.3 17.4 %collective-permute-start.2 = (bf16[784,128]{1,0:T(8,128)(2,1)S(1)}, bf16[784,128]{1,0:T(8,128)(2,1)S(1)}, u32[]{:S(2)}, u32[]{:S(2)}) collective-permute-start(bf16[784,128]{1,0:T(8,128)(2,1)S(1)} %concatenate.89), channel_id=1, source_target_pairs={{0,16},{8,24},{16,0},{24,8},{1,17},{9,25},{17,1},{25,9},{2,18},{10... | collective-permute-start | bytes 602120 | tf_op jit(solution)/shard_map/ppermute | solution.py:962
  24.9 14.8 %collective-permute-start.3 = (bf16[784,128]{1,0:T(8,128)(2,1)S(1)}, bf16[784,128]{1,0:T(8,128)(2,1)S(1)}, u32[]{:S(2)}, u32[]{:S(2)}) collective-permute-start(bf16[784,128]{1,0:T(8,128)(2,1)S(1)} %concatenate.89), channel_id=1, source_target_pairs={{0,24},{8,16},{16,8},{24,0},{1,25},{9,17},{17,9},{25,1},{2,26},{10... | collective-permute-start | bytes 602120 | tf_op jit(solution)/shard_map/ppermute | solution.py:962
  41.6 32.4 %all-to-all-start.1 = ((bf16[4,3,784,128]{3,2,1,0:T(8,128)(2,1)}), bf16[4,3,784,128]{3,2,1,0:T(8,128)(2,1)}, u32[]{:S(2)}, u32[]{:S(2)}) async-start(bf16[4,3,784,128]{3,2,1,0:T(8,128)(2,1)} %broadcast_in_dim.86), calls=%async_computation.1 | async-start | bytes 4816896 | tf_op jit(solution)/shard_map/all_to_all | solution.py:971
  46.3 116.2 %all-gather.3.cloned.1.call-start = ((), (), s32[]{:S(2)}) async-start(), calls=%async_computation.5 | async-start | bytes 4866048 | tf_op jit(solution)/shard_map/all_gather | solution.py:1049
  47.9 9.5 %collective-permute-start.5 = (bf16[768,128]{1,0:T(8,128)(2,1)S(1)}, bf16[768,128]{1,0:T(8,128)(2,1)S(1)}, u32[]{:S(2)}, u32[]{:S(2)}) collective-permute-start(bf16[768,128]{1,0:T(8,128)(2,1)S(1)} %pad_maximum_fusion.24), channel_id=1, source_target_pairs={{0,8},{8,0},{16,24},{24,16},{1,9},{9,1},{17,25},{25,17},{2,10},{10... | collective-permute-start | bytes 589832 | tf_op jit(solution)/shard_map/ppermute | solution.py:962
  51.3 16.6 %collective-permute-start.6 = (bf16[768,128]{1,0:T(8,128)(2,1)S(1)}, bf16[768,128]{1,0:T(8,128)(2,1)S(1)}, u32[]{:S(2)}, u32[]{:S(2)}) collective-permute-start(bf16[768,128]{1,0:T(8,128)(2,1)S(1)} %pad_maximum_fusion.24), channel_id=1, source_target_pairs={{0,16},{8,24},{16,0},{24,8},{1,17},{9,25},{17,1},{25,9},{2,18},{10... | collective-permute-start | bytes 589832 | tf_op jit(solution)/shard_map/ppermute | solution.py:962
  52.3 15.5 %collective-permute-start.7 = (bf16[768,128]{1,0:T(8,128)(2,1)S(1)}, bf16[768,128]{1,0:T(8,128)(2,1)S(1)}, u32[]{:S(2)}, u32[]{:S(2)}) collective-permute-start(bf16[768,128]{1,0:T(8,128)(2,1)S(1)} %pad_maximum_fusion.24), channel_id=1, source_target_pairs={{0,24},{8,16},{16,8},{24,0},{1,25},{9,17},{17,9},{25,1},{2,26},{10... | collective-permute-start | bytes 589832 | tf_op jit(solution)/shard_map/ppermute | solution.py:962
  67.8 126.2 %all-gather.5.cloned.1.call-start = ((), (), s32[]{:S(2)}) async-start(), calls=%async_computation.7 | async-start | bytes 1310720 | tf_op jit(solution)/shard_map/all_gather | solution.py:1088
  74.0 9.8 %collective-permute-start.4 = (bf16[4,3,784,128]{3,2,1,0:T(8,128)(2,1)}, bf16[4,3,784,128]{3,2,1,0:T(8,128)(2,1)}, u32[]{:S(2)}, u32[]{:S(2)}) collective-permute-start(bf16[4,3,784,128]{3,2,1,0:T(8,128)(2,1)} %all-to-all-done.1.refs_2_), channel_id=1, source_target_pairs={{0,1},{1,0},{2,3},{3,2},{4,5},{5,4},{6,7},{7,6},{8,9},{9,8},{10,11... | collective-permute-start | bytes 7225352 | tf_op jit(solution)/shard_map/ppermute | solution.py:962
  74.0 9.8 %collective-permute-start = (bf16[4,1552,128]{2,1,0:T(8,128)(2,1)S(1)}, bf16[4,1552,128]{2,1,0:T(8,128)(2,1)}, u32[]{:S(2)}, u32[]{:S(2)}) collective-permute-start(bf16[4,1552,128]{2,1,0:T(8,128)(2,1)S(1)} %all-to-all-done.refs_0_), channel_id=1, source_target_pairs={{0,1},{1,0},{2,3},{3,2},{4,5},{5,4},{6,7},{7,6},{8,9},{9,8},{10,11... | collective-permute-start | bytes 4767752 | tf_op jit(solution)/shard_map/ppermute | solution.py:962
  80.2 29.3 %collective-permute-start.8 = (bf16[3,768,128]{2,1,0:T(8,128)(2,1)S(1)}, bf16[3,768,128]{2,1,0:T(8,128)(2,1)}, u32[]{:S(2)}, u32[]{:S(2)}) collective-permute-start(bf16[3,768,128]{2,1,0:T(8,128)(2,1)S(1)} %pad_maximum_fusion.8.refs_2_), channel_id=1, source_target_pairs={{0,2},{2,0},{4,6},{6,4},{1,3},{3,1},{5,7},{7,5},{8,10},{10,8},{12,... | collective-permute-start | bytes 1769480 | tf_op jit(solution)/shard_map/ppermute | solution.py:962
  81.6 27.9 %collective-permute-start.9 = (bf16[3,768,128]{2,1,0:T(8,128)(2,1)S(1)}, bf16[3,768,128]{2,1,0:T(8,128)(2,1)}, u32[]{:S(2)}, u32[]{:S(2)}) collective-permute-start(bf16[3,768,128]{2,1,0:T(8,128)(2,1)S(1)} %pad_maximum_fusion.8.refs_2_), channel_id=1, source_target_pairs={{0,4},{2,6},{4,0},{6,2},{1,5},{3,7},{5,1},{7,3},{8,12},{10,14},{12... | collective-permute-start | bytes 1769480 | tf_op jit(solution)/shard_map/ppermute | solution.py:962
  82.2 27.3 %collective-permute-start.10 = (bf16[3,768,128]{2,1,0:T(8,128)(2,1)S(1)}, bf16[3,768,128]{2,1,0:T(8,128)(2,1)}, u32[]{:S(2)}, u32[]{:S(2)}) collective-permute-start(bf16[3,768,128]{2,1,0:T(8,128)(2,1)S(1)} %pad_maximum_fusion.8.refs_2_), channel_id=1, source_target_pairs={{0,6},{2,4},{4,2},{6,0},{1,7},{3,5},{5,3},{7,1},{8,14},{10,12},{12... | collective-permute-start | bytes 1769480 | tf_op jit(solution)/shard_map/ppermute | solution.py:962
  109.6 3.4 collective-permute-start.12
  110.1 3.7 collective-permute-start.13
  110.2 4.5 %collective-permute-start.14 = (bf16[3,768,128]{2,1,0:T(8,128)(2,1)}, bf16[3,768,128]{2,1,0:T(8,128)(2,1)}, u32[]{:S(2)}, u32[]{:S(2)}) collective-permute-start(bf16[3,768,128]{2,1,0:T(8,128)(2,1)} %collective-permute-done.10.refs_5_), channel_id=1, source_target_pairs={{0,1},{1,0},{2,3},{3,2},{4,5},{5,4},{6,7},{7,6},{8,9},{9,8},{10,11... | collective-permute-start | bytes 1769480 | tf_op jit(solution)/shard_map/ppermute | solution.py:962
  145.2 10.3 %collective-permute-start.17 = (bf16[128,1024]{1,0:T(8,128)(2,1)S(1)}, bf16[128,1024]{1,0:T(8,128)(2,1)}, u32[]{:S(2)}, u32[]{:S(2)}) collective-permute-start(bf16[128,1024]{1,0:T(8,128)(2,1)S(1)} %multiply_convert_fusion.2), channel_id=1, source_target_pairs={{0,6},{2,4},{4,2},{6,0},{1,7},{3,5},{5,3},{7,1},{8,14},{10,12},{12... | collective-permute-start | bytes 786440 | tf_op jit(solution)/shard_map/ppermute | solution.py:962
  146.6 13.6 %collective-permute-start.16 = (bf16[128,1024]{1,0:T(8,128)(2,1)S(1)}, bf16[128,1024]{1,0:T(8,128)(2,1)}, u32[]{:S(2)}, u32[]{:S(2)}) collective-permute-start(bf16[128,1024]{1,0:T(8,128)(2,1)S(1)} %multiply_convert_fusion.2), channel_id=1, source_target_pairs={{0,4},{2,6},{4,0},{6,2},{1,5},{3,7},{5,1},{7,3},{8,12},{10,14},{12... | collective-permute-start | bytes 786440 | tf_op jit(solution)/shard_map/ppermute | solution.py:962
  148.0 12.2 %collective-permute-start.15 = (bf16[128,1024]{1,0:T(8,128)(2,1)S(1)}, bf16[128,1024]{1,0:T(8,128)(2,1)}, u32[]{:S(2)}, u32[]{:S(2)}) collective-permute-start(bf16[128,1024]{1,0:T(8,128)(2,1)S(1)} %multiply_convert_fusion.2), channel_id=1, source_target_pairs={{0,2},{2,0},{4,6},{6,4},{1,3},{3,1},{5,7},{7,5},{8,10},{10,8},{12,... | collective-permute-start | bytes 786440 | tf_op jit(solution)/shard_map/ppermute | solution.py:962
  150.1 235.7 %reduce-scatter.2.cloned.1.call-start = ((), (), s32[]{:S(2)}) async-start(), calls=%async_computation.8 | async-start | bytes 5013504 | tf_op jit(solution)/shard_map/reduce_scatter | solution.py:1109
  181.5 207.5 %all-reduce.5.cloned.1.call-start = ((), (), s32[]{:S(2)}) async-start(), calls=%async_computation.6 | async-start | bytes 2097152 | tf_op jit(solution)/shard_map/psum | solution.py:1107
  190.6 9.5 %collective-permute-start.18 = (bf16[128,1024]{1,0:T(8,128)(2,1)}, bf16[128,1024]{1,0:T(8,128)(2,1)}, u32[]{:S(2)}, u32[]{:S(2)}) collective-permute-start(bf16[128,1024]{1,0:T(8,128)(2,1)} %get-tuple-element.203), channel_id=1, source_target_pairs={{0,2},{2,0},{4,6},{6,4},{1,3},{3,1},{5,7},{7,5},{8,10},{10,8},{12,... | collective-permute-start | bytes 786440 | tf_op jit(solution)/shard_map/ppermute | solution.py:962
  191.9 9.5 %collective-permute-start.19 = (bf16[128,1024]{1,0:T(8,128)(2,1)}, bf16[128,1024]{1,0:T(8,128)(2,1)}, u32[]{:S(2)}, u32[]{:S(2)}) collective-permute-start(bf16[128,1024]{1,0:T(8,128)(2,1)} %get-tuple-element.202), channel_id=1, source_target_pairs={{0,4},{2,6},{4,0},{6,2},{1,5},{3,7},{5,1},{7,3},{8,12},{10,14},{12... | collective-permute-start | bytes 786440 | tf_op jit(solution)/shard_map/ppermute | solution.py:962
  192.5 13.3 %collective-permute-start.20 = (bf16[128,1024]{1,0:T(8,128)(2,1)}, bf16[128,1024]{1,0:T(8,128)(2,1)}, u32[]{:S(2)}, u32[]{:S(2)}) collective-permute-start(bf16[128,1024]{1,0:T(8,128)(2,1)} %get-tuple-element.201), channel_id=1, source_target_pairs={{0,6},{2,4},{4,2},{6,0},{1,7},{3,5},{5,3},{7,1},{8,14},{10,12},{12... | collective-permute-start | bytes 786440 | tf_op jit(solution)/shard_map/ppermute | solution.py:962
  210.8 31.9 %collective-permute-start.21 = (bf16[128,1536]{1,0:T(8,128)(2,1)}, bf16[128,1536]{1,0:T(8,128)(2,1)}, u32[]{:S(2)}, u32[]{:S(2)}) collective-permute-start(bf16[128,1536]{1,0:T(8,128)(2,1)} %get-tuple-element.249), channel_id=1, source_target_pairs={{0,2},{2,0},{4,6},{6,4},{1,3},{3,1},{5,7},{7,5},{8,10},{10,8},{12,... | collective-permute-start | bytes 1179656 | tf_op jit(solution)/shard_map/ppermute | solution.py:962
  211.5 31.2 %collective-permute-start.22 = (bf16[128,1536]{1,0:T(8,128)(2,1)}, bf16[128,1536]{1,0:T(8,128)(2,1)}, u32[]{:S(2)}, u32[]{:S(2)}) collective-permute-start(bf16[128,1536]{1,0:T(8,128)(2,1)} %get-tuple-element.250), channel_id=1, source_target_pairs={{0,4},{2,6},{4,0},{6,2},{1,5},{3,7},{5,1},{7,3},{8,12},{10,14},{12... | collective-permute-start | bytes 1179656 | tf_op jit(solution)/shard_map/ppermute | solution.py:962
  213.0 29.7 %collective-permute-start.23 = (bf16[128,1536]{1,0:T(8,128)(2,1)}, bf16[128,1536]{1,0:T(8,128)(2,1)}, u32[]{:S(2)}, u32[]{:S(2)}) collective-permute-start(bf16[128,1536]{1,0:T(8,128)(2,1)} %get-tuple-element.248), channel_id=1, source_target_pairs={{0,6},{2,4},{4,2},{6,0},{1,7},{3,5},{5,3},{7,1},{8,14},{10,12},{12... | collective-permute-start | bytes 1179656 | tf_op jit(solution)/shard_map/ppermute | solution.py:962
  249.6 11.9 %collective-permute-start.24 = (bf16[128,1280]{1,0:T(8,128)(2,1)}, bf16[128,1280]{1,0:T(8,128)(2,1)}, u32[]{:S(2)}, u32[]{:S(2)}) collective-permute-start(bf16[128,1280]{1,0:T(8,128)(2,1)} %get-tuple-element.94), channel_id=1, source_target_pairs={{0,2},{2,0},{4,6},{6,4},{1,3},{3,1},{5,7},{7,5},{8,10},{10,8},{12,... | collective-permute-start | bytes 983048 | tf_op jit(solution)/shard_map/ppermute | solution.py:962
  250.3 12.2 %collective-permute-start.25 = (bf16[128,1280]{1,0:T(8,128)(2,1)}, bf16[128,1280]{1,0:T(8,128)(2,1)}, u32[]{:S(2)}, u32[]{:S(2)}) collective-permute-start(bf16[128,1280]{1,0:T(8,128)(2,1)} %get-tuple-element.95), channel_id=1, source_target_pairs={{0,4},{2,6},{4,0},{6,2},{1,5},{3,7},{5,1},{7,3},{8,12},{10,14},{12... | collective-permute-start | bytes 983048 | tf_op jit(solution)/shard_map/ppermute | solution.py:962
  251.9 19.4 %collective-permute-start.26 = (bf16[128,1280]{1,0:T(8,128)(2,1)}, bf16[128,1280]{1,0:T(8,128)(2,1)}, u32[]{:S(2)}, u32[]{:S(2)}) collective-permute-start(bf16[128,1280]{1,0:T(8,128)(2,1)} %get-tuple-element.96), channel_id=1, source_target_pairs={{0,6},{2,4},{4,2},{6,0},{1,7},{3,5},{5,3},{7,1},{8,14},{10,12},{12... | collective-permute-start | bytes 983048 | tf_op jit(solution)/shard_map/ppermute | solution.py:962
  272.8 23.1 %collective-permute-start.27 = (bf16[128,1536]{1,0:T(8,128)(2,1)S(1)}, bf16[128,1536]{1,0:T(8,128)(2,1)S(1)}, u32[]{:S(2)}, u32[]{:S(2)}) collective-permute-start(bf16[128,1536]{1,0:T(8,128)(2,1)S(1)} %get-tuple-element.98), channel_id=1, source_target_pairs={{0,2},{2,0},{4,6},{6,4},{1,3},{3,1},{5,7},{7,5},{8,10},{10,8},{12,... | collective-permute-start | bytes 1179656 | tf_op jit(solution)/shard_map/ppermute | solution.py:962
  273.4 22.4 %collective-permute-start.28 = (bf16[128,1536]{1,0:T(8,128)(2,1)S(1)}, bf16[128,1536]{1,0:T(8,128)(2,1)S(1)}, u32[]{:S(2)}, u32[]{:S(2)}) collective-permute-start(bf16[128,1536]{1,0:T(8,128)(2,1)S(1)} %get-tuple-element.99), channel_id=1, source_target_pairs={{0,4},{2,6},{4,0},{6,2},{1,5},{3,7},{5,1},{7,3},{8,12},{10,14},{12... | collective-permute-start | bytes 1179656 | tf_op jit(solution)/shard_map/ppermute | solution.py:962
  273.8 22.0 %collective-permute-start.29 = (bf16[128,1536]{1,0:T(8,128)(2,1)S(1)}, bf16[128,1536]{1,0:T(8,128)(2,1)S(1)}, u32[]{:S(2)}, u32[]{:S(2)}) collective-permute-start(bf16[128,1536]{1,0:T(8,128)(2,1)S(1)} %get-tuple-element.100), channel_id=1, source_target_pairs={{0,6},{2,4},{4,2},{6,0},{1,7},{3,5},{5,3},{7,1},{8,14},{10,12},{12... | collective-permute-start | bytes 1179656 | tf_op jit(solution)/shard_map/ppermute | solution.py:962
  280.1 21.7 %collective-permute-start.33 = (bf16[4,128,512]{2,1,0:T(8,128)(2,1)S(1)}, bf16[4,128,512]{2,1,0:T(8,128)(2,1)S(1)}, u32[]{:S(2)}, u32[]{:S(2)}) collective-permute-start(bf16[4,128,512]{2,1,0:T(8,128)(2,1)S(1)} %get-tuple-element.113), channel_id=1, source_target_pairs={{0,1},{1,0},{2,3},{3,2},{4,5},{5,4},{6,7},{7,6},{8,9},{9,8},{10,11... | collective-permute-start | bytes 1572872 | tf_op jit(solution)/shard_map/ppermute | solution.py:962
  289.1 15.4 %collective-permute-start.35 = (bf16[4,128,1024]{2,1,0:T(8,128)(2,1)S(1)}, bf16[4,128,1024]{2,1,0:T(8,128)(2,1)S(1)}, u32[]{:S(2)}, u32[]{:S(2)}) collective-permute-start(bf16[4,128,1024]{2,1,0:T(8,128)(2,1)S(1)} %get-tuple-element.118), channel_id=1, source_target_pairs={{0,1},{1,0},{2,3},{3,2},{4,5},{5,4},{6,7},{7,6},{8,9},{9,8},{10,11... | collective-permute-start | bytes 3145736 | tf_op jit(solution)/shard_map/ppermute | solution.py:962
  295.9 27.7 %collective-permute-start.30 = (bf16[2048,256]{1,0:T(8,128)(2,1)S(1)}, bf16[2048,256]{1,0:T(8,128)(2,1)}, u32[]{:S(2)}, u32[]{:S(2)}) collective-permute-start(bf16[2048,256]{1,0:T(8,128)(2,1)S(1)} %get-tuple-element.108), channel_id=1, source_target_pairs={{0,2},{2,0},{4,6},{6,4},{1,3},{3,1},{5,7},{7,5},{8,10},{10,8},{12,... | collective-permute-start | bytes 3145736 | tf_op jit(solution)/shard_map/ppermute | solution.py:962
  296.5 52.5 %collective-permute-start.31 = (bf16[2048,256]{1,0:T(8,128)(2,1)S(1)}, bf16[2048,256]{1,0:T(8,128)(2,1)}, u32[]{:S(2)}, u32[]{:S(2)}) collective-permute-start(bf16[2048,256]{1,0:T(8,128)(2,1)S(1)} %get-tuple-element.109), channel_id=1, source_target_pairs={{0,4},{2,6},{4,0},{6,2},{1,5},{3,7},{5,1},{7,3},{8,12},{10,14},{12... | collective-permute-start | bytes 3145736 | tf_op jit(solution)/shard_map/ppermute | solution.py:962
  301.1 7.8 %collective-permute-start.34 = (bf16[4,128,768]{2,1,0:T(8,128)(2,1)S(1)}, bf16[4,128,768]{2,1,0:T(8,128)(2,1)S(1)}, u32[]{:S(2)}, u32[]{:S(2)}) collective-permute-start(bf16[4,128,768]{2,1,0:T(8,128)(2,1)S(1)} %get-tuple-element.115), channel_id=1, source_target_pairs={{0,1},{1,0},{2,3},{3,2},{4,5},{5,4},{6,7},{7,6},{8,9},{9,8},{10,11... | collective-permute-start | bytes 2359304 | tf_op jit(solution)/shard_map/ppermute | solution.py:962
  301.8 65.0 %collective-permute-start.32 = (bf16[2048,256]{1,0:T(8,128)(2,1)S(1)}, bf16[2048,256]{1,0:T(8,128)(2,1)}, u32[]{:S(2)}, u32[]{:S(2)}) collective-permute-start(bf16[2048,256]{1,0:T(8,128)(2,1)S(1)} %get-tuple-element.110), channel_id=1, source_target_pairs={{0,6},{2,4},{4,2},{6,0},{1,7},{3,5},{5,3},{7,1},{8,14},{10,12},{12... | collective-permute-start | bytes 3145736 | tf_op jit(solution)/shard_map/ppermute | solution.py:962
  305.9 41.4 %collective-permute-start.36 = (bf16[2,128,1024]{2,1,0:T(8,128)(2,1)}, bf16[2,128,1024]{2,1,0:T(8,128)(2,1)}, u32[]{:S(2)}, u32[]{:S(2)}) collective-permute-start(bf16[2,128,1024]{2,1,0:T(8,128)(2,1)} %slice.423), channel_id=1, source_target_pairs={{0,16},{8,24},{16,0},{24,8},{1,17},{9,25},{17,1},{25,9},{2,18},{10... | collective-permute-start | bytes 1572872 | tf_op jit(solution)/shard_map/ppermute | solution.py:962
  310.4 60.2 %all-to-all-start.2 = ((bf16[4,128,1280]{2,1,0:T(8,128)(2,1)}), bf16[4,128,1280]{2,1,0:T(8,128)(2,1)}, u32[]{:S(2)}, u32[]{:S(2)}) async-start(bf16[4,128,1280]{2,1,0:T(8,128)(2,1)} %pad_maximum_fusion.2), calls=%async_computation.2 | async-start | bytes 2621440 | tf_op jit(solution)/shard_map/all_to_all | solution.py:1199
  348.5 14.6 %collective-permute-start.37 = (bf16[1,128,1024]{2,1,0:T(8,128)(2,1)S(1)}, bf16[1,128,1024]{2,1,0:T(8,128)(2,1)S(1)}, u32[]{:S(2)}, u32[]{:S(2)}) collective-permute-start(bf16[1,128,1024]{2,1,0:T(8,128)(2,1)S(1)} %slice.424), channel_id=1, source_target_pairs={{0,8},{8,0},{16,24},{24,16},{1,9},{9,1},{17,25},{25,17},{2,10},{10... | collective-permute-start | bytes 786440 | tf_op jit(solution)/shard_map/ppermute | solution.py:962
  363.2 5.8 %collective-permute-start.40 = (bf16[128,256]{1,0:T(8,128)(2,1)S(1)}, bf16[128,256]{1,0:T(8,128)(2,1)S(1)}, u32[]{:S(2)}, u32[]{:S(2)}) collective-permute-start(bf16[128,256]{1,0:T(8,128)(2,1)S(1)} %get-tuple-element.226), channel_id=1, source_target_pairs={{0,6},{2,4},{4,2},{6,0},{1,7},{3,5},{5,3},{7,1},{8,14},{10,12},{12... | collective-permute-start | bytes 196616 | tf_op jit(solution)/shard_map/ppermute | solution.py:962
  365.6 4.3 %collective-permute-start.39 = (bf16[128,256]{1,0:T(8,128)(2,1)S(1)}, bf16[128,256]{1,0:T(8,128)(2,1)S(1)}, u32[]{:S(2)}, u32[]{:S(2)}) collective-permute-start(bf16[128,256]{1,0:T(8,128)(2,1)S(1)} %get-tuple-element.227), channel_id=1, source_target_pairs={{0,4},{2,6},{4,0},{6,2},{1,5},{3,7},{5,1},{7,3},{8,12},{10,14},{12... | collective-permute-start | bytes 196616 | tf_op jit(solution)/shard_map/ppermute | solution.py:962
  365.6 4.3 %collective-permute-start.38 = (bf16[128,256]{1,0:T(8,128)(2,1)S(1)}, bf16[128,256]{1,0:T(8,128)(2,1)S(1)}, u32[]{:S(2)}, u32[]{:S(2)}) collective-permute-start(bf16[128,256]{1,0:T(8,128)(2,1)S(1)} %get-tuple-element.225), channel_id=1, source_target_pairs={{0,2},{2,0},{4,6},{6,4},{1,3},{3,1},{5,7},{7,5},{8,10},{10,8},{12,... | collective-permute-start | bytes 196616 | tf_op jit(solution)/shard_map/ppermute | solution.py:962
  372.2 12.2 %all-to-all-start.3 = ((bf16[32,8,128]{2,1,0:T(8,128)(2,1)}), bf16[32,8,128]{2,1,0:T(8,128)(2,1)S(1)}, u32[]{:S(2)}, u32[]{:S(2)}) async-start(bf16[32,8,128]{2,1,0:T(8,128)(2,1)} %bitcast.40), calls=%async_computation.3 | async-start | bytes 131072 | tf_op jit(solution)/shard_map/all_to_all | solution.py:1224
  (98 other events, 666.1 us)
Sparse Core Ops, SparseCore 0:
  68.0 49.8 all-gather.2
  150.2 27.0 all-gather.4
  181.6 54.3 reduce-scatter.1
  239.5 63.4 all-reduce.4

commit v2 on v1

--- a/solution.py
+++ b/solution.py
@@ -789,31 +789,69 @@
     )
 
 
-def memory_terms(index, pairs, weight, tp):
+def memory_terms(index, seq, memory, pairs, weight, tp):
     rows, width = pairs.shape
+    shard = width // (2 * seq)
     features = weight.shape[0] // tp
-    steps = 4
+    steps = 2 * seq
     block = rows // steps
-
-    def kernel(index_ref, pairs_ref, weight_ref, *outs):
-        for k, out in enumerate(outs):
+    early = max(steps // 4, 1)
+
+    def row_of(step, index):
+        return 2 * (index[0] ^ (step % seq)) + (index[2] ^ (1 - step // seq))
+
+    def kernel(index_ref, memory_ref, pairs_ref, weight_ref, sent_ref, kept_ref, *outs):
+        step = pl.program_id(0)
+        part = t_dot(memory_ref[0], pairs_ref[...])
+
+        @pl.when(step < seq)
+        def _():
+            sent_ref[0] = low(part)
+
+        @pl.when(step >= seq)
+        def _():
+            kept_ref[0] = part
+
+        values = pairs_ref[pl.ds(pl.multiple_of(step * block, block), block), :]
+        for k in range(tp):
             at = pl.multiple_of((index_ref[1] ^ k) * features, features)
-            out[...] = low(dot_t(pairs_ref[...], weight_ref[pl.ds(at, features), :]))
-
-    spec = pl.BlockSpec((block, features), lambda k, index: (k, 0))
+            outs[tp + k][...] = low(dot_t(values, weight_ref[pl.ds(at, features), :]))
+
+        @pl.when(step < early)
+        def _():
+            for k in range(tp):
+                outs[k][...] = outs[tp + k][...]
+
+    shape = (seq, shard, width)
+    first = pl.BlockSpec((block, features), lambda s, index: (jnp.minimum(s, early - 1), 0))
+    second = pl.BlockSpec((block, features), lambda s, index: (jnp.maximum(s - early, 0), 0))
     return with_index(
         kernel,
         "memory_terms",
         (steps,),
         [
-            pl.BlockSpec((block, width), lambda k, index: (k, 0)),
-            pl.BlockSpec(weight.shape, lambda k, index: (0, 0)),
+            pl.BlockSpec((1, rows, shard), lambda s, index: (index[1], 0, row_of(s, index))),
+            pl.BlockSpec(pairs.shape, lambda s, index: (0, 0)),
+            pl.BlockSpec(weight.shape, lambda s, index: (0, 0)),
         ],
-        [(spec, (rows, features), jnp.bfloat16)] * tp,
+        [
+            (
+                pl.BlockSpec((1, shard, width), lambda s, index: (jnp.minimum(s, seq - 1), 0, 0)),
+                shape,
+                jnp.bfloat16,
+            ),
+            (
+                pl.BlockSpec((1, shard, width), lambda s, index: (jnp.maximum(s - seq, 0), 0, 0)),
+                shape,
+                jnp.float32,
+            ),
+        ]
+        + [(first, (early * block, features), jnp.bfloat16)] * tp
+        + [(second, (rows - early * block, features), jnp.bfloat16)] * tp,
         [],
-        (2 * rows * width * weight.shape[0], 2 * (2 * pairs.size + weight.size)),
+        (4 * rows * width * width, 6 * pairs.size),
         index,
-        (pairs, weight),
+        (memory, pairs, weight),
     )
 
 
@@ -856,10 +894,9 @@
 
 
 def row_terms(index, seq, name, pairs):
-    rows = pairs[0][0].shape[-2]
-    width = pairs[0][0].shape[-1]
+    width = pairs[0][0][0].shape[-1] if isinstance(pairs[0][0], list) else pairs[0][0].shape[-1]
     shard = width // (2 * seq)
-    columns = sum(right.shape[1] for _, right in pairs)
+    columns = sum(right[0][2] - right[0][1] for _, right in pairs)
 
     def row_of(step, index):
         return 2 * (index[0] ^ (step % seq)) + (index[2] ^ (1 - step // seq))
@@ -867,10 +904,17 @@
     def kernel(index_ref, *refs):
         sent_ref, kept_ref = refs[-2:]
         parts = []
-        for entry in range(len(pairs)):
-            left, right = refs[2 * entry], refs[2 * entry + 1]
-            left = left[0] if len(left.shape) == 3 else left[...]
-            parts.append(t_dot(left, right[...]))
+        at = 0
+        for left, right in pairs:
+            if isinstance(left, list):
+                value = jnp.concatenate([ref[...] for ref in refs[at : at + len(left)]], axis=0)
+                at += len(left)
+            else:
+                value = refs[at][0]
+                at += 1
+            other = [ref[:, low_at:high_at] for ref, (_, low_at, high_at) in zip(refs[at:], right)]
+            at += len(right)
+            parts.append(t_dot(value, jnp.concatenate(other, axis=0)))
 
         def put(ref, kind):
             at = 0
@@ -888,15 +932,24 @@
 
     specs = []
     arguments = []
+    depth = 0
     for left, right in pairs:
-        if left.ndim == 3:
+        if isinstance(left, list):
+            for part in left:
+                rows = part.shape[0]
+                specs.append(pl.BlockSpec((rows, shard), lambda s, index: (0, row_of(s, index))))
+                arguments.append(part)
+        else:
             specs.append(
-                pl.BlockSpec((1, rows, shard), lambda s, index: (index[1], 0, row_of(s, index)))
+                pl.BlockSpec(
+                    (1, left.shape[1], shard), lambda s, index: (index[1], 0, row_of(s, index))
+                )
             )
-        else:
-            specs.append(pl.BlockSpec((rows, shard), lambda s, index: (0, row_of(s, index))))
-        specs.append(pl.BlockSpec(right.shape, lambda s, index: (0, 0)))
-        arguments += [left, right]
+            arguments.append(left)
+        for part, _, _ in right:
+            specs.append(pl.BlockSpec(part.shape, lambda s, index: (0, 0)))
+            arguments.append(part)
+        depth = max(depth, sum(part.shape[0] for part, _, _ in right))
     shape = (seq, shard, columns)
     block = (1, shard, columns)
     return with_index(
@@ -917,9 +970,10 @@
             ),
         ],
         [],
-        (2 * rows * width * columns, 2 * rows * (width + columns) + 3 * width * columns),
+        (2 * depth * width * columns, 2 * depth * (width + columns) + 3 * width * columns),
         index,
         tuple(arguments),
+        limit=56,
     )
 
 
@@ -956,6 +1010,9 @@
 
     def after(value, *earlier):
         return lax.optimization_barrier((value, earlier))[0]
+
+    def together(*values):
+        return lax.optimization_barrier(values)
 
     def swap(value, axis, flip):
         size = {"seq": seq, "tp": tp, "fsdp": 2}[axis]
@@ -1045,7 +1102,9 @@
         ring_a = gather(pack_a, "seq", seq)
         ring_b = gather(after(pack_b, *ring_a), "seq", seq)
         far_a = to_everyone(after(jnp.stack(ring_a[1:]), near))
-        far_b = gather(after(jnp.stack(ring_b[1:]), far_a), "tp", tp)
+        far_b = after(jnp.stack(ring_b[1:]), far_a)
+        buckets, decoder_in, cotangent = after((buckets, decoder_in, cotangent), far_b)
+        far_b = gather(far_b, "tp", tp)
         full_f = lax.all_gather(after(pack_f, *ring_b), ("seq", "fsdp"), axis=0, tiled=True)
         near = [near, swap(near, "fsdp", 1)]
         far_a = [far_a, swap(far_a, "fsdp", 1)]
@@ -1100,146 +1159,172 @@
         def row_parts(value):
             return [value[k * rows : (k + 1) * rows] for k in range(tp)]
 
-        grad_parts = exchange(row_parts(low(dot_t(grad_joined, weight_gate_up))), "tp")
+        partial_normed = row_parts(low(dot_t(grad_joined, weight_gate_up)))
+        grad_parts = exchange(partial_normed, "tp")
+        all_normed, grad_joined, rounded, hidden, o_self, o_cross = after(
+            (all_normed, grad_joined, rounded, hidden, mixed_self, mixed_cross), partial_normed
+        )
         hidden_grads = hidden_terms(all_normed, grad_joined, rounded, hidden)
         partial_out = hidden_out(index, hidden, weight_down, after_cross, tp)
-        grad_normed = total([after(grad_parts[0], hidden_grads, partial_out)] + grad_parts[1:])
-        decoder_out = lax.psum(after(partial_out, *grad_parts), "tp")
+        o_blocks = [
+            jnp.concatenate(blocks, axis=1)
+            for blocks in zip(head_blocks(o_self), head_blocks(o_cross))
+        ]
+        grad_parts, hidden_grads, partial_out, o_blocks = together(
+            grad_parts, hidden_grads, partial_out, o_blocks
+        )
         hidden_grads = high(
             lax.psum_scatter(hidden_grads, ("seq", "fsdp"), scatter_dimension=0, tiled=True)
         )
 
+        grad_normed = total(grad_parts)
         grad_residual, gain_ffn = norm_backward(after_cross, gain_rows[2], grad_normed)
-        grad_cross = high(rounded[:rows]) + grad_residual
+        grad_cross = high(own(cotangent)) + grad_residual
         rounded_cross = low(grad_cross)
-        grad_mixed = low(dot_t(rounded_cross, weight_cross_out))
-        cross_parts = exchange(
-            [
-                jnp.concatenate([rounded_cross, o_self, o_cross], axis=1)
-                for o_self, o_cross in zip(head_blocks(mixed_self), head_blocks(mixed_cross))
-            ],
-            "tp",
-        )
+        cross_operands = [jnp.concatenate([rounded_cross, block], axis=1) for block in o_blocks]
+        cross_parts = exchange(cross_operands, "tp")
+        grad_mixed = low(dot_t(after(rounded_cross, cross_operands), weight_cross_out))
         grad_query, grad_pairs = attention_backward(
             query_cross, grad_mixed, mixed_cross, pairs, log_cross, None
         )
+        cross_parts, grad_query, grad_pairs = together(cross_parts, grad_query, grad_pairs)
         grad_normed = dot_t(grad_query, weight_cross_q)
         grad_residual, gain_cross = norm_backward(after_self, gain_rows[1], grad_normed)
         grad_self = grad_cross + grad_residual
         rounded_self = low(grad_self)
-        self_parts = exchange(
-            after(
-                [
-                    jnp.concatenate([rounded_self, block], axis=1)
-                    for block in head_blocks(grad_query)
-                ],
-                *cross_parts,
-            ),
-            "tp",
-        )
-
-        grad_mixed_self = low(dot_t(rounded_self, weight_self_out))
+        self_operands = [
+            jnp.concatenate([rounded_self, block], axis=1) for block in head_blocks(grad_query)
+        ]
+        self_parts = exchange(self_operands, "tp")
+
+        grad_mixed_self = low(dot_t(after(rounded_self, self_operands), weight_self_out))
         grad_query_self, grad_pair_self, grad_scores = attention_backward(
-            query_self, after(grad_mixed_self, *cross_parts), mixed_self, pair_self, log_self, bias
+            query_self, grad_mixed_self, mixed_self, pair_self, log_self, bias
         )
         grad_normed = dot_t(grad_query_self, weight_self_q) + dot_t(grad_pair_self, weight_self_kv)
         grad_residual, gain_self = norm_backward(start, gain_rows[0], grad_normed)
         grad_tokens = low(grad_self + grad_residual)
-        last_parts = [
+        last_operands = [
             jnp.concatenate([grad_tokens, q_block, kv_block], axis=1)
             for q_block, kv_block in zip(head_blocks(grad_query_self), head_blocks(grad_pair_self))
         ]
-        grad_pairs = after(grad_pairs, *last_parts, *self_parts)
-        last_parts = exchange(after(last_parts, *self_parts), "tp")
-        decoder_grad = in_order([part[:, :width] for part in last_parts], jnp.float32)
-
-        memory_grad = in_order(
-            exchange(after(memory_terms(index, grad_pairs, cross_pairs, tp), *last_parts), "tp"),
-            jnp.bfloat16,
-        )
-
-        def core_sum(name, *terms):
-            sent, kept = row_terms(index, seq, name, terms)
-            return kept + high(swap(sent, "fsdp", 1))
-
-        kv_rows = core_sum("memory_weights", (memory, grad_pairs))
-        step = seq // 2
-        while step:
-            kv_rows = kv_rows[:step] + high(swap(low(kv_rows[step:]), "seq", step))
-            step //= 2
-        kv_rows = kv_rows[0]
-        cross_kv_grad = total(
-            exchange([kv_rows[:, : 2 * GROUP]] + head_blocks(low(kv_rows))[1:], "tp")
-        )
-        all_back = jnp.concatenate(cross_parts, axis=0)
-        all_self = jnp.concatenate(self_parts, axis=0)
-        all_last = jnp.concatenate([part[:, width:] for part in last_parts], axis=0)
-        cross_grads = core_sum(
-            "cross_weights",
-            (jnp.concatenate(from_here(all_cross.reshape(tp, rows, width)), axis=0), all_self[:, width:]),
-            (all_back[:, :width], all_back[:, width + 2 * GROUP :]),
-        )
-        all_start = low(
-            rms_norm(high(jnp.concatenate(from_here(decoder_in), axis=0)), gain_rows[0])
-        )
-        self_grads = core_sum(
-            "self_weights",
-            (all_start, all_last),
-            (all_self[:, :width], all_back[:, width : width + 2 * GROUP]),
-        )
-
-        both_grads = low(jnp.concatenate([cross_grads, self_grads], axis=2))
+        self_parts, last_operands, memory_pairs, decoder_in, gains, grad_scores = together(
+            self_parts,
+            last_operands,
+            grad_pairs,
+            decoder_in,
+            (gain_self, gain_cross, gain_ffn),
+            grad_scores,
+        )
+        last_parts = exchange(last_operands, "tp")
+
+        kv_sent, kv_rows, *memory_parts = memory_terms(
+            index, seq, memory, memory_pairs, cross_pairs, tp
+        )
+        last_parts, kv_sent, kv_rows, memory_parts, gains, grad_scores, partial_out = together(
+            last_parts, kv_sent, kv_rows, memory_parts, gains, grad_scores, partial_out
+        )
+        decoder_out = lax.psum(partial_out, "tp")
+        first_parts = exchange(memory_parts[:tp], "tp")
+        kv_rows = kv_rows + high(swap(kv_sent, "fsdp", 1))
+
+        def span_of(parts, first, last):
+            return [(part, first, last) for part in parts]
+
+        all_start = [
+            low(rms_norm(high(part), gain_rows[0])) for part in from_here(decoder_in)
+        ]
+        both_sent, both_kept = row_terms(
+            index,
+            seq,
+            "head_weights",
+            [
+                (
+                    from_here(all_cross.reshape(tp, rows, width)),
+                    span_of(self_parts, width, width + 2 * GROUP),
+                ),
+                (cross_parts, span_of(cross_parts, width + 2 * GROUP, width + 4 * GROUP)),
+                (all_start, span_of(last_parts, width, width + 4 * GROUP)),
+                (self_parts, span_of(cross_parts, width, width + 2 * GROUP)),
+            ],
+        )
+        kv_far = low(kv_rows[seq // 2 :])
+        first_parts, kv_far, kv_rows, both_sent, both_kept, second_parts = together(
+            first_parts, kv_far, kv_rows, both_sent, both_kept, memory_parts[tp:]
+        )
+        kv_far = swap(kv_far, "seq", seq // 2)
+        second_parts = exchange(second_parts, "tp")
+        both_grads = low(both_kept + high(swap(both_sent, "fsdp", 1)))
         both_grads = jnp.concatenate(
             [
                 lax.dynamic_index_in_dim(both_grads, z ^ k, 0, keepdims=True) for k in range(seq)
             ],
             axis=0,
         )
-        both_grads = jnp.sum(
-            high(lax.all_to_all(both_grads, "seq", 0, 0, tiled=True)), axis=0
-        )
+        gains, grad_scores, last_parts, kv_far, second_parts, hidden_grads = after(
+            (gains, grad_scores, last_parts, kv_far, second_parts, hidden_grads), both_grads
+        )
+        gate_up_grad = hidden_grads[:, : 2 * hidden_width].reshape(gate_up.shape)
+        down_grad = hidden_grads[:, 2 * hidden_width :].T
+        both_grads = lax.all_to_all(both_grads, "seq", 0, 0, tiled=True)
+        kv_rows = kv_rows[: seq // 2] + high(kv_far)
+        step = seq // 4
+        while step:
+            kv_rows = kv_rows[:step] + high(swap(low(kv_rows[step:]), "seq", step))
+            step //= 2
+        kv_rows = kv_rows[0]
+        memory_grad = jnp.zeros((count, memory.shape[1], first_parts[0].shape[1]), jnp.bfloat16)
+        cut = first_parts[0].shape[0]
+        for at, parts in ((0, first_parts), (cut, second_parts)):
+            for k in range(tp):
+                memory_grad = lax.dynamic_update_slice(
+                    memory_grad, parts[k][None], (t ^ k, at, 0)
+                )
+        decoder_grad = in_order([part[:, :width] for part in last_parts], jnp.float32)
+
+        table_grad = jnp.einsum(
+            "jin,hji->nh", onehot, grad_scores, preferred_element_type=jnp.float32
+        )
+        gain_parts = jnp.stack([gain.reshape(-1, GROUP) for gain in gains], axis=1)
+        table_parts = jnp.pad(
+            table_grad.reshape(seq * cores, 1, -1),
+            ((0, 0), (0, 0), (0, GROUP - tables * tp * heads)),
+        )
+        little = low(jnp.concatenate([gain_parts, table_parts], axis=1))
+        little = jnp.broadcast_to(
+            little.reshape(seq, 1, cores, 4, GROUP), (seq, tp, cores, 4, GROUP)
+        )
+        both_grads, little, gate_up_grad, down_grad, decoder_grad, kv_rows, memory_grad = together(
+            both_grads, little, gate_up_grad, down_grad, decoder_grad, kv_rows, memory_grad
+        )
+        cross_kv_grad = total(
+            exchange([kv_rows[:, : 2 * GROUP]] + head_blocks(low(kv_rows))[1:], "tp")
+        )
+        little = lax.all_to_all(little.reshape(-1, 4, GROUP), everyone, 0, 0, tiled=True)
+        little = jnp.sum(high(little).reshape(seq, tp, cores, 4, GROUP), axis=(0, 2))
+        sender = jnp.arange(tp, dtype=jnp.int32)
+        chosen = (sender[:, None] ^ sender[None, :]) == t
+        table_sum = little[:, 3, : tables * tp * heads].reshape(tp, tables, tp, heads)
+        table_sum = jnp.sum(jnp.where(chosen[:, None, :, None], table_sum, 0.0), axis=(0, 2))
+        little = jnp.sum(little, axis=0)
+        both_grads = jnp.sum(high(both_grads), axis=0)
         cross_grads = both_grads[:, : 4 * GROUP]
         self_grads = both_grads[:, 4 * GROUP :]
-
-        table_grad = jnp.einsum(
-            "jin,hji->nh", onehot, grad_scores, preferred_element_type=jnp.float32
-        )
-        gains = jnp.stack([gain_self, gain_cross, gain_ffn])
-        gain_parts = gains.reshape(3, seq, 1, cores, GROUP).transpose(1, 2, 3, 0, 4)
-        gain_parts = jnp.broadcast_to(gain_parts, (seq, tp, cores, 3, GROUP))
-        table_parts = table_grad.reshape(seq, cores, tables, tp, heads)
-        table_parts = jnp.stack(
-            [
-                lax.dynamic_index_in_dim(table_parts, t ^ k, 3, keepdims=False)
-                for k in range(tp)
-            ],
-            axis=1,
-        )
-        table_parts = jnp.pad(
-            table_parts.reshape(seq, tp, cores, 1, -1),
-            ((0, 0),) * 4 + ((0, GROUP - tables * heads),),
-        )
-        little = jnp.concatenate([gain_parts, table_parts], axis=3)
-        little = jnp.pad(low(little), ((0, 0),) * 3 + ((0, 4), (0, 0)))
-        little = lax.all_to_all(
-            after(little.reshape(-1, 8, GROUP), both_grads), everyone, 0, 0, tiled=True
-        )
-        little = jnp.sum(high(little), axis=0)
 
         return (
             decoder_out,
             decoder_grad,
             memory_grad,
             little[0:3],
-            little[3, 0 : tables * heads].reshape(tables, heads),
+            table_sum,
             self_grads[:, 0 : 2 * GROUP],
             self_grads[:, 2 * GROUP : 4 * GROUP].reshape(self_kv.shape),
             self_grads[:, 4 * GROUP :].T,
             cross_grads[:, 0 : 2 * GROUP],
             cross_kv_grad.reshape(cross_kv.shape),
             cross_grads[:, 2 * GROUP :].T,
-            hidden_grads[:, : 2 * hidden_width].reshape(gate_up.shape),
-            hidden_grads[:, 2 * hidden_width :].T,
+            gate_up_grad,
+            down_grad,
         )
 
     return run
@@ -1259,7 +1344,7 @@
             and width == 2 * seq * GROUP
             and arrays[5].shape[1] == 4 * DH
             and arrays[6].shape[2] == 2 * DH
-            and arrays[4].size <= GROUP
+            and tp * arrays[4].size <= GROUP
             and 2 * arrays[12].shape[0] % GROUP == 0
         )
         return (one_each(seq, tp) if fits else per_device)(*arrays)

time: 404 us -> 383 us (0.948)
  waiting for transfers between devices: 110 us -> 89.6 us
  local copies, waits for them, and re-layouts: 68 us -> 59.8 us
    ppermute x41 -> x43, waiting for transfers between devices: 99.9 us -> 81.6 us  [swap(): lax.ppermute(value, axis, [(place, place ^ flip) for place in range(size)])]
    all_to_all x2, waiting for transfers between devices: 4.29 us -> 0.01 us  [the longest x1 0.01 us: run(): lax.all_to_all(little.reshape(-1, 4, GROUP), everyone, 0, 0, tiled=True)]
    pallas_call x7 -> x5, Pallas kernels: 36.2 us -> 39.9 us  [with_index(): pl.pallas_call(kernel, grid_spec=pltpu.PrefetchScalarGridSpec(num_scalar_...]
    unnamed x220 -> x170, local copies, waits for them, and re-layouts: 30.7 us -> 27.9 us
    dynamic_update_slice x4 -> x8, local copies, waits for them, and re-layouts: 6.87 us -> 9.1 us  [run(): lax.dynamic_update_slice(memory_grad, parts[k][None], (t ^ k, at, 0))]
    ppermute x41 -> x43, starting transfers between devices: 44.4 us -> 43 us  [swap(): lax.ppermute(value, axis, [(place, place ^ flip) for place in range(size)])]
  transfers between devices with their start and end apart: 49 -> 51, of which waited for: 20 -> 18; matrix products, arithmetic and copies ran while one was open for 23% -> 23% of each run, Pallas kernels for 21% -> 24%
where the time goes in v2:
time: 383 us; the launch traced here: 376 us
  waiting for transfers between devices  89.6 us (23%)
  Pallas kernels  88.7 us (23%)
  starting transfers between devices  62.4 us (16%)
  local copies, waits for them, and re-layouts  59.8 us (16%)
  other arithmetic  31 us (8%)
  matrix products  28.5 us (7%)
  between operations  15.7 us (4%)
    ppermute x43, waiting for transfers between devices, swap(): lax.ppermute(value, axis, [(place, place ^ flip) for place in range(size)])  81.6 us
    pallas_call x6, Pallas kernels, kernel_call(): pl.pallas_call(kernel, grid=(blocks,), in_specs=specs, out_specs=[spec fo...  48.8 us
    ppermute x43, starting transfers between devices, swap(): lax.ppermute(value, axis, [(place, place ^ flip) for place in range(size)])  43 us
    pallas_call x5, Pallas kernels, with_index(): pl.pallas_call(kernel, grid_spec=pltpu.PrefetchScalarGridSpec(num_scalar_...  39.9 us
    unnamed x170, local copies, waits for them, and re-layouts  27.9 us
    dot_general x7, matrix products, dot(): return jnp.dot(left, right, preferred_element_type=jnp.float32)  18.5 us
    all_to_all x2, starting transfers between devices, exchange_all(): return lax.all_to_all(value, 'tp', 0, 0, tiled=True)  9.8 us
    dot_general x7, matrix products, dot_t(): lax.dot_general(left, right, (((1,), (1,)), ((), ())), preferred_element_...  9.24 us
  transfers between devices with their start and end apart: 51, of which 18 were waited for; matrix products, arithmetic and copies ran while one was open for 23% of the time, Pallas kernels for 24%

profile of v2, /device:TPU:0, one launch (start us, length us, event | category | flops | bytes accessed | tf_op | source)
XLA Modules:
  0.0 375.6 jit_solution(1394460938939383325)
XLA Ops:
  11.3 2.6 concatenate.92
  15.2 5.2 %all-to-all-start = ((bf16[4,1552,128]{2,1,0:T(8,128)(2,1)}), bf16[4,1552,128]{2,1,0:T(8,128)(2,1)S(1)}, u32[]{:S(2)}, u32[]{:S(2)}) async-start(bf16[4,1552,128]{2,1,0:T(8,128)(2,1)} %broadcast_in_dim.114), calls=%async_computation | async-start | bytes 3178496 | tf_op jit(solution)/shard_map/all_to_all | solution.py:1028
  20.6 3.7 collective-permute-start.2
  25.1 5.4 %collective-permute-done.2 = bf16[784,128]{1,0:T(8,128)(2,1)S(1)} collective-permute-done((bf16[784,128]{1,0:T(8,128)(2,1)S(1)}, bf16[784,128]{1,0:T(8,128)(2,1)S(1)}, u32[]{:S(2)}, u32[]{:S(2)}) %collective-permute-start.2) | collective-permute-done | bytes 200736 | tf_op jit(solution)/shard_map/ppermute | solution.py:1019
  30.5 10.7 %collective-permute-done.1 = bf16[784,128]{1,0:T(8,128)(2,1)S(1)} collective-permute-done((bf16[784,128]{1,0:T(8,128)(2,1)S(1)}, bf16[784,128]{1,0:T(8,128)(2,1)S(1)}, u32[]{:S(2)}, u32[]{:S(2)}) %collective-permute-start.1) | collective-permute-done | bytes 200736 | tf_op jit(solution)/shard_map/ppermute | solution.py:1019
  43.0 4.6 %all-to-all-start.1 = ((bf16[4,3,784,128]{3,2,1,0:T(8,128)(2,1)}), bf16[4,3,784,128]{3,2,1,0:T(8,128)(2,1)}, u32[]{:S(2)}, u32[]{:S(2)}) async-start(bf16[4,3,784,128]{3,2,1,0:T(8,128)(2,1)} %broadcast_in_dim.115), calls=%async_computation.1 | async-start | bytes 4816896 | tf_op jit(solution)/shard_map/all_to_all | solution.py:1028
  49.4 2.5 collective-permute-start.5
  51.9 1.9 collective-permute-start.3
  53.9 5.3 %collective-permute-done.5 = bf16[768,128]{1,0:T(8,128)(2,1)S(1)} collective-permute-done((bf16[768,128]{1,0:T(8,128)(2,1)S(1)}, bf16[768,128]{1,0:T(8,128)(2,1)S(1)}, u32[]{:S(2)}, u32[]{:S(2)}) %collective-permute-start.5) | collective-permute-done | bytes 196640 | tf_op jit(solution)/shard_map/ppermute | solution.py:1019
  59.2 8.4 %collective-permute-done.4 = bf16[768,128]{1,0:T(8,128)(2,1)S(1)} collective-permute-done((bf16[768,128]{1,0:T(8,128)(2,1)S(1)}, bf16[768,128]{1,0:T(8,128)(2,1)S(1)}, u32[]{:S(2)}, u32[]{:S(2)}) %collective-permute-start.4) | collective-permute-done | bytes 196640 | tf_op jit(solution)/shard_map/ppermute | solution.py:1019
  67.7 7.8 %all-to-all-done.1.refs_2_ = bf16[4,3,784,128]{3,2,1,0:T(8,128)(2,1)} async-done(((bf16[4,3,784,128]{3,2,1,0:T(8,128)(2,1)}), bf16[4,3,784,128]{3,2,1,0:T(8,128)(2,1)}, u32[]{:S(2)}, u32[]{:S(2)}) %all-to-all-start.1) | async-done | bytes 2408480 | tf_op jit(solution)/shard_map/all_to_all | solution.py:1028
  80.9 2.4 copy.162
  84.4 5.5 %unpack_heads.2 = (bf16[1024,1024]{1,0:T(8,128)(2,1)S(1)}, bf16[1024,1024]{1,0:T(8,128)(2,1)S(1)}, bf16[1024,1024]{1,0:T(8,128)(2,1)S(1)}, bf16[4,8,16,128]{3,2,1,0:T(8,128)(2,1)S(1)}) custom-call(s32[3]{0:T(128)S(1)} %pad_add_fusion.index_ref, bf16[4,1552,128]{2,1,0:T(8,128)(2,1)S(1)} %all-to-all-done.refs_0_, ...), custom_call_target="tpu_custom_call" | custom-call | bytes 12845056 | tf_op jit(solution)/shard_map/unpack_heads/pallas_call | solution.py:669
  99.1 3.7 self_forward.1
  102.8 8.3 %fusion.3.kv_ref = bf16[2048,1024]{1,0:T(8,128)(2,1)} fusion(bf16[1024,1024]{1,0:T(8,128)(2,1)S(1)} %copy-done.30, bf16[4,2048,1024]{2,1,0:T(8,128)(2,1)} %memory_ref.1, s32[]{:T(128)S(6)} %select_n.56), kind=kOutput, calls=%fused_computation.3 | convolution fusion | flops 4297064448 | bytes 10485764 | tf_op jit(solution)/shard_map/dot_general | solution.py:412
  116.3 5.3 %unpack_heads.3 = (bf16[1024,1024]{1,0:T(8,128)(2,1)S(1)}, bf16[1024,1024]{1,0:T(8,128)(2,1)S(1)}, bf16[1024,1024]{1,0:T(8,128)(2,1)S(1)}) custom-call(s32[3]{0:T(128)S(1)} %pad_add_fusion.index_ref, bf16[4,1552,128]{2,1,0:T(8,128)(2,1)S(1)} %all-to-all-done.refs_0_, bf16[4,1552,128]{2,1,0:T(8,128)(2,1)} %collective-permute-done.6.refs_1_, ...), custom_call_target="tpu_custom_call" | custom-call | bytes 12582912 | tf_op jit(solution)/shard_map/unpack_heads/pallas_call | solution.py:669
  126.0 2.2 fusion.14.q_ref
  128.2 2.2 copy-done.35
  130.4 15.9 %cross_forward.1 = (bf16[128,1024]{1,0:T(8,128)(2,1)S(1)}, f32[4,2,256]{2,1,0:T(2,128)S(1)}) custom-call(bf16[128,1024]{1,0:T(8,128)(2,1)S(1)} %fusion.14.q_ref, bf16[2048,1024]{1,0:T(8,128)(2,1)S(1)} %copy-done.35), custom_call_target="tpu_custom_call" | custom-call | flops 1073741824 | bytes 4718592 | tf_op jit(solution)/shard_map/cross_forward/pallas_call | solution.py:583
  151.9 5.3 %collective-permute-done.17 = bf16[128,1024]{1,0:T(8,128)(2,1)S(1)} collective-permute-done((bf16[128,1024]{1,0:T(8,128)(2,1)S(1)}, bf16[128,1024]{1,0:T(8,128)(2,1)S(1)}, u32[]{:S(2)}, u32[]{:S(2)}) %collective-permute-start.17) | collective-permute-done | bytes 262176 | tf_op jit(solution)/shard_map/ppermute | solution.py:1019
  157.2 5.8 %collective-permute-done.16 = bf16[128,1024]{1,0:T(8,128)(2,1)} collective-permute-done((bf16[128,1024]{1,0:T(8,128)(2,1)S(1)}, bf16[128,1024]{1,0:T(8,128)(2,1)}, u32[]{:S(2)}, u32[]{:S(2)}) %collective-permute-start.16) | collective-permute-done | bytes 262176 | tf_op jit(solution)/shard_map/ppermute | solution.py:1019
  163.8 2.1 pad_maximum_fusion.3.normed_ref
  166.0 2.2 copy-done.14
  169.4 2.8 fusion.51
  172.2 3.0 fusion.12
  184.1 3.2 hidden_out.1
  190.9 4.9 %hidden_terms.1 = bf16[1024,2112]{1,0:T(8,128)(2,1)S(1)} custom-call(bf16[512,1024]{1,0:T(8,128)(2,1)S(1)} %copy-done.16, bf16[512,1408]{1,0:T(8,128)(2,1)S(1)} %pad_maximum_fusion.joined_ref, bf16[512,1024]{1,0:T(8,128)(2,1)S(1)} %copy-done.15, bf16[512,704]{1,0:T(8,128)(2,1)S(1)} %copy-done.18), custom_call_target="tpu_custom_call" | custom-call | flops 2214592512 | bytes 10747904 | tf_op jit(solution)/shard_map/hidden_terms/pallas_call | solution.py:583
  195.8 2.1 copy-done
  198.1 2.3 dynamic-slice_bitcast_fusion
  208.7 19.6 %cross_backward.1 = (bf16[128,1024]{1,0:T(8,128)(2,1)S(1)}, bf16[2048,1024]{1,0:T(8,128)(2,1)S(1)}) custom-call(bf16[128,1024]{1,0:T(8,128)(2,1)S(1)} %copy-done.27, bf16[128,1024]{1,0:T(8,128)(2,1)S(1)} %convolution_convert_fusion.2.do_ref, bf16[128,1024]{1,0:T(8,128)(2,1)S(1)} %copy-done.25, bf16[2048,1024]{1,0:T(8,128)(2,1)S(1)} %copy-done.36, ...), custom_call_target="tpu_custom_call" | custom-call | flops 2684354560 | bytes 9437184 | tf_op jit(solution)/shard_map/cross_backward/pallas_call | solution.py:583
  234.8 3.5 self_backward.1
  241.4 3.2 collective-permute-done.25.refs_6_.refs_26_
  244.6 2.1 collective-permute-done.26.refs_7_.refs_27_
  247.1 1.9 collective-permute-start.28
  250.2 14.8 %memory_terms.1 = (bf16[4,128,1024]{2,1,0:T(8,128)(2,1)S(1)}, f32[4,128,1024]{2,1,0:T(8,128)S(1)}, bf16[512,256]{1,0:T(8,128)(2,1)S(1)}, bf16[512,256]{1,0:T(8,1...) custom-call(s32[3]{0:T(128)S(1)} %pad_add_fusion.index_ref, ...), custom_call_target="tpu_custom_call" | custom-call | flops 8589934592 | bytes 12582912 | tf_op jit(solution)/shard_map/memory_terms/pallas_call | solution.py:669
  267.6 1.9 collective-permute-start.31
  270.6 11.0 %head_weights.1 = (bf16[4,128,1280]{2,1,0:T(8,128)(2,1)}, f32[4,128,1280]{2,1,0:T(8,128)}) custom-call(s32[3]{0:T(128)} %copy-done.28, bf16[128,1024]{1,0:T(8,128)(2,1)} %get-tuple-element.381.refs_0_, bf16[128,1024]{1,0:T(8,128)(2,1)} %get-tuple-element.380.refs_1_, bf16[128,1024]{1,0:T(8,128)(2,1)} %get-tuple-element.379.refs_2_, ...), custom_call_target="tpu_custom_call" | custom-call | flops 1342177280 | bytes 6291456 | tf_op jit(solution)/shard_map/head_weights/pallas_call | solution.py:669
  291.9 2.6 add_convert_fusion
  295.9 4.7 %all-to-all-start.2 = ((bf16[4,128,1280]{2,1,0:T(8,128)(2,1)}), bf16[4,128,1280]{2,1,0:T(8,128)(2,1)}, u32[]{:S(2)}, u32[]{:S(2)}) async-start(bf16[4,128,1280]{2,1,0:T(8,128)(2,1)} %pad_maximum_fusion.1), calls=%async_computation.2 | async-start | bytes 2621440 | tf_op jit(solution)/shard_map/all_to_all | solution.py:1269
  300.6 2.1 convert_element_type.201
  302.7 16.3 %collective-permute-done.35 = bf16[2,128,1024]{2,1,0:T(8,128)(2,1)} collective-permute-done((bf16[2,128,1024]{2,1,0:T(8,128)(2,1)}, bf16[2,128,1024]{2,1,0:T(8,128)(2,1)}, u32[]{:S(2)}, u32[]{:S(2)}) %collective-permute-start.35) | collective-permute-done | bytes 524320 | tf_op jit(solution)/shard_map/ppermute | solution.py:1019
  319.0 13.2 %collective-permute-done.38 = bf16[1536,256]{1,0:T(8,128)(2,1)} collective-permute-done((bf16[1536,256]{1,0:T(8,128)(2,1)S(1)}, bf16[1536,256]{1,0:T(8,128)(2,1)}, u32[]{:S(2)}, u32[]{:S(2)}) %collective-permute-start.38) | collective-permute-done | bytes 786464 | tf_op jit(solution)/shard_map/ppermute | solution.py:1019
  337.9 2.1 bitcast_dynamic-update-slice_fusion.2
  340.1 2.8 bitcast_dynamic-update-slice_fusion.1
  342.9 2.1 bitcast_dynamic-update-slice_fusion
  349.6 4.7 %all-to-all-start.3 = ((bf16[32,4,128]{2,1,0:T(4,128)(2,1)}), bf16[32,4,128]{2,1,0:T(4,128)(2,1)S(1)}, u32[]{:S(2)}, u32[]{:S(2)}) async-start(bf16[32,4,128]{2,1,0:T(4,128)(2,1)} %bitcast.60), calls=%async_computation.4 | async-start | bytes 65536 | tf_op jit(solution)/shard_map/all_to_all | solution.py:1303
  358.3 2.7 collective-permute-start.42
  366.6 2.3 copy.214
  (377 shorter events, 109.1 us)
Async XLA Ops:
  15.2 26.1 %all-to-all-start = ((bf16[4,1552,128]{2,1,0:T(8,128)(2,1)}), bf16[4,1552,128]{2,1,0:T(8,128)(2,1)S(1)}, u32[]{:S(2)}, u32[]{:S(2)}) async-start(bf16[4,1552,128]{2,1,0:T(8,128)(2,1)} %broadcast_in_dim.114), calls=%async_computation | async-start | bytes 3178496 | tf_op jit(solution)/shard_map/all_to_all | solution.py:1028
  20.6 9.8 %collective-permute-start.2 = (bf16[784,128]{1,0:T(8,128)(2,1)S(1)}, bf16[784,128]{1,0:T(8,128)(2,1)S(1)}, u32[]{:S(2)}, u32[]{:S(2)}) collective-permute-start(bf16[784,128]{1,0:T(8,128)(2,1)S(1)} %concatenate.91), channel_id=1, source_target_pairs={{0,24},{8,16},{16,8},{24,0},{1,25},{9,17},{17,9},{25,1},{2,26},{10... | collective-permute-start | bytes 602120 | tf_op jit(solution)/shard_map/ppermute | solution.py:1019
  24.3 16.9 %collective-permute-start.1 = (bf16[784,128]{1,0:T(8,128)(2,1)S(1)}, bf16[784,128]{1,0:T(8,128)(2,1)S(1)}, u32[]{:S(2)}, u32[]{:S(2)}) collective-permute-start(bf16[784,128]{1,0:T(8,128)(2,1)S(1)} %concatenate.91), channel_id=1, source_target_pairs={{0,16},{8,24},{16,0},{24,8},{1,17},{9,25},{17,1},{25,9},{2,18},{10... | collective-permute-start | bytes 602120 | tf_op jit(solution)/shard_map/ppermute | solution.py:1019
  24.3 16.9 %collective-permute-start = (bf16[784,128]{1,0:T(8,128)(2,1)S(1)}, bf16[784,128]{1,0:T(8,128)(2,1)S(1)}, u32[]{:S(2)}, u32[]{:S(2)}) collective-permute-start(bf16[784,128]{1,0:T(8,128)(2,1)S(1)} %concatenate.91), channel_id=1, source_target_pairs={{0,8},{8,0},{16,24},{24,16},{1,9},{9,1},{17,25},{25,17},{2,10},{10... | collective-permute-start | bytes 602120 | tf_op jit(solution)/shard_map/ppermute | solution.py:1019
  43.0 32.5 %all-to-all-start.1 = ((bf16[4,3,784,128]{3,2,1,0:T(8,128)(2,1)}), bf16[4,3,784,128]{3,2,1,0:T(8,128)(2,1)}, u32[]{:S(2)}, u32[]{:S(2)}) async-start(bf16[4,3,784,128]{3,2,1,0:T(8,128)(2,1)} %broadcast_in_dim.115), calls=%async_computation.1 | async-start | bytes 4816896 | tf_op jit(solution)/shard_map/all_to_all | solution.py:1028
  47.7 118.2 %all-gather.3.cloned.1.call-start = ((), (), s32[]{:S(2)}) async-start(), calls=%async_computation.5 | async-start | bytes 4866048 | tf_op jit(solution)/shard_map/all_gather | solution.py:1108
  49.4 9.8 %collective-permute-start.5 = (bf16[768,128]{1,0:T(8,128)(2,1)S(1)}, bf16[768,128]{1,0:T(8,128)(2,1)S(1)}, u32[]{:S(2)}, u32[]{:S(2)}) collective-permute-start(bf16[768,128]{1,0:T(8,128)(2,1)S(1)} %pad_maximum_fusion.18), channel_id=1, source_target_pairs={{0,24},{8,16},{16,8},{24,0},{1,25},{9,17},{17,9},{25,1},{2,26},{10... | collective-permute-start | bytes 589832 | tf_op jit(solution)/shard_map/ppermute | solution.py:1019
  51.9 15.7 %collective-permute-start.4 = (bf16[768,128]{1,0:T(8,128)(2,1)S(1)}, bf16[768,128]{1,0:T(8,128)(2,1)S(1)}, u32[]{:S(2)}, u32[]{:S(2)}) collective-permute-start(bf16[768,128]{1,0:T(8,128)(2,1)S(1)} %pad_maximum_fusion.18), channel_id=1, source_target_pairs={{0,16},{8,24},{16,0},{24,8},{1,17},{9,25},{17,1},{25,9},{2,18},{10... | collective-permute-start | bytes 589832 | tf_op jit(solution)/shard_map/ppermute | solution.py:1019
  51.9 15.7 %collective-permute-start.3 = (bf16[768,128]{1,0:T(8,128)(2,1)S(1)}, bf16[768,128]{1,0:T(8,128)(2,1)S(1)}, u32[]{:S(2)}, u32[]{:S(2)}) collective-permute-start(bf16[768,128]{1,0:T(8,128)(2,1)S(1)} %pad_maximum_fusion.18), channel_id=1, source_target_pairs={{0,8},{8,0},{16,24},{24,16},{1,9},{9,1},{17,25},{25,17},{2,10},{10... | collective-permute-start | bytes 589832 | tf_op jit(solution)/shard_map/ppermute | solution.py:1019
  67.6 130.4 %all-gather.5.cloned.1.call-start = ((), (), s32[]{:S(2)}) async-start(), calls=%async_computation.7 | async-start | bytes 1310720 | tf_op jit(solution)/shard_map/all_gather | solution.py:1147
  75.5 8.9 %collective-permute-start.7 = (bf16[4,3,784,128]{3,2,1,0:T(8,128)(2,1)}, bf16[4,3,784,128]{3,2,1,0:T(8,128)(2,1)}, u32[]{:S(2)}, u32[]{:S(2)}) collective-permute-start(bf16[4,3,784,128]{3,2,1,0:T(8,128)(2,1)} %all-to-all-done.1.refs_2_), channel_id=1, source_target_pairs={{0,1},{1,0},{2,3},{3,2},{4,5},{5,4},{6,7},{7,6},{8,9},{9,8},{10,11... | collective-permute-start | bytes 7225352 | tf_op jit(solution)/shard_map/ppermute | solution.py:1019
  75.5 8.9 %collective-permute-start.6 = (bf16[4,1552,128]{2,1,0:T(8,128)(2,1)S(1)}, bf16[4,1552,128]{2,1,0:T(8,128)(2,1)}, u32[]{:S(2)}, u32[]{:S(2)}) collective-permute-start(bf16[4,1552,128]{2,1,0:T(8,128)(2,1)S(1)} %all-to-all-done.refs_0_), channel_id=1, source_target_pairs={{0,1},{1,0},{2,3},{3,2},{4,5},{5,4},{6,7},{7,6},{8,9},{9,8},{10,11... | collective-permute-start | bytes 4767752 | tf_op jit(solution)/shard_map/ppermute | solution.py:1019
  76.2 34.9 %collective-permute-start.8 = (bf16[3,768,128]{2,1,0:T(8,128)(2,1)S(1)}, bf16[3,768,128]{2,1,0:T(8,128)(2,1)}, u32[]{:S(2)}, u32[]{:S(2)}) collective-permute-start(bf16[3,768,128]{2,1,0:T(8,128)(2,1)S(1)} %pad_maximum_fusion.5.refs_2_), channel_id=1, source_target_pairs={{0,2},{2,0},{4,6},{6,4},{1,3},{3,1},{5,7},{7,5},{8,10},{10,8},{12,... | collective-permute-start | bytes 1769480 | tf_op jit(solution)/shard_map/ppermute | solution.py:1019
  77.7 33.4 %collective-permute-start.9 = (bf16[3,768,128]{2,1,0:T(8,128)(2,1)S(1)}, bf16[3,768,128]{2,1,0:T(8,128)(2,1)}, u32[]{:S(2)}, u32[]{:S(2)}) collective-permute-start(bf16[3,768,128]{2,1,0:T(8,128)(2,1)S(1)} %pad_maximum_fusion.5.refs_2_), channel_id=1, source_target_pairs={{0,4},{2,6},{4,0},{6,2},{1,5},{3,7},{5,1},{7,3},{8,12},{10,14},{12... | collective-permute-start | bytes 1769480 | tf_op jit(solution)/shard_map/ppermute | solution.py:1019
  78.2 32.9 %collective-permute-start.10 = (bf16[3,768,128]{2,1,0:T(8,128)(2,1)S(1)}, bf16[3,768,128]{2,1,0:T(8,128)(2,1)}, u32[]{:S(2)}, u32[]{:S(2)}) collective-permute-start(bf16[3,768,128]{2,1,0:T(8,128)(2,1)S(1)} %pad_maximum_fusion.5.refs_2_), channel_id=1, source_target_pairs={{0,6},{2,4},{4,2},{6,0},{1,7},{3,5},{5,3},{7,1},{8,14},{10,12},{12... | collective-permute-start | bytes 1769480 | tf_op jit(solution)/shard_map/ppermute | solution.py:1019
  111.8 4.5 %collective-permute-start.14 = (bf16[3,768,128]{2,1,0:T(8,128)(2,1)}, bf16[3,768,128]{2,1,0:T(8,128)(2,1)}, u32[]{:S(2)}, u32[]{:S(2)}) collective-permute-start(bf16[3,768,128]{2,1,0:T(8,128)(2,1)} %collective-permute-done.10.refs_5_), channel_id=1, source_target_pairs={{0,1},{1,0},{2,3},{3,2},{4,5},{5,4},{6,7},{7,6},{8,9},{9,8},{10,11... | collective-permute-start | bytes 1769480 | tf_op jit(solution)/shard_map/ppermute | solution.py:1019
  147.0 10.2 %collective-permute-start.17 = (bf16[128,1024]{1,0:T(8,128)(2,1)S(1)}, bf16[128,1024]{1,0:T(8,128)(2,1)S(1)}, u32[]{:S(2)}, u32[]{:S(2)}) collective-permute-start(bf16[128,1024]{1,0:T(8,128)(2,1)S(1)} %multiply_convert_fusion.2), channel_id=1, source_target_pairs={{0,6},{2,4},{4,2},{6,0},{1,7},{3,5},{5,3},{7,1},{8,14},{10,12},{12... | collective-permute-start | bytes 786440 | tf_op jit(solution)/shard_map/ppermute | solution.py:1019
  148.5 14.4 %collective-permute-start.16 = (bf16[128,1024]{1,0:T(8,128)(2,1)S(1)}, bf16[128,1024]{1,0:T(8,128)(2,1)}, u32[]{:S(2)}, u32[]{:S(2)}) collective-permute-start(bf16[128,1024]{1,0:T(8,128)(2,1)S(1)} %multiply_convert_fusion.2), channel_id=1, source_target_pairs={{0,4},{2,6},{4,0},{6,2},{1,5},{3,7},{5,1},{7,3},{8,12},{10,14},{12... | collective-permute-start | bytes 786440 | tf_op jit(solution)/shard_map/ppermute | solution.py:1019
  149.9 13.9 %collective-permute-start.15 = (bf16[128,1024]{1,0:T(8,128)(2,1)S(1)}, bf16[128,1024]{1,0:T(8,128)(2,1)}, u32[]{:S(2)}, u32[]{:S(2)}) collective-permute-start(bf16[128,1024]{1,0:T(8,128)(2,1)S(1)} %multiply_convert_fusion.2), channel_id=1, source_target_pairs={{0,2},{2,0},{4,6},{6,4},{1,3},{3,1},{5,7},{7,5},{8,10},{10,8},{12,... | collective-permute-start | bytes 786440 | tf_op jit(solution)/shard_map/ppermute | solution.py:1019
  151.8 148.8 %reduce-scatter.2.cloned.1.call-start = ((), (), s32[]{:S(2)}) async-start(), calls=%async_computation.8 | async-start | bytes 5013504 | tf_op jit(solution)/shard_map/reduce_scatter | solution.py:1177
  178.6 19.4 %collective-permute-start.18 = (bf16[128,1024]{1,0:T(8,128)(2,1)}, bf16[128,1024]{1,0:T(8,128)(2,1)}, u32[]{:S(2)}, u32[]{:S(2)}) collective-permute-start(bf16[128,1024]{1,0:T(8,128)(2,1)} %get-tuple-element.384), channel_id=1, source_target_pairs={{0,2},{2,0},{4,6},{6,4},{1,3},{3,1},{5,7},{7,5},{8,10},{10,8},{12,... | collective-permute-start | bytes 786440 | tf_op jit(solution)/shard_map/ppermute | solution.py:1019
  179.3 18.7 %collective-permute-start.19 = (bf16[128,1024]{1,0:T(8,128)(2,1)}, bf16[128,1024]{1,0:T(8,128)(2,1)}, u32[]{:S(2)}, u32[]{:S(2)}) collective-permute-start(bf16[128,1024]{1,0:T(8,128)(2,1)} %get-tuple-element.383), channel_id=1, source_target_pairs={{0,4},{2,6},{4,0},{6,2},{1,5},{3,7},{5,1},{7,3},{8,12},{10,14},{12... | collective-permute-start | bytes 786440 | tf_op jit(solution)/shard_map/ppermute | solution.py:1019
  180.4 17.6 %collective-permute-start.20 = (bf16[128,1024]{1,0:T(8,128)(2,1)}, bf16[128,1024]{1,0:T(8,128)(2,1)}, u32[]{:S(2)}, u32[]{:S(2)}) collective-permute-start(bf16[128,1024]{1,0:T(8,128)(2,1)} %get-tuple-element.382), channel_id=1, source_target_pairs={{0,6},{2,4},{4,2},{6,0},{1,7},{3,5},{5,3},{7,1},{8,14},{10,12},{12... | collective-permute-start | bytes 786440 | tf_op jit(solution)/shard_map/ppermute | solution.py:1019
  198.0 168.6 %all-reduce.4.cloned.1.call-start = ((), (), s32[]{:S(2)}) async-start(), calls=%async_computation.6 | async-start | bytes 2097152 | tf_op jit(solution)/shard_map/psum | solution.py:1227
  204.3 24.0 %collective-permute-start.21 = (bf16[128,1536]{1,0:T(8,128)(2,1)S(1)}, bf16[128,1536]{1,0:T(8,128)(2,1)S(1)}, u32[]{:S(2)}, u32[]{:S(2)}) collective-permute-start(bf16[128,1536]{1,0:T(8,128)(2,1)S(1)} %get-tuple-element.430), channel_id=1, source_target_pairs={{0,2},{2,0},{4,6},{6,4},{1,3},{3,1},{5,7},{7,5},{8,10},{10,8},{12,... | collective-permute-start | bytes 1179656 | tf_op jit(solution)/shard_map/ppermute | solution.py:1019
  205.2 23.1 %collective-permute-start.22 = (bf16[128,1536]{1,0:T(8,128)(2,1)S(1)}, bf16[128,1536]{1,0:T(8,128)(2,1)S(1)}, u32[]{:S(2)}, u32[]{:S(2)}) collective-permute-start(bf16[128,1536]{1,0:T(8,128)(2,1)S(1)} %get-tuple-element.431), channel_id=1, source_target_pairs={{0,4},{2,6},{4,0},{6,2},{1,5},{3,7},{5,1},{7,3},{8,12},{10,14},{12... | collective-permute-start | bytes 1179656 | tf_op jit(solution)/shard_map/ppermute | solution.py:1019
  206.2 22.2 %collective-permute-start.23 = (bf16[128,1536]{1,0:T(8,128)(2,1)S(1)}, bf16[128,1536]{1,0:T(8,128)(2,1)S(1)}, u32[]{:S(2)}, u32[]{:S(2)}) collective-permute-start(bf16[128,1536]{1,0:T(8,128)(2,1)S(1)} %get-tuple-element.429), channel_id=1, source_target_pairs={{0,6},{2,4},{4,2},{6,0},{1,7},{3,5},{5,3},{7,1},{8,14},{10,12},{12... | collective-permute-start | bytes 1179656 | tf_op jit(solution)/shard_map/ppermute | solution.py:1019
  230.5 10.9 %collective-permute-start.24 = (bf16[128,1280]{1,0:T(8,128)(2,1)S(1)}, bf16[128,1280]{1,0:T(8,128)(2,1)S(1)}, u32[]{:S(2)}, u32[]{:S(2)}) collective-permute-start(bf16[128,1280]{1,0:T(8,128)(2,1)S(1)} %get-tuple-element.422), channel_id=1, source_target_pairs={{0,2},{2,0},{4,6},{6,4},{1,3},{3,1},{5,7},{7,5},{8,10},{10,8},{12,... | collective-permute-start | bytes 983048 | tf_op jit(solution)/shard_map/ppermute | solution.py:1019
  231.4 13.2 %collective-permute-start.25 = (bf16[128,1280]{1,0:T(8,128)(2,1)S(1)}, bf16[128,1280]{1,0:T(8,128)(2,1)S(1)}, u32[]{:S(2)}, u32[]{:S(2)}) collective-permute-start(bf16[128,1280]{1,0:T(8,128)(2,1)S(1)} %get-tuple-element.423), channel_id=1, source_target_pairs={{0,4},{2,6},{4,0},{6,2},{1,5},{3,7},{5,1},{7,3},{8,12},{10,14},{12... | collective-permute-start | bytes 983048 | tf_op jit(solution)/shard_map/ppermute | solution.py:1019
  232.3 14.4 %collective-permute-start.26 = (bf16[128,1280]{1,0:T(8,128)(2,1)S(1)}, bf16[128,1280]{1,0:T(8,128)(2,1)S(1)}, u32[]{:S(2)}, u32[]{:S(2)}) collective-permute-start(bf16[128,1280]{1,0:T(8,128)(2,1)S(1)} %get-tuple-element.421), channel_id=1, source_target_pairs={{0,6},{2,4},{4,2},{6,0},{1,7},{3,5},{5,3},{7,1},{8,14},{10,12},{12... | collective-permute-start | bytes 983048 | tf_op jit(solution)/shard_map/ppermute | solution.py:1019
  246.7 18.6 %collective-permute-start.27 = (bf16[128,1536]{1,0:T(8,128)(2,1)S(1)}, bf16[128,1536]{1,0:T(8,128)(2,1)S(1)}, u32[]{:S(2)}, u32[]{:S(2)}) collective-permute-start(bf16[128,1536]{1,0:T(8,128)(2,1)S(1)} %get-tuple-element.192), channel_id=1, source_target_pairs={{0,2},{2,0},{4,6},{6,4},{1,3},{3,1},{5,7},{7,5},{8,10},{10,8},{12,... | collective-permute-start | bytes 1179656 | tf_op jit(solution)/shard_map/ppermute | solution.py:1019
  247.1 18.2 %collective-permute-start.28 = (bf16[128,1536]{1,0:T(8,128)(2,1)S(1)}, bf16[128,1536]{1,0:T(8,128)(2,1)S(1)}, u32[]{:S(2)}, u32[]{:S(2)}) collective-permute-start(bf16[128,1536]{1,0:T(8,128)(2,1)S(1)} %get-tuple-element.193), channel_id=1, source_target_pairs={{0,4},{2,6},{4,0},{6,2},{1,5},{3,7},{5,1},{7,3},{8,12},{10,14},{12... | collective-permute-start | bytes 1179656 | tf_op jit(solution)/shard_map/ppermute | solution.py:1019
  249.0 16.3 %collective-permute-start.29 = (bf16[128,1536]{1,0:T(8,128)(2,1)S(1)}, bf16[128,1536]{1,0:T(8,128)(2,1)S(1)}, u32[]{:S(2)}, u32[]{:S(2)}) collective-permute-start(bf16[128,1536]{1,0:T(8,128)(2,1)S(1)} %get-tuple-element.194), channel_id=1, source_target_pairs={{0,6},{2,4},{4,2},{6,0},{1,7},{3,5},{5,3},{7,1},{8,14},{10,12},{12... | collective-permute-start | bytes 1179656 | tf_op jit(solution)/shard_map/ppermute | solution.py:1019
  265.4 16.2 %collective-permute-start.33 = (bf16[4,128,1024]{2,1,0:T(8,128)(2,1)S(1)}, bf16[4,128,1024]{2,1,0:T(8,128)(2,1)}, u32[]{:S(2)}, u32[]{:S(2)}) collective-permute-start(bf16[4,128,1024]{2,1,0:T(8,128)(2,1)S(1)} %get-tuple-element.217), channel_id=1, source_target_pairs={{0,1},{1,0},{2,3},{3,2},{4,5},{5,4},{6,7},{7,6},{8,9},{9,8},{10,11... | collective-permute-start | bytes 3145736 | tf_op jit(solution)/shard_map/ppermute | solution.py:1019
  267.1 17.1 %collective-permute-start.30 = (bf16[512,256]{1,0:T(8,128)(2,1)S(1)}, bf16[512,256]{1,0:T(8,128)(2,1)S(1)}, u32[]{:S(2)}, u32[]{:S(2)}) collective-permute-start(bf16[512,256]{1,0:T(8,128)(2,1)S(1)} %get-tuple-element.213), channel_id=1, source_target_pairs={{0,2},{2,0},{4,6},{6,4},{1,3},{3,1},{5,7},{7,5},{8,10},{10,8},{12,... | collective-permute-start | bytes 786440 | tf_op jit(solution)/shard_map/ppermute | solution.py:1019
  267.6 17.2 %collective-permute-start.31 = (bf16[512,256]{1,0:T(8,128)(2,1)}, bf16[512,256]{1,0:T(8,128)(2,1)S(1)}, u32[]{:S(2)}, u32[]{:S(2)}) collective-permute-start(bf16[512,256]{1,0:T(8,128)(2,1)} %get-tuple-element.214), channel_id=1, source_target_pairs={{0,4},{2,6},{4,0},{6,2},{1,5},{3,7},{5,1},{7,3},{8,12},{10,14},{12... | collective-permute-start | bytes 786440 | tf_op jit(solution)/shard_map/ppermute | solution.py:1019
  269.5 16.0 %collective-permute-start.32 = (bf16[512,256]{1,0:T(8,128)(2,1)}, bf16[512,256]{1,0:T(8,128)(2,1)}, u32[]{:S(2)}, u32[]{:S(2)}) collective-permute-start(bf16[512,256]{1,0:T(8,128)(2,1)} %get-tuple-element.215), channel_id=1, source_target_pairs={{0,6},{2,4},{4,2},{6,0},{1,7},{3,5},{5,3},{7,1},{8,14},{10,12},{12... | collective-permute-start | bytes 786440 | tf_op jit(solution)/shard_map/ppermute | solution.py:1019
  286.1 5.5 %collective-permute-start.34 = (bf16[4,128,1280]{2,1,0:T(8,128)(2,1)}, bf16[4,128,1280]{2,1,0:T(8,128)(2,1)}, u32[]{:S(2)}, u32[]{:S(2)}) collective-permute-start(bf16[4,128,1280]{2,1,0:T(8,128)(2,1)} %get-tuple-element.238), channel_id=1, source_target_pairs={{0,1},{1,0},{2,3},{3,2},{4,5},{5,4},{6,7},{7,6},{8,9},{9,8},{10,11... | collective-permute-start | bytes 3932168 | tf_op jit(solution)/shard_map/ppermute | solution.py:1019
  286.4 32.6 %collective-permute-start.35 = (bf16[2,128,1024]{2,1,0:T(8,128)(2,1)}, bf16[2,128,1024]{2,1,0:T(8,128)(2,1)}, u32[]{:S(2)}, u32[]{:S(2)}) collective-permute-start(bf16[2,128,1024]{2,1,0:T(8,128)(2,1)} %slice.368), channel_id=1, source_target_pairs={{0,16},{8,24},{16,0},{24,8},{1,17},{9,25},{17,1},{25,9},{2,18},{10... | collective-permute-start | bytes 1572872 | tf_op jit(solution)/shard_map/ppermute | solution.py:1019
  286.5 32.5 %collective-permute-start.36 = (bf16[1536,256]{1,0:T(8,128)(2,1)}, bf16[1536,256]{1,0:T(8,128)(2,1)}, u32[]{:S(2)}, u32[]{:S(2)}) collective-permute-start(bf16[1536,256]{1,0:T(8,128)(2,1)} %copy-done.34), channel_id=1, source_target_pairs={{0,2},{2,0},{4,6},{6,4},{1,3},{3,1},{5,7},{7,5},{8,10},{10,8},{12,... | collective-permute-start | bytes 2359304 | tf_op jit(solution)/shard_map/ppermute | solution.py:1019
  287.0 32.0 %collective-permute-start.37 = (bf16[1536,256]{1,0:T(8,128)(2,1)S(1)}, bf16[1536,256]{1,0:T(8,128)(2,1)}, u32[]{:S(2)}, u32[]{:S(2)}) collective-permute-start(bf16[1536,256]{1,0:T(8,128)(2,1)S(1)} %copy-done.33), channel_id=1, source_target_pairs={{0,4},{2,6},{4,0},{6,2},{1,5},{3,7},{5,1},{7,3},{8,12},{10,14},{12... | collective-permute-start | bytes 2359304 | tf_op jit(solution)/shard_map/ppermute | solution.py:1019
  288.9 43.3 %collective-permute-start.38 = (bf16[1536,256]{1,0:T(8,128)(2,1)S(1)}, bf16[1536,256]{1,0:T(8,128)(2,1)}, u32[]{:S(2)}, u32[]{:S(2)}) collective-permute-start(bf16[1536,256]{1,0:T(8,128)(2,1)S(1)} %get-tuple-element.247), channel_id=1, source_target_pairs={{0,6},{2,4},{4,2},{6,0},{1,7},{3,5},{5,3},{7,1},{8,14},{10,12},{12... | collective-permute-start | bytes 2359304 | tf_op jit(solution)/shard_map/ppermute | solution.py:1019
  295.9 53.0 %all-to-all-start.2 = ((bf16[4,128,1280]{2,1,0:T(8,128)(2,1)}), bf16[4,128,1280]{2,1,0:T(8,128)(2,1)}, u32[]{:S(2)}, u32[]{:S(2)}) async-start(bf16[4,128,1280]{2,1,0:T(8,128)(2,1)} %pad_maximum_fusion.1), calls=%async_computation.2 | async-start | bytes 2621440 | tf_op jit(solution)/shard_map/all_to_all | solution.py:1269
  335.8 12.1 %collective-permute-start.39 = (bf16[1,128,1024]{2,1,0:T(8,128)(2,1)}, bf16[1,128,1024]{2,1,0:T(8,128)(2,1)}, u32[]{:S(2)}, u32[]{:S(2)}) collective-permute-start(bf16[1,128,1024]{2,1,0:T(8,128)(2,1)} %slice.369), channel_id=1, source_target_pairs={{0,8},{8,0},{16,24},{24,16},{1,9},{9,1},{17,25},{25,17},{2,10},{10... | collective-permute-start | bytes 786440 | tf_op jit(solution)/shard_map/ppermute | solution.py:1019
  349.6 13.9 %all-to-all-start.3 = ((bf16[32,4,128]{2,1,0:T(4,128)(2,1)}), bf16[32,4,128]{2,1,0:T(4,128)(2,1)S(1)}, u32[]{:S(2)}, u32[]{:S(2)}) async-start(bf16[32,4,128]{2,1,0:T(4,128)(2,1)} %bitcast.60), calls=%async_computation.4 | async-start | bytes 65536 | tf_op jit(solution)/shard_map/all_to_all | solution.py:1303
  358.3 6.5 %collective-permute-start.42 = (bf16[128,256]{1,0:T(8,128)(2,1)S(1)}, bf16[128,256]{1,0:T(8,128)(2,1)S(1)}, u32[]{:S(2)}, u32[]{:S(2)}) collective-permute-start(bf16[128,256]{1,0:T(8,128)(2,1)S(1)} %get-tuple-element.407), channel_id=1, source_target_pairs={{0,6},{2,4},{4,2},{6,0},{1,7},{3,5},{5,3},{7,1},{8,14},{10,12},{12... | collective-permute-start | bytes 196616 | tf_op jit(solution)/shard_map/ppermute | solution.py:1019
  361.0 4.3 %collective-permute-start.41 = (bf16[128,256]{1,0:T(8,128)(2,1)S(1)}, bf16[128,256]{1,0:T(8,128)(2,1)S(1)}, u32[]{:S(2)}, u32[]{:S(2)}) collective-permute-start(bf16[128,256]{1,0:T(8,128)(2,1)S(1)} %get-tuple-element.408), channel_id=1, source_target_pairs={{0,4},{2,6},{4,0},{6,2},{1,5},{3,7},{5,1},{7,3},{8,12},{10,14},{12... | collective-permute-start | bytes 196616 | tf_op jit(solution)/shard_map/ppermute | solution.py:1019
  361.5 4.3 %collective-permute-start.40 = (bf16[128,256]{1,0:T(8,128)(2,1)S(1)}, bf16[128,256]{1,0:T(8,128)(2,1)S(1)}, u32[]{:S(2)}, u32[]{:S(2)}) collective-permute-start(bf16[128,256]{1,0:T(8,128)(2,1)S(1)} %get-tuple-element.406), channel_id=1, source_target_pairs={{0,2},{2,0},{4,6},{6,4},{1,3},{3,1},{5,7},{7,5},{8,10},{10,8},{12,... | collective-permute-start | bytes 196616 | tf_op jit(solution)/shard_map/ppermute | solution.py:1019
  (80 other events, 663.2 us)
Sparse Core Ops, SparseCore 0:
  67.8 48.6 all-gather.2
  151.9 25.5 all-gather.4
  198.1 50.1 reduce-scatter.1
  286.5 73.4 all-reduce.3

commit v3 on v2

--- a/solution.py
+++ b/solution.py
@@ -453,73 +453,56 @@
     return jnp.concatenate(heads, axis=1)
 
 
-def cross_forward_kernel(q_ref, kv_ref, o_ref, lse_ref, scores, probs):
-    span = kv_ref.shape[0]
-    chunk = 256
+def all_stacked(block):
     lanes = lax.broadcasted_iota(jnp.int32, (1, GROUP), 1)
-    outs = []
-    for pair in range(2):
-        query = stacked(q_ref[...], pair, lanes)
-
-        def first(index, best):
-            rows = pl.ds(index * chunk, chunk)
-            part = dot_t(kv_ref[rows, 0:GROUP], query)
-            scores[rows, :] = part
-            return jnp.maximum(best, jnp.max(part, axis=0, keepdims=True))
-
-        best = lax.fori_loop(
-            0, span // chunk, first, jnp.full((1, 2 * GROUP), MASKED, jnp.float32), unroll=2
-        )
-
-        def second(index, total):
-            rows = pl.ds(index * chunk, chunk)
-            part = jnp.exp(scores[rows, :] - best)
-            probs[rows, :] = low(part)
-            return total + jnp.sum(part, axis=0, keepdims=True)
-
-        total = lax.fori_loop(
-            0, span // chunk, second, jnp.zeros((1, 2 * GROUP), jnp.float32), unroll=2
-        )
-        mixed = t_dot(kv_ref[:, GROUP : 2 * GROUP], probs[...])
-        outs.append((mixed / total).T)
-        lse_ref[0, pair : pair + 1, :] = best + jnp.log(total)
-    o_ref[...] = low(unstacked(outs))
+    return jnp.concatenate([stacked(block, 0, lanes), stacked(block, 1, lanes)], axis=0)
+
+
+def all_unstacked(value):
+    return low(unstacked([value[0 : 2 * GROUP], value[2 * GROUP :]]))
+
+
+def pieces(span):
+    return [slice(at, at + 512) for at in range(0, span, 512)]
+
+
+def cross_forward_kernel(q_ref, kv_ref, o_ref, lse_ref, scores):
+    query = all_stacked(q_ref[...])
+    best = jnp.full((1, 4 * GROUP), MASKED, jnp.float32)
+    for rows in pieces(kv_ref.shape[0]):
+        part = dot_t(kv_ref[rows, 0:GROUP], query)
+        scores[rows, :] = part
+        best = jnp.maximum(best, jnp.max(part, axis=0, keepdims=True))
+    total = jnp.zeros((1, 4 * GROUP), jnp.float32)
+    mixed = jnp.zeros((GROUP, 4 * GROUP), jnp.float32)
+    for rows in pieces(kv_ref.shape[0]):
+        part = jnp.exp(scores[rows, :] - best)
+        total = total + jnp.sum(part, axis=0, keepdims=True)
+        mixed = mixed + t_dot(kv_ref[rows, GROUP : 2 * GROUP], low(part))
+    o_ref[...] = all_unstacked((mixed / total).T)
+    lse = best + jnp.log(total)
+    lse_ref[0, 0:1, :] = lse[:, 0 : 2 * GROUP]
+    lse_ref[0, 1:2, :] = lse[:, 2 * GROUP :]
 
 
 def inner_of(dout, out):
     return jnp.sum((high(dout) * high(out)).T, axis=0, keepdims=True)
 
 
-def cross_backward_kernel(q_ref, do_ref, o_ref, kv_ref, lse_ref, dq_ref, dkv_ref, probs, grads):
-    span = kv_ref.shape[0]
-    chunk = 256
-    lanes = lax.broadcasted_iota(jnp.int32, (1, GROUP), 1)
-    queries = []
-    douts = []
-    for pair in range(2):
-        query = stacked(q_ref[...], pair, lanes)
-        dout = stacked(do_ref[...], pair, lanes)
-        inner = inner_of(dout, stacked(o_ref[...], pair, lanes))
-        lse = lse_ref[0, pair : pair + 1, :]
-        columns = slice(pair * 2 * GROUP, (pair + 1) * 2 * GROUP)
-
-        def step(index, carry):
-            rows = pl.ds(index * chunk, chunk)
-            prob = jnp.exp(dot_t(kv_ref[rows, 0:GROUP], query) - lse)
-            grad = prob * (dot_t(kv_ref[rows, GROUP : 2 * GROUP], dout) - inner)
-            probs[rows, columns] = low(prob)
-            grads[rows, columns] = low(grad)
-            return carry
-
-        lax.fori_loop(0, span // chunk, step, 0, unroll=2)
-        queries.append(query)
-        douts.append(dout)
-    query = jnp.concatenate(queries, axis=0)
-    dout = jnp.concatenate(douts, axis=0)
-    dkv_ref[:, 0:GROUP] = low(dot(grads[...], query))
-    dkv_ref[:, GROUP : 2 * GROUP] = low(dot(probs[...], dout))
-    dq = (t_dot(kv_ref[:, 0:GROUP], grads[...]) * DH ** (-0.5)).T
-    dq_ref[...] = low(unstacked([dq[0 : 2 * GROUP], dq[2 * GROUP :]]))
+def cross_backward_kernel(q_ref, do_ref, o_ref, kv_ref, lse_ref, dq_ref, dkv_ref):
+    query = all_stacked(q_ref[...])
+    dout = all_stacked(do_ref[...])
+    inner = inner_of(dout, all_stacked(o_ref[...]))
+    lse = jnp.concatenate([lse_ref[0, 0:1, :], lse_ref[0, 1:2, :]], axis=1)
+    dq = jnp.zeros((GROUP, 4 * GROUP), jnp.float32)
+    for rows in pieces(kv_ref.shape[0]):
+        keys = kv_ref[rows, 0:GROUP]
+        prob = jnp.exp(dot_t(keys, query) - lse)
+        grad = low(prob * (dot_t(kv_ref[rows, GROUP : 2 * GROUP], dout) - inner))
+        dkv_ref[rows, 0:GROUP] = low(dot(grad, query))
+        dkv_ref[rows, GROUP : 2 * GROUP] = low(dot(low(prob), dout))
+        dq = dq + t_dot(keys, grad)
+    dq_ref[...] = all_unstacked((dq * DH ** (-0.5)).T)
 
 
 def self_scores(kv_ref, query, bias_ref, pair):
@@ -623,10 +606,7 @@
         blocks,
         [narrow, tall],
         outs,
-        [
-            pltpu.VMEM((span, 2 * GROUP), jnp.float32),
-            pltpu.VMEM((span, 2 * GROUP), jnp.bfloat16),
-        ],
+        [pltpu.VMEM((span, 4 * GROUP), jnp.float32)],
         cost,
         (query, pairs),
     )
@@ -659,7 +639,7 @@
         blocks,
         [narrow, narrow, narrow, tall, lse],
         outs,
-        [pltpu.VMEM((span, 4 * GROUP), jnp.bfloat16)] * 2,
+        [],
         cost,
         (query, dout, out, pairs, lse_value),
     )
@@ -680,6 +660,47 @@
         cost_estimate=pl.CostEstimate(flops=cost[0], bytes_accessed=cost[1], transcendentals=0),
         name=name,
     )(index, *arguments)
+
+
+def pack_shards(tp, cross_kv, self_q, self_kv, small, self_out, cross_q, cross_out):
+    groups = [[cross_kv, self_q, self_kv, small], [self_out, cross_q, cross_out]]
+    depths = [sum(part.size // GROUP for part in parts) for parts in groups]
+    arguments = [part for parts in groups for part in parts]
+
+    def kernel(*refs):
+        ins, (near, *packs) = refs[: len(arguments)], refs[len(arguments) :]
+        taken = 0
+        above = 0
+        for parts, pack, depth in zip(groups, packs, depths):
+            at = 0
+            for part in parts:
+                rows = part.shape[0]
+                for b in range(part.size // GROUP // rows):
+                    if part.ndim == 3:
+                        pack[at : at + rows, :] = ins[taken][:, b, :]
+                    else:
+                        pack[at : at + rows, :] = ins[taken][:, b * GROUP : (b + 1) * GROUP]
+                    at += rows
+                taken += 1
+            for k in range(tp):
+                near[k, above : above + depth, :] = pack[...]
+            above += depth
+
+    shapes = [(tp, depths[0] + depths[1], GROUP)] + [(depth, GROUP) for depth in depths]
+    whole = [
+        pl.BlockSpec(shape, lambda k, nothing=(0,) * len(shape): nothing) for shape in shapes
+    ]
+    return kernel_call(
+        kernel,
+        "pack_shards",
+        1,
+        [pl.BlockSpec(part.shape, lambda k, at=(0,) * part.ndim: at) for part in arguments],
+        [(spec, shape, jnp.bfloat16) for spec, shape in zip(whole, shapes)],
+        [],
+        (0, 4 * sum(depths) * GROUP, 0),
+        tuple(arguments),
+        limit=56,
+    )
 
 
 def unpack_heads(index, near, far, depth, top, rows_first, width, extra):
@@ -1090,15 +1111,14 @@
             ],
             axis=0,
         )
-        pack_a = jnp.concatenate(
-            [lane_blocks(flatten(cross_kv)), lane_blocks(self_q), lane_blocks(flatten(self_kv)), small],
-            axis=0,
-        )
-        pack_b = jnp.concatenate([self_out, lane_blocks(cross_q), cross_out], axis=0)
+        near, pack_a, pack_b = pack_shards(
+            tp, cross_kv, self_q, self_kv, small, self_out, cross_q, cross_out
+        )
+        gate_up, down = after((gate_up, down), near)
         pack_f = jnp.concatenate([lane_blocks(flatten(gate_up)), down], axis=0)
 
         depth_a, depth_b = pack_a.shape[0], pack_b.shape[0]
-        near = to_everyone(jnp.concatenate([pack_a, pack_b], axis=0))
+        near = exchange_all(near)
         ring_a = gather(pack_a, "seq", seq)
         ring_b = gather(after(pack_b, *ring_a), "seq", seq)
         far_a = to_everyone(after(jnp.stack(ring_a[1:]), near))
@@ -1145,8 +1165,14 @@
         normed_ffn = low(rms_norm(after_cross, gain_rows[2]))
 
         all_cross = lax.all_gather(normed_cross, "tp", axis=0, tiled=True)
-        all_normed = jnp.concatenate(gather(normed_ffn, "tp", tp), axis=0)
-        rounded = jnp.concatenate(from_here(cotangent), axis=0)
+        normed_parts, weight_gate_up, weight_down, own_cotangent, rounded = together(
+            gather(normed_ffn, "tp", tp),
+            weight_gate_up,
+            weight_down,
+            own(cotangent),
+            jnp.concatenate(from_here(cotangent), axis=0),
+        )
+        all_normed = jnp.concatenate(normed_parts, axis=0)
         joined = dot(all_normed, weight_gate_up)
         gate = joined[:, :hidden_width]
         up = joined[:, hidden_width:]
@@ -1179,7 +1205,7 @@
 
         grad_normed = total(grad_parts)
         grad_residual, gain_ffn = norm_backward(after_cross, gain_rows[2], grad_normed)
-        grad_cross = high(own(cotangent)) + grad_residual
+        grad_cross = high(own_cotangent) + grad_residual
         rounded_cross = low(grad_cross)
         cross_operands = [jnp.concatenate([rounded_cross, block], axis=1) for block in o_blocks]
         cross_parts = exchange(cross_operands, "tp")
@@ -1341,6 +1367,7 @@
             and tp & (tp - 1) == 0
             and count == tp
             and rows == GROUP
+            and arrays[1].shape[1] % 512 == 0
             and width == 2 * seq * GROUP
             and arrays[5].shape[1] == 4 * DH
             and arrays[6].shape[2] == 2 * DH

time: 383 us -> 364 us (0.950)
  Pallas kernels: 88.7 us -> 77.8 us
  waiting for transfers between devices: 89.6 us -> 80 us
  starting transfers between devices: 62.4 us -> 68 us
    pallas_call x6 -> x7, Pallas kernels: 48.8 us -> 37.6 us  [kernel_call(): pl.pallas_call(kernel, grid=(blocks,), in_specs=specs, out_specs=[spec fo...]
    ppermute x43, waiting for transfers between devices: 81.6 us -> 71.6 us  [swap(): lax.ppermute(value, axis, [(place, place ^ flip) for place in range(size)])]
    ppermute x43, starting transfers between devices: 43 us -> 49.4 us  [swap(): lax.ppermute(value, axis, [(place, place ^ flip) for place in range(size)])]
    unnamed x170 -> x179, local copies, waits for them, and re-layouts: 27.9 us -> 30.1 us
  transfers between devices with their start and end apart: 51 -> 51, of which waited for: 18 -> 16; matrix products, arithmetic and copies ran while one was open for 23% -> 24% of each run, Pallas kernels for 24% -> 21%
where the time goes in v3:
time: 364 us; the launch traced here: 357 us
  waiting for transfers between devices  80 us (22%)
  Pallas kernels  77.8 us (21%)
  starting transfers between devices  68 us (19%)
  local copies, waits for them, and re-layouts  57.9 us (16%)
  other arithmetic  31.6 us (9%)
  matrix products  26.6 us (7%)
  between operations  15.5 us (4%)
    ppermute x43, waiting for transfers between devices, swap(): lax.ppermute(value, axis, [(place, place ^ flip) for place in range(size)])  71.6 us
    ppermute x43, starting transfers between devices, swap(): lax.ppermute(value, axis, [(place, place ^ flip) for place in range(size)])  49.4 us
    pallas_call x5, Pallas kernels, with_index(): pl.pallas_call(kernel, grid_spec=pltpu.PrefetchScalarGridSpec(num_scalar_...  40.1 us
    pallas_call x7, Pallas kernels, kernel_call(): pl.pallas_call(kernel, grid=(blocks,), in_specs=specs, out_specs=[spec fo...  37.6 us
    unnamed x179, local copies, waits for them, and re-layouts  30.1 us
    dot_general x7, matrix products, dot(): return jnp.dot(left, right, preferred_element_type=jnp.float32)  17.5 us
    all_to_all x2, starting transfers between devices, exchange_all(): return lax.all_to_all(value, 'tp', 0, 0, tiled=True)  9.94 us
    dynamic_update_slice x8, local copies, waits for them, and re-layouts, run(): lax.dynamic_update_slice(memory_grad, parts[k][None], (t ^ k, at, 0))  8.54 us
  transfers between devices with their start and end apart: 51, of which 16 were waited for; matrix products, arithmetic and copies ran while one was open for 24% of the time, Pallas kernels for 21%

profile of v3, /device:TPU:0, one launch (start us, length us, event | category | flops | bytes accessed | tf_op | source)
XLA Modules:
  0.0 357.3 jit_solution(13912162968944530782)
XLA Ops:
  9.4 2.9 pack_shards.1
  12.3 5.3 %all-to-all-start = ((bf16[4,1552,128]{2,1,0:T(8,128)(2,1)}), bf16[4,1552,128]{2,1,0:T(8,128)(2,1)S(1)}, u32[]{:S(2)}, u32[]{:S(2)}) async-start(bf16[4,1552,128]{2,1,0:T(8,128)(2,1)} %get-tuple-element.160), calls=%async_computation | async-start | bytes 3178496 | tf_op jit(solution)/shard_map/all_to_all | solution.py:1049
  19.2 2.6 collective-permute-start.1
  22.0 5.6 %collective-permute-done = bf16[784,128]{1,0:T(8,128)(2,1)S(1)} collective-permute-done((bf16[784,128]{1,0:T(8,128)(2,1)S(1)}, bf16[784,128]{1,0:T(8,128)(2,1)S(1)}, u32[]{:S(2)}, u32[]{:S(2)}) %collective-permute-start) | collective-permute-done | bytes 200736 | tf_op jit(solution)/shard_map/ppermute | solution.py:1040
  27.6 9.1 %collective-permute-done.1 = bf16[784,128]{1,0:T(8,128)(2,1)S(1)} collective-permute-done((bf16[784,128]{1,0:T(8,128)(2,1)S(1)}, bf16[784,128]{1,0:T(8,128)(2,1)S(1)}, u32[]{:S(2)}, u32[]{:S(2)}) %collective-permute-start.1) | collective-permute-done | bytes 200736 | tf_op jit(solution)/shard_map/ppermute | solution.py:1040
  38.8 4.6 %all-to-all-start.1 = ((bf16[4,3,784,128]{3,2,1,0:T(8,128)(2,1)}), bf16[4,3,784,128]{3,2,1,0:T(8,128)(2,1)}, u32[]{:S(2)}, u32[]{:S(2)}) async-start(bf16[4,3,784,128]{3,2,1,0:T(8,128)(2,1)} %broadcast_in_dim.108), calls=%async_computation.1 | async-start | bytes 4816896 | tf_op jit(solution)/shard_map/all_to_all | solution.py:1049
  45.1 3.1 collective-permute-start.3
  50.7 3.6 %collective-permute-done.3 = bf16[768,128]{1,0:T(8,128)(2,1)S(1)} collective-permute-done((bf16[768,128]{1,0:T(8,128)(2,1)S(1)}, bf16[768,128]{1,0:T(8,128)(2,1)S(1)}, u32[]{:S(2)}, u32[]{:S(2)}) %collective-permute-start.3) | collective-permute-done | bytes 196640 | tf_op jit(solution)/shard_map/ppermute | solution.py:1040
  54.4 10.4 %collective-permute-done.4 = bf16[768,128]{1,0:T(8,128)(2,1)S(1)} collective-permute-done((bf16[768,128]{1,0:T(8,128)(2,1)S(1)}, bf16[768,128]{1,0:T(8,128)(2,1)S(1)}, u32[]{:S(2)}, u32[]{:S(2)}) %collective-permute-start.4) | collective-permute-done | bytes 196640 | tf_op jit(solution)/shard_map/ppermute | solution.py:1040
  64.9 6.3 %all-to-all-done.1.refs_2_ = bf16[4,3,784,128]{3,2,1,0:T(8,128)(2,1)} async-done(((bf16[4,3,784,128]{3,2,1,0:T(8,128)(2,1)}), bf16[4,3,784,128]{3,2,1,0:T(8,128)(2,1)}, u32[]{:S(2)}, u32[]{:S(2)}) %all-to-all-start.1) | async-done | bytes 2408480 | tf_op jit(solution)/shard_map/all_to_all | solution.py:1049
  76.5 2.4 copy.151
  80.0 5.5 %unpack_heads.2 = (bf16[1024,1024]{1,0:T(8,128)(2,1)S(1)}, bf16[1024,1024]{1,0:T(8,128)(2,1)S(1)}, bf16[1024,1024]{1,0:T(8,128)(2,1)S(1)}, bf16[4,8,16,128]{3,2,1,0:T(8,128)(2,1)S(1)}) custom-call(s32[3]{0:T(128)S(1)} %pad_add_fusion.index_ref, bf16[4,1552,128]{2,1,0:T(8,128)(2,1)S(1)} %all-to-all-done.refs_0_, ...), custom_call_target="tpu_custom_call" | custom-call | bytes 12845056 | tf_op jit(solution)/shard_map/unpack_heads/pallas_call | solution.py:649
  94.7 3.7 %self_forward.1 = (bf16[128,1024]{1,0:T(8,128)(2,1)S(1)}, f32[4,2,256]{2,1,0:T(2,128)S(1)}) custom-call(bf16[128,1024]{1,0:T(8,128)(2,1)S(1)} %fusion.13.q_ref, bf16[128,1024]{1,0:T(8,128)(2,1)S(1)} %convolution_convert_fusion.3.kv_ref, f32[16,128,128]{2,1,0:T(8,128)S(1)} %copy.152.bias_ref), custom_call_target="tpu_custom_call" | custom-call | flops 67108864 | bytes 786432 | tf_op jit(solution)/shard_map/self_forward/pallas_call | solution.py:566
  98.4 8.4 %fusion.3.kv_ref = bf16[2048,1024]{1,0:T(8,128)(2,1)} fusion(bf16[1024,1024]{1,0:T(8,128)(2,1)S(1)} %copy-done.34, bf16[4,2048,1024]{2,1,0:T(8,128)(2,1)} %memory_ref.1, s32[]{:T(128)S(6)} %select_n.56), kind=kOutput, calls=%fused_computation.3 | convolution fusion | flops 4297064448 | bytes 10485764 | tf_op jit(solution)/shard_map/dot_general | solution.py:412
  109.3 1.9 collective-permute-done.13.refs_8_
  112.0 5.3 %unpack_heads.3 = (bf16[1024,1024]{1,0:T(8,128)(2,1)S(1)}, bf16[1024,1024]{1,0:T(8,128)(2,1)S(1)}, bf16[1024,1024]{1,0:T(8,128)(2,1)S(1)}) custom-call(s32[3]{0:T(128)S(1)} %pad_add_fusion.index_ref, bf16[4,1552,128]{2,1,0:T(8,128)(2,1)S(1)} %all-to-all-done.refs_0_, bf16[4,1552,128]{2,1,0:T(8,128)(2,1)} %collective-permute-done.6.refs_1_, ...), custom_call_target="tpu_custom_call" | custom-call | bytes 12582912 | tf_op jit(solution)/shard_map/unpack_heads/pallas_call | solution.py:649
  121.7 2.2 fusion.14.q_ref
  123.9 2.2 copy-done.39
  126.1 8.4 %cross_forward.1 = (bf16[128,1024]{1,0:T(8,128)(2,1)S(1)}, f32[4,2,256]{2,1,0:T(2,128)S(1)}) custom-call(bf16[128,1024]{1,0:T(8,128)(2,1)S(1)} %fusion.14.q_ref, bf16[2048,1024]{1,0:T(8,128)(2,1)S(1)} %copy-done.39), custom_call_target="tpu_custom_call" | custom-call | flops 1073741824 | bytes 4718592 | tf_op jit(solution)/shard_map/cross_forward/pallas_call | solution.py:566
  139.9 2.5 copy-done.14
  144.5 6.0 %collective-permute-done.16 = bf16[128,1024]{1,0:T(8,128)(2,1)} collective-permute-done((bf16[128,1024]{1,0:T(8,128)(2,1)S(1)}, bf16[128,1024]{1,0:T(8,128)(2,1)}, u32[]{:S(2)}, u32[]{:S(2)}) %collective-permute-start.16) | collective-permute-done | bytes 262176 | tf_op jit(solution)/shard_map/ppermute | solution.py:1040
  152.4 1.8 fusion.69
  155.2 2.0 fusion.12
  157.7 1.8 convolution_convert_fusion
  166.1 3.2 hidden_out.1
  172.9 4.9 %hidden_terms.1 = bf16[1024,2112]{1,0:T(8,128)(2,1)S(1)} custom-call(bf16[512,1024]{1,0:T(8,128)(2,1)S(1)} %copy-done.26, bf16[512,1408]{1,0:T(8,128)(2,1)S(1)} %pad_maximum_fusion.joined_ref, bf16[512,1024]{1,0:T(8,128)(2,1)S(1)} %copy-done.16, bf16[512,704]{1,0:T(8,128)(2,1)S(1)} %copy-done.18), custom_call_target="tpu_custom_call" | custom-call | flops 2214592512 | bytes 10747904 | tf_op jit(solution)/shard_map/hidden_terms/pallas_call | solution.py:566
  177.8 2.1 copy-done
  180.1 2.2 dynamic-slice_bitcast_fusion
  190.6 13.0 %cross_backward.1 = (bf16[128,1024]{1,0:T(8,128)(2,1)S(1)}, bf16[2048,1024]{1,0:T(8,128)(2,1)S(1)}) custom-call(bf16[128,1024]{1,0:T(8,128)(2,1)S(1)} %copy-done.31, bf16[128,1024]{1,0:T(8,128)(2,1)S(1)} %convolution_convert_fusion.2.do_ref, bf16[128,1024]{1,0:T(8,128)(2,1)S(1)} %copy-done.29, bf16[2048,1024]{1,0:T(8,128)(2,1)S(1)} %copy-done.40, ...), custom_call_target="tpu_custom_call" | custom-call | flops 2684354560 | bytes 9437184 | tf_op jit(solution)/shard_map/cross_backward/pallas_call | solution.py:566
  211.0 3.5 self_backward.1
  217.5 4.7 %collective-permute-done.25.refs_6_.refs_26_ = bf16[128,1280]{1,0:T(8,128)(2,1)S(1)} collective-permute-done((bf16[128,1280]{1,0:T(8,128)(2,1)S(1)}, bf16[128,1280]{1,0:T(8,128)(2,1)S(1)}, u32[]{:S(2)}, u32[]{:S(2)}) %collective-permute-start.25) | collective-permute-done | bytes 327712 | tf_op jit(solution)/shard_map/ppermute | solution.py:1040
  222.6 2.1 collective-permute-start.28
  225.9 14.8 %memory_terms.1 = (bf16[4,128,1024]{2,1,0:T(8,128)(2,1)S(1)}, f32[4,128,1024]{2,1,0:T(8,128)S(1)}, bf16[512,256]{1,0:T(8,128)(2,1)S(1)}, bf16[512,256]{1,0:T(8,1...) custom-call(s32[3]{0:T(128)S(1)} %pad_add_fusion.index_ref, ...), custom_call_target="tpu_custom_call" | custom-call | flops 8589934592 | bytes 12582912 | tf_op jit(solution)/shard_map/memory_terms/pallas_call | solution.py:649
  243.1 2.0 collective-permute-start.31
  246.4 11.2 %head_weights.1 = (bf16[4,128,1280]{2,1,0:T(8,128)(2,1)}, f32[4,128,1280]{2,1,0:T(8,128)}) custom-call(s32[3]{0:T(128)} %copy-done.32, bf16[128,1024]{1,0:T(8,128)(2,1)} %get-tuple-element.407.refs_0_, bf16[128,1024]{1,0:T(8,128)(2,1)} %get-tuple-element.406.refs_1_, bf16[128,1024]{1,0:T(8,128)(2,1)} %get-tuple-element.405.refs_2_, ...), custom_call_target="tpu_custom_call" | custom-call | flops 1342177280 | bytes 6291456 | tf_op jit(solution)/shard_map/head_weights/pallas_call | solution.py:649
  262.8 2.0 collective-permute-start.37
  266.0 3.8 %collective-permute-start.35 = (bf16[2,128,1024]{2,1,0:T(8,128)(2,1)}, bf16[2,128,1024]{2,1,0:T(8,128)(2,1)}, u32[]{:S(2)}, u32[]{:S(2)}) collective-permute-start(bf16[2,128,1024]{2,1,0:T(8,128)(2,1)} %slice.332), channel_id=1, source_target_pairs={{0,16},{8,24},{16,0},{24,8},{1,17},{9,25},{17,1},{25,9},{2,18},{10... | collective-permute-start | bytes 1572872 | tf_op jit(solution)/shard_map/ppermute | solution.py:1040
  271.6 2.6 add_convert_fusion
  275.6 4.3 %all-to-all-start.2 = ((bf16[4,128,1280]{2,1,0:T(8,128)(2,1)}), bf16[4,128,1280]{2,1,0:T(8,128)(2,1)}, u32[]{:S(2)}, u32[]{:S(2)}) async-start(bf16[4,128,1280]{2,1,0:T(8,128)(2,1)} %pad_maximum_fusion.1), calls=%async_computation.2 | async-start | bytes 2621440 | tf_op jit(solution)/shard_map/all_to_all | solution.py:1295
  279.9 2.1 convert_element_type.201
  282.1 26.1 %collective-permute-done.35 = bf16[2,128,1024]{2,1,0:T(8,128)(2,1)} collective-permute-done((bf16[2,128,1024]{2,1,0:T(8,128)(2,1)}, bf16[2,128,1024]{2,1,0:T(8,128)(2,1)}, u32[]{:S(2)}, u32[]{:S(2)}) %collective-permute-start.35) | collective-permute-done | bytes 524320 | tf_op jit(solution)/shard_map/ppermute | solution.py:1040
  311.5 2.3 collective-permute-start.39
  315.3 2.2 bitcast_dynamic-update-slice_fusion.2
  322.2 2.1 bitcast_dynamic-update-slice_fusion.1
  324.4 2.1 bitcast_dynamic-update-slice_fusion
  327.6 1.8 convert_dynamic-update-slice_fusion
  334.7 4.1 %all-to-all-start.3 = ((bf16[32,4,128]{2,1,0:T(4,128)(2,1)}), bf16[32,4,128]{2,1,0:T(4,128)(2,1)S(1)}, u32[]{:S(2)}, u32[]{:S(2)}) async-start(bf16[32,4,128]{2,1,0:T(4,128)(2,1)} %bitcast.60), calls=%async_computation.4 | async-start | bytes 65536 | tf_op jit(solution)/shard_map/all_to_all | solution.py:1329
  348.3 2.3 copy.211
  (381 shorter events, 112.6 us)
Async XLA Ops:
  12.3 24.7 %all-to-all-start = ((bf16[4,1552,128]{2,1,0:T(8,128)(2,1)}), bf16[4,1552,128]{2,1,0:T(8,128)(2,1)S(1)}, u32[]{:S(2)}, u32[]{:S(2)}) async-start(bf16[4,1552,128]{2,1,0:T(8,128)(2,1)} %get-tuple-element.160), calls=%async_computation | async-start | bytes 3178496 | tf_op jit(solution)/shard_map/all_to_all | solution.py:1049
  17.6 9.9 %collective-permute-start = (bf16[784,128]{1,0:T(8,128)(2,1)S(1)}, bf16[784,128]{1,0:T(8,128)(2,1)S(1)}, u32[]{:S(2)}, u32[]{:S(2)}) collective-permute-start(bf16[784,128]{1,0:T(8,128)(2,1)S(1)} %copy-done.78), channel_id=1, source_target_pairs={{0,8},{8,0},{16,24},{24,16},{1,9},{9,1},{17,25},{25,17},{2,10},{10... | collective-permute-start | bytes 602120 | tf_op jit(solution)/shard_map/ppermute | solution.py:1040
  19.2 17.4 %collective-permute-start.1 = (bf16[784,128]{1,0:T(8,128)(2,1)S(1)}, bf16[784,128]{1,0:T(8,128)(2,1)S(1)}, u32[]{:S(2)}, u32[]{:S(2)}) collective-permute-start(bf16[784,128]{1,0:T(8,128)(2,1)S(1)} %copy-done.78), channel_id=1, source_target_pairs={{0,16},{8,24},{16,0},{24,8},{1,17},{9,25},{17,1},{25,9},{2,18},{10... | collective-permute-start | bytes 602120 | tf_op jit(solution)/shard_map/ppermute | solution.py:1040
  21.8 14.8 %collective-permute-start.2 = (bf16[784,128]{1,0:T(8,128)(2,1)S(1)}, bf16[784,128]{1,0:T(8,128)(2,1)S(1)}, u32[]{:S(2)}, u32[]{:S(2)}) collective-permute-start(bf16[784,128]{1,0:T(8,128)(2,1)S(1)} %copy-done.78), channel_id=1, source_target_pairs={{0,24},{8,16},{16,8},{24,0},{1,25},{9,17},{17,9},{25,1},{2,26},{10... | collective-permute-start | bytes 602120 | tf_op jit(solution)/shard_map/ppermute | solution.py:1040
  38.8 32.4 %all-to-all-start.1 = ((bf16[4,3,784,128]{3,2,1,0:T(8,128)(2,1)}), bf16[4,3,784,128]{3,2,1,0:T(8,128)(2,1)}, u32[]{:S(2)}, u32[]{:S(2)}) async-start(bf16[4,3,784,128]{3,2,1,0:T(8,128)(2,1)} %broadcast_in_dim.108), calls=%async_computation.1 | async-start | bytes 4816896 | tf_op jit(solution)/shard_map/all_to_all | solution.py:1049
  43.5 96.4 %all-gather.3.cloned.1.call-start = ((), (), s32[]{:S(2)}) async-start(), calls=%async_computation.5 | async-start | bytes 4866048 | tf_op jit(solution)/shard_map/all_gather | solution.py:1128
  45.1 9.3 %collective-permute-start.3 = (bf16[768,128]{1,0:T(8,128)(2,1)S(1)}, bf16[768,128]{1,0:T(8,128)(2,1)S(1)}, u32[]{:S(2)}, u32[]{:S(2)}) collective-permute-start(bf16[768,128]{1,0:T(8,128)(2,1)S(1)} %copy-done.79), channel_id=1, source_target_pairs={{0,8},{8,0},{16,24},{24,16},{1,9},{9,1},{17,25},{25,17},{2,10},{10... | collective-permute-start | bytes 589832 | tf_op jit(solution)/shard_map/ppermute | solution.py:1040
  48.2 16.6 %collective-permute-start.4 = (bf16[768,128]{1,0:T(8,128)(2,1)S(1)}, bf16[768,128]{1,0:T(8,128)(2,1)S(1)}, u32[]{:S(2)}, u32[]{:S(2)}) collective-permute-start(bf16[768,128]{1,0:T(8,128)(2,1)S(1)} %copy-done.79), channel_id=1, source_target_pairs={{0,16},{8,24},{16,0},{24,8},{1,17},{9,25},{17,1},{25,9},{2,18},{10... | collective-permute-start | bytes 589832 | tf_op jit(solution)/shard_map/ppermute | solution.py:1040
  49.4 15.4 %collective-permute-start.5 = (bf16[768,128]{1,0:T(8,128)(2,1)S(1)}, bf16[768,128]{1,0:T(8,128)(2,1)S(1)}, u32[]{:S(2)}, u32[]{:S(2)}) collective-permute-start(bf16[768,128]{1,0:T(8,128)(2,1)S(1)} %copy-done.79), channel_id=1, source_target_pairs={{0,24},{8,16},{16,8},{24,0},{1,25},{9,17},{17,9},{25,1},{2,26},{10... | collective-permute-start | bytes 589832 | tf_op jit(solution)/shard_map/ppermute | solution.py:1040
  64.8 115.2 %all-gather.5.cloned.1.call-start = ((), (), s32[]{:S(2)}) async-start(), calls=%async_computation.7 | async-start | bytes 1310720 | tf_op jit(solution)/shard_map/all_gather | solution.py:1167
  71.2 8.9 %collective-permute-start.7 = (bf16[4,3,784,128]{3,2,1,0:T(8,128)(2,1)}, bf16[4,3,784,128]{3,2,1,0:T(8,128)(2,1)}, u32[]{:S(2)}, u32[]{:S(2)}) collective-permute-start(bf16[4,3,784,128]{3,2,1,0:T(8,128)(2,1)} %all-to-all-done.1.refs_2_), channel_id=1, source_target_pairs={{0,1},{1,0},{2,3},{3,2},{4,5},{5,4},{6,7},{7,6},{8,9},{9,8},{10,11... | collective-permute-start | bytes 7225352 | tf_op jit(solution)/shard_map/ppermute | solution.py:1040
  71.2 8.9 %collective-permute-start.6 = (bf16[4,1552,128]{2,1,0:T(8,128)(2,1)S(1)}, bf16[4,1552,128]{2,1,0:T(8,128)(2,1)}, u32[]{:S(2)}, u32[]{:S(2)}) collective-permute-start(bf16[4,1552,128]{2,1,0:T(8,128)(2,1)S(1)} %all-to-all-done.refs_0_), channel_id=1, source_target_pairs={{0,1},{1,0},{2,3},{3,2},{4,5},{5,4},{6,7},{7,6},{8,9},{9,8},{10,11... | collective-permute-start | bytes 4767752 | tf_op jit(solution)/shard_map/ppermute | solution.py:1040
  71.8 35.0 %collective-permute-start.10 = (bf16[3,768,128]{2,1,0:T(8,128)(2,1)S(1)}, bf16[3,768,128]{2,1,0:T(8,128)(2,1)}, u32[]{:S(2)}, u32[]{:S(2)}) collective-permute-start(bf16[3,768,128]{2,1,0:T(8,128)(2,1)S(1)} %pad_maximum_fusion.4.refs_2_), channel_id=1, source_target_pairs={{0,6},{2,4},{4,2},{6,0},{1,7},{3,5},{5,3},{7,1},{8,14},{10,12},{12... | collective-permute-start | bytes 1769480 | tf_op jit(solution)/shard_map/ppermute | solution.py:1040
  73.3 33.6 %collective-permute-start.9 = (bf16[3,768,128]{2,1,0:T(8,128)(2,1)S(1)}, bf16[3,768,128]{2,1,0:T(8,128)(2,1)}, u32[]{:S(2)}, u32[]{:S(2)}) collective-permute-start(bf16[3,768,128]{2,1,0:T(8,128)(2,1)S(1)} %pad_maximum_fusion.4.refs_2_), channel_id=1, source_target_pairs={{0,4},{2,6},{4,0},{6,2},{1,5},{3,7},{5,1},{7,3},{8,12},{10,14},{12... | collective-permute-start | bytes 1769480 | tf_op jit(solution)/shard_map/ppermute | solution.py:1040
  74.8 32.7 %collective-permute-start.8 = (bf16[3,768,128]{2,1,0:T(8,128)(2,1)S(1)}, bf16[3,768,128]{2,1,0:T(8,128)(2,1)}, u32[]{:S(2)}, u32[]{:S(2)}) collective-permute-start(bf16[3,768,128]{2,1,0:T(8,128)(2,1)S(1)} %pad_maximum_fusion.4.refs_2_), channel_id=1, source_target_pairs={{0,2},{2,0},{4,6},{6,4},{1,3},{3,1},{5,7},{7,5},{8,10},{10,8},{12,... | collective-permute-start | bytes 1769480 | tf_op jit(solution)/shard_map/ppermute | solution.py:1040
  107.4 4.6 %collective-permute-start.12 = (bf16[3,768,128]{2,1,0:T(8,128)(2,1)}, bf16[3,768,128]{2,1,0:T(8,128)(2,1)}, u32[]{:S(2)}, u32[]{:S(2)}) collective-permute-start(bf16[3,768,128]{2,1,0:T(8,128)(2,1)} %collective-permute-done.8.refs_3_), channel_id=1, source_target_pairs={{0,1},{1,0},{2,3},{3,2},{4,5},{5,4},{6,7},{7,6},{8,9},{9,8},{10,11... | collective-permute-start | bytes 1769480 | tf_op jit(solution)/shard_map/ppermute | solution.py:1040
  135.3 9.2 %collective-permute-start.15 = (bf16[128,1024]{1,0:T(8,128)(2,1)S(1)}, bf16[128,1024]{1,0:T(8,128)(2,1)S(1)}, u32[]{:S(2)}, u32[]{:S(2)}) collective-permute-start(bf16[128,1024]{1,0:T(8,128)(2,1)S(1)} %multiply_convert_fusion.2), channel_id=1, source_target_pairs={{0,2},{2,0},{4,6},{6,4},{1,3},{3,1},{5,7},{7,5},{8,10},{10,8},{12,... | collective-permute-start | bytes 786440 | tf_op jit(solution)/shard_map/ppermute | solution.py:1040
  136.7 13.8 %collective-permute-start.16 = (bf16[128,1024]{1,0:T(8,128)(2,1)S(1)}, bf16[128,1024]{1,0:T(8,128)(2,1)}, u32[]{:S(2)}, u32[]{:S(2)}) collective-permute-start(bf16[128,1024]{1,0:T(8,128)(2,1)S(1)} %multiply_convert_fusion.2), channel_id=1, source_target_pairs={{0,4},{2,6},{4,0},{6,2},{1,5},{3,7},{5,1},{7,3},{8,12},{10,14},{12... | collective-permute-start | bytes 786440 | tf_op jit(solution)/shard_map/ppermute | solution.py:1040
  137.2 13.2 %collective-permute-start.17 = (bf16[128,1024]{1,0:T(8,128)(2,1)S(1)}, bf16[128,1024]{1,0:T(8,128)(2,1)}, u32[]{:S(2)}, u32[]{:S(2)}) collective-permute-start(bf16[128,1024]{1,0:T(8,128)(2,1)S(1)} %multiply_convert_fusion.2), channel_id=1, source_target_pairs={{0,6},{2,4},{4,2},{6,0},{1,7},{3,5},{5,3},{7,1},{8,14},{10,12},{12... | collective-permute-start | bytes 786440 | tf_op jit(solution)/shard_map/ppermute | solution.py:1040
  139.8 140.2 %reduce-scatter.2.cloned.1.call-start = ((), (), s32[]{:S(2)}) async-start(), calls=%async_computation.8 | async-start | bytes 5013504 | tf_op jit(solution)/shard_map/reduce_scatter | solution.py:1203
  160.6 19.4 %collective-permute-start.18 = (bf16[128,1024]{1,0:T(8,128)(2,1)}, bf16[128,1024]{1,0:T(8,128)(2,1)}, u32[]{:S(2)}, u32[]{:S(2)}) collective-permute-start(bf16[128,1024]{1,0:T(8,128)(2,1)} %get-tuple-element.410), channel_id=1, source_target_pairs={{0,2},{2,0},{4,6},{6,4},{1,3},{3,1},{5,7},{7,5},{8,10},{10,8},{12,... | collective-permute-start | bytes 786440 | tf_op jit(solution)/shard_map/ppermute | solution.py:1040
  161.3 18.7 %collective-permute-start.19 = (bf16[128,1024]{1,0:T(8,128)(2,1)}, bf16[128,1024]{1,0:T(8,128)(2,1)}, u32[]{:S(2)}, u32[]{:S(2)}) collective-permute-start(bf16[128,1024]{1,0:T(8,128)(2,1)} %get-tuple-element.409), channel_id=1, source_target_pairs={{0,4},{2,6},{4,0},{6,2},{1,5},{3,7},{5,1},{7,3},{8,12},{10,14},{12... | collective-permute-start | bytes 786440 | tf_op jit(solution)/shard_map/ppermute | solution.py:1040
  162.6 17.3 %collective-permute-start.20 = (bf16[128,1024]{1,0:T(8,128)(2,1)}, bf16[128,1024]{1,0:T(8,128)(2,1)}, u32[]{:S(2)}, u32[]{:S(2)}) collective-permute-start(bf16[128,1024]{1,0:T(8,128)(2,1)} %get-tuple-element.408), channel_id=1, source_target_pairs={{0,6},{2,4},{4,2},{6,0},{1,7},{3,5},{5,3},{7,1},{8,14},{10,12},{12... | collective-permute-start | bytes 786440 | tf_op jit(solution)/shard_map/ppermute | solution.py:1040
  180.0 168.3 %all-reduce.4.cloned.1.call-start = ((), (), s32[]{:S(2)}) async-start(), calls=%async_computation.6 | async-start | bytes 2097152 | tf_op jit(solution)/shard_map/psum | solution.py:1253
  186.2 17.3 %collective-permute-start.21 = (bf16[128,1536]{1,0:T(8,128)(2,1)S(1)}, bf16[128,1536]{1,0:T(8,128)(2,1)S(1)}, u32[]{:S(2)}, u32[]{:S(2)}) collective-permute-start(bf16[128,1536]{1,0:T(8,128)(2,1)S(1)} %get-tuple-element.456), channel_id=1, source_target_pairs={{0,2},{2,0},{4,6},{6,4},{1,3},{3,1},{5,7},{7,5},{8,10},{10,8},{12,... | collective-permute-start | bytes 1179656 | tf_op jit(solution)/shard_map/ppermute | solution.py:1040
  187.0 17.6 %collective-permute-start.22 = (bf16[128,1536]{1,0:T(8,128)(2,1)S(1)}, bf16[128,1536]{1,0:T(8,128)(2,1)S(1)}, u32[]{:S(2)}, u32[]{:S(2)}) collective-permute-start(bf16[128,1536]{1,0:T(8,128)(2,1)S(1)} %get-tuple-element.457), channel_id=1, source_target_pairs={{0,4},{2,6},{4,0},{6,2},{1,5},{3,7},{5,1},{7,3},{8,12},{10,14},{12... | collective-permute-start | bytes 1179656 | tf_op jit(solution)/shard_map/ppermute | solution.py:1040
  188.3 16.2 %collective-permute-start.23 = (bf16[128,1536]{1,0:T(8,128)(2,1)S(1)}, bf16[128,1536]{1,0:T(8,128)(2,1)S(1)}, u32[]{:S(2)}, u32[]{:S(2)}) collective-permute-start(bf16[128,1536]{1,0:T(8,128)(2,1)S(1)} %get-tuple-element.455), channel_id=1, source_target_pairs={{0,6},{2,4},{4,2},{6,0},{1,7},{3,5},{5,3},{7,1},{8,14},{10,12},{12... | collective-permute-start | bytes 1179656 | tf_op jit(solution)/shard_map/ppermute | solution.py:1040
  206.6 10.9 %collective-permute-start.24 = (bf16[128,1280]{1,0:T(8,128)(2,1)S(1)}, bf16[128,1280]{1,0:T(8,128)(2,1)S(1)}, u32[]{:S(2)}, u32[]{:S(2)}) collective-permute-start(bf16[128,1280]{1,0:T(8,128)(2,1)S(1)} %get-tuple-element.448), channel_id=1, source_target_pairs={{0,2},{2,0},{4,6},{6,4},{1,3},{3,1},{5,7},{7,5},{8,10},{10,8},{12,... | collective-permute-start | bytes 983048 | tf_op jit(solution)/shard_map/ppermute | solution.py:1040
  208.1 14.0 %collective-permute-start.25 = (bf16[128,1280]{1,0:T(8,128)(2,1)S(1)}, bf16[128,1280]{1,0:T(8,128)(2,1)S(1)}, u32[]{:S(2)}, u32[]{:S(2)}) collective-permute-start(bf16[128,1280]{1,0:T(8,128)(2,1)S(1)} %get-tuple-element.449), channel_id=1, source_target_pairs={{0,4},{2,6},{4,0},{6,2},{1,5},{3,7},{5,1},{7,3},{8,12},{10,14},{12... | collective-permute-start | bytes 983048 | tf_op jit(solution)/shard_map/ppermute | solution.py:1040
  208.7 13.8 %collective-permute-start.26 = (bf16[128,1280]{1,0:T(8,128)(2,1)S(1)}, bf16[128,1280]{1,0:T(8,128)(2,1)S(1)}, u32[]{:S(2)}, u32[]{:S(2)}) collective-permute-start(bf16[128,1280]{1,0:T(8,128)(2,1)S(1)} %get-tuple-element.447), channel_id=1, source_target_pairs={{0,6},{2,4},{4,2},{6,0},{1,7},{3,5},{5,3},{7,1},{8,14},{10,12},{12... | collective-permute-start | bytes 983048 | tf_op jit(solution)/shard_map/ppermute | solution.py:1040
  222.4 18.7 %collective-permute-start.27 = (bf16[128,1536]{1,0:T(8,128)(2,1)S(1)}, bf16[128,1536]{1,0:T(8,128)(2,1)S(1)}, u32[]{:S(2)}, u32[]{:S(2)}) collective-permute-start(bf16[128,1536]{1,0:T(8,128)(2,1)S(1)} %get-tuple-element.218), channel_id=1, source_target_pairs={{0,2},{2,0},{4,6},{6,4},{1,3},{3,1},{5,7},{7,5},{8,10},{10,8},{12,... | collective-permute-start | bytes 1179656 | tf_op jit(solution)/shard_map/ppermute | solution.py:1040
  222.6 18.5 %collective-permute-start.28 = (bf16[128,1536]{1,0:T(8,128)(2,1)S(1)}, bf16[128,1536]{1,0:T(8,128)(2,1)S(1)}, u32[]{:S(2)}, u32[]{:S(2)}) collective-permute-start(bf16[128,1536]{1,0:T(8,128)(2,1)S(1)} %get-tuple-element.219), channel_id=1, source_target_pairs={{0,4},{2,6},{4,0},{6,2},{1,5},{3,7},{5,1},{7,3},{8,12},{10,14},{12... | collective-permute-start | bytes 1179656 | tf_op jit(solution)/shard_map/ppermute | solution.py:1040
  224.7 16.4 %collective-permute-start.29 = (bf16[128,1536]{1,0:T(8,128)(2,1)S(1)}, bf16[128,1536]{1,0:T(8,128)(2,1)S(1)}, u32[]{:S(2)}, u32[]{:S(2)}) collective-permute-start(bf16[128,1536]{1,0:T(8,128)(2,1)S(1)} %get-tuple-element.220), channel_id=1, source_target_pairs={{0,6},{2,4},{4,2},{6,0},{1,7},{3,5},{5,3},{7,1},{8,14},{10,12},{12... | collective-permute-start | bytes 1179656 | tf_op jit(solution)/shard_map/ppermute | solution.py:1040
  241.1 16.4 %collective-permute-start.33 = (bf16[4,128,1024]{2,1,0:T(8,128)(2,1)S(1)}, bf16[4,128,1024]{2,1,0:T(8,128)(2,1)}, u32[]{:S(2)}, u32[]{:S(2)}) collective-permute-start(bf16[4,128,1024]{2,1,0:T(8,128)(2,1)S(1)} %get-tuple-element.243), channel_id=1, source_target_pairs={{0,1},{1,0},{2,3},{3,2},{4,5},{5,4},{6,7},{7,6},{8,9},{9,8},{10,11... | collective-permute-start | bytes 3145736 | tf_op jit(solution)/shard_map/ppermute | solution.py:1040
  242.9 17.3 %collective-permute-start.30 = (bf16[512,256]{1,0:T(8,128)(2,1)S(1)}, bf16[512,256]{1,0:T(8,128)(2,1)S(1)}, u32[]{:S(2)}, u32[]{:S(2)}) collective-permute-start(bf16[512,256]{1,0:T(8,128)(2,1)S(1)} %get-tuple-element.239), channel_id=1, source_target_pairs={{0,2},{2,0},{4,6},{6,4},{1,3},{3,1},{5,7},{7,5},{8,10},{10,8},{12,... | collective-permute-start | bytes 786440 | tf_op jit(solution)/shard_map/ppermute | solution.py:1040
  243.1 17.6 %collective-permute-start.31 = (bf16[512,256]{1,0:T(8,128)(2,1)}, bf16[512,256]{1,0:T(8,128)(2,1)S(1)}, u32[]{:S(2)}, u32[]{:S(2)}) collective-permute-start(bf16[512,256]{1,0:T(8,128)(2,1)} %get-tuple-element.240), channel_id=1, source_target_pairs={{0,4},{2,6},{4,0},{6,2},{1,5},{3,7},{5,1},{7,3},{8,12},{10,14},{12... | collective-permute-start | bytes 786440 | tf_op jit(solution)/shard_map/ppermute | solution.py:1040
  245.1 16.3 %collective-permute-start.32 = (bf16[512,256]{1,0:T(8,128)(2,1)}, bf16[512,256]{1,0:T(8,128)(2,1)}, u32[]{:S(2)}, u32[]{:S(2)}) collective-permute-start(bf16[512,256]{1,0:T(8,128)(2,1)} %get-tuple-element.241), channel_id=1, source_target_pairs={{0,6},{2,4},{4,2},{6,0},{1,7},{3,5},{5,3},{7,1},{8,14},{10,12},{12... | collective-permute-start | bytes 786440 | tf_op jit(solution)/shard_map/ppermute | solution.py:1040
  262.1 9.2 %collective-permute-start.34 = (bf16[4,128,1280]{2,1,0:T(8,128)(2,1)}, bf16[4,128,1280]{2,1,0:T(8,128)(2,1)}, u32[]{:S(2)}, u32[]{:S(2)}) collective-permute-start(bf16[4,128,1280]{2,1,0:T(8,128)(2,1)} %get-tuple-element.264), channel_id=1, source_target_pairs={{0,1},{1,0},{2,3},{3,2},{4,5},{5,4},{6,7},{7,6},{8,9},{9,8},{10,11... | collective-permute-start | bytes 3932168 | tf_op jit(solution)/shard_map/ppermute | solution.py:1040
  262.4 45.8 %collective-permute-start.36 = (bf16[1536,256]{1,0:T(8,128)(2,1)}, bf16[1536,256]{1,0:T(8,128)(2,1)}, u32[]{:S(2)}, u32[]{:S(2)}) collective-permute-start(bf16[1536,256]{1,0:T(8,128)(2,1)} %copy-done.38), channel_id=1, source_target_pairs={{0,2},{2,0},{4,6},{6,4},{1,3},{3,1},{5,7},{7,5},{8,10},{10,8},{12,... | collective-permute-start | bytes 2359304 | tf_op jit(solution)/shard_map/ppermute | solution.py:1040
  262.8 45.4 %collective-permute-start.37 = (bf16[1536,256]{1,0:T(8,128)(2,1)S(1)}, bf16[1536,256]{1,0:T(8,128)(2,1)}, u32[]{:S(2)}, u32[]{:S(2)}) collective-permute-start(bf16[1536,256]{1,0:T(8,128)(2,1)S(1)} %copy-done.37), channel_id=1, source_target_pairs={{0,4},{2,6},{4,0},{6,2},{1,5},{3,7},{5,1},{7,3},{8,12},{10,14},{12... | collective-permute-start | bytes 2359304 | tf_op jit(solution)/shard_map/ppermute | solution.py:1040
  264.7 43.4 %collective-permute-start.38 = (bf16[1536,256]{1,0:T(8,128)(2,1)S(1)}, bf16[1536,256]{1,0:T(8,128)(2,1)}, u32[]{:S(2)}, u32[]{:S(2)}) collective-permute-start(bf16[1536,256]{1,0:T(8,128)(2,1)S(1)} %get-tuple-element.273), channel_id=1, source_target_pairs={{0,6},{2,4},{4,2},{6,0},{1,7},{3,5},{5,3},{7,1},{8,14},{10,12},{12... | collective-permute-start | bytes 2359304 | tf_op jit(solution)/shard_map/ppermute | solution.py:1040
  266.0 42.2 %collective-permute-start.35 = (bf16[2,128,1024]{2,1,0:T(8,128)(2,1)}, bf16[2,128,1024]{2,1,0:T(8,128)(2,1)}, u32[]{:S(2)}, u32[]{:S(2)}) collective-permute-start(bf16[2,128,1024]{2,1,0:T(8,128)(2,1)} %slice.332), channel_id=1, source_target_pairs={{0,16},{8,24},{16,0},{24,8},{1,17},{9,25},{17,1},{25,9},{2,18},{10... | collective-permute-start | bytes 1572872 | tf_op jit(solution)/shard_map/ppermute | solution.py:1040
  275.6 54.8 %all-to-all-start.2 = ((bf16[4,128,1280]{2,1,0:T(8,128)(2,1)}), bf16[4,128,1280]{2,1,0:T(8,128)(2,1)}, u32[]{:S(2)}, u32[]{:S(2)}) async-start(bf16[4,128,1280]{2,1,0:T(8,128)(2,1)} %pad_maximum_fusion.1), calls=%async_computation.2 | async-start | bytes 2621440 | tf_op jit(solution)/shard_map/all_to_all | solution.py:1295
  311.5 17.8 %collective-permute-start.39 = (bf16[1,128,1024]{2,1,0:T(8,128)(2,1)}, bf16[1,128,1024]{2,1,0:T(8,128)(2,1)}, u32[]{:S(2)}, u32[]{:S(2)}) collective-permute-start(bf16[1,128,1024]{2,1,0:T(8,128)(2,1)} %slice.333), channel_id=1, source_target_pairs={{0,8},{8,0},{16,24},{24,16},{1,9},{9,1},{17,25},{25,17},{2,10},{10... | collective-permute-start | bytes 786440 | tf_op jit(solution)/shard_map/ppermute | solution.py:1040
  331.1 16.4 %collective-permute-start.40 = (bf16[128,256]{1,0:T(8,128)(2,1)S(1)}, bf16[128,256]{1,0:T(8,128)(2,1)S(1)}, u32[]{:S(2)}, u32[]{:S(2)}) collective-permute-start(bf16[128,256]{1,0:T(8,128)(2,1)S(1)} %get-tuple-element.432), channel_id=1, source_target_pairs={{0,2},{2,0},{4,6},{6,4},{1,3},{3,1},{5,7},{7,5},{8,10},{10,8},{12,... | collective-permute-start | bytes 196616 | tf_op jit(solution)/shard_map/ppermute | solution.py:1040
  332.8 14.7 %collective-permute-start.41 = (bf16[128,256]{1,0:T(8,128)(2,1)S(1)}, bf16[128,256]{1,0:T(8,128)(2,1)S(1)}, u32[]{:S(2)}, u32[]{:S(2)}) collective-permute-start(bf16[128,256]{1,0:T(8,128)(2,1)S(1)} %get-tuple-element.434), channel_id=1, source_target_pairs={{0,4},{2,6},{4,0},{6,2},{1,5},{3,7},{5,1},{7,3},{8,12},{10,14},{12... | collective-permute-start | bytes 196616 | tf_op jit(solution)/shard_map/ppermute | solution.py:1040
  333.6 13.9 %collective-permute-start.42 = (bf16[128,256]{1,0:T(8,128)(2,1)S(1)}, bf16[128,256]{1,0:T(8,128)(2,1)S(1)}, u32[]{:S(2)}, u32[]{:S(2)}) collective-permute-start(bf16[128,256]{1,0:T(8,128)(2,1)S(1)} %get-tuple-element.433), channel_id=1, source_target_pairs={{0,6},{2,4},{4,2},{6,0},{1,7},{3,5},{5,3},{7,1},{8,14},{10,12},{12... | collective-permute-start | bytes 196616 | tf_op jit(solution)/shard_map/ppermute | solution.py:1040
  334.7 11.4 %all-to-all-start.3 = ((bf16[32,4,128]{2,1,0:T(4,128)(2,1)}), bf16[32,4,128]{2,1,0:T(4,128)(2,1)S(1)}, u32[]{:S(2)}, u32[]{:S(2)}) async-start(bf16[32,4,128]{2,1,0:T(4,128)(2,1)} %bitcast.60), calls=%async_computation.4 | async-start | bytes 65536 | tf_op jit(solution)/shard_map/all_to_all | solution.py:1329
  (84 other events, 594.6 us)
Sparse Core Ops, SparseCore 0:
  64.9 49.8 all-gather.2
  139.9 31.3 all-gather.4
  180.1 54.1 reduce-scatter.1
  262.5 77.2 all-reduce.3

commit v4 on v3

--- a/solution.py
+++ b/solution.py
@@ -1120,10 +1120,16 @@
         depth_a, depth_b = pack_a.shape[0], pack_b.shape[0]
         near = exchange_all(near)
         ring_a = gather(pack_a, "seq", seq)
+        onehot = (
+            buckets.T[:, :, None] == jnp.arange(NB, dtype=jnp.int32)[None, None, :]
+        ).astype(jnp.bfloat16)
+        start = high(own(decoder_in))
+        unit_self = start * lax.rsqrt(jnp.mean(start * start, axis=-1, keepdims=True) + EPSILON)
+        pack_b, onehot, unit_self = together(pack_b, onehot, unit_self)
         ring_b = gather(after(pack_b, *ring_a), "seq", seq)
         far_a = to_everyone(after(jnp.stack(ring_a[1:]), near))
         far_b = after(jnp.stack(ring_b[1:]), far_a)
-        buckets, decoder_in, cotangent = after((buckets, decoder_in, cotangent), far_b)
+        decoder_in, cotangent = after((decoder_in, cotangent), far_b)
         far_b = gather(far_b, "tp", tp)
         full_f = lax.all_gather(after(pack_f, *ring_b), ("seq", "fsdp"), axis=0, tiled=True)
         near = [near, swap(near, "fsdp", 1)]
@@ -1138,16 +1144,12 @@
         gain_rows = high(smalls[0, :, 0:3].transpose(1, 0, 2).reshape(3, width))
         table = smalls[:, :, 3, 0 : tables * heads].reshape(tp, seq * cores, tables, heads)
         table = table.transpose(1, 2, 0, 3).reshape(NB, tp * heads)
-        onehot = (
-            buckets.T[:, :, None] == jnp.arange(NB, dtype=jnp.int32)[None, None, :]
-        ).astype(jnp.bfloat16)
         bias = jnp.einsum("jin,nh->hji", onehot, table, preferred_element_type=jnp.float32)
 
         pairs = low(dot(own(memory), cross_pairs))
-        start = high(own(decoder_in))
         scale = DH ** (-0.5)
 
-        normed_self = low(rms_norm(start, gain_rows[0]))
+        normed_self = low(unit_self * gain_rows[0])
         query_self = low(dot(normed_self, weight_self_q) * scale)
         pair_self = low(dot(normed_self, weight_self_kv))
         mixed_self, log_self = attention_forward(query_self, pair_self, bias)
@@ -1191,14 +1193,11 @@
             (all_normed, grad_joined, rounded, hidden, mixed_self, mixed_cross), partial_normed
         )
         hidden_grads = hidden_terms(all_normed, grad_joined, rounded, hidden)
-        partial_out = hidden_out(index, hidden, weight_down, after_cross, tp)
         o_blocks = [
             jnp.concatenate(blocks, axis=1)
             for blocks in zip(head_blocks(o_self), head_blocks(o_cross))
         ]
-        grad_parts, hidden_grads, partial_out, o_blocks = together(
-            grad_parts, hidden_grads, partial_out, o_blocks
-        )
+        grad_parts, hidden_grads, o_blocks = together(grad_parts, hidden_grads, o_blocks)
         hidden_grads = high(
             lax.psum_scatter(hidden_grads, ("seq", "fsdp"), scatter_dimension=0, tiled=True)
         )
@@ -1234,7 +1233,11 @@
             jnp.concatenate([grad_tokens, q_block, kv_block], axis=1)
             for q_block, kv_block in zip(head_blocks(grad_query_self), head_blocks(grad_pair_self))
         ]
-        self_parts, last_operands, memory_pairs, decoder_in, gains, grad_scores = together(
+        partial_out = hidden_out(
+            index, after(hidden, last_operands), weight_down, after_cross, tp
+        )
+        partial_out, self_parts, last_operands, memory_pairs, decoder_in, gains, grad_scores = together(
+            partial_out,
             self_parts,
             last_operands,
             grad_pairs,
@@ -1247,10 +1250,18 @@
         kv_sent, kv_rows, *memory_parts = memory_terms(
             index, seq, memory, memory_pairs, cross_pairs, tp
         )
-        last_parts, kv_sent, kv_rows, memory_parts, gains, grad_scores, partial_out = together(
-            last_parts, kv_sent, kv_rows, memory_parts, gains, grad_scores, partial_out
-        )
         decoder_out = lax.psum(partial_out, "tp")
+        last_parts, kv_sent, kv_rows, memory_parts, gains, grad_scores, all_cross = (
+            together(
+                last_parts,
+                kv_sent,
+                kv_rows,
+                memory_parts,
+                gains,
+                grad_scores,
+                all_cross,
+            )
+        )
         first_parts = exchange(memory_parts[:tp], "tp")
         kv_rows = kv_rows + high(swap(kv_sent, "fsdp", 1))
 
@@ -1287,11 +1298,33 @@
             ],
             axis=0,
         )
-        gains, grad_scores, last_parts, kv_far, second_parts, hidden_grads = after(
-            (gains, grad_scores, last_parts, kv_far, second_parts, hidden_grads), both_grads
+        gains, grad_scores, last_parts, hidden_grads = after(
+            (gains, grad_scores, last_parts, hidden_grads), both_sent
         )
         gate_up_grad = hidden_grads[:, : 2 * hidden_width].reshape(gate_up.shape)
         down_grad = hidden_grads[:, 2 * hidden_width :].T
+        decoder_grad = in_order([part[:, :width] for part in last_parts], jnp.float32)
+        cut = first_parts[0].shape[0]
+        memory_grad = jnp.zeros((count, memory.shape[1], first_parts[0].shape[1]), jnp.bfloat16)
+        for k in range(tp):
+            memory_grad = lax.dynamic_update_slice(
+                memory_grad, first_parts[k][None], (t ^ k, 0, 0)
+            )
+        table_grad = jnp.einsum(
+            "jin,hji->nh", onehot, grad_scores, preferred_element_type=jnp.float32
+        )
+        gain_parts = jnp.stack([gain.reshape(-1, GROUP) for gain in gains], axis=1)
+        table_parts = jnp.pad(
+            table_grad.reshape(seq * cores, 1, -1),
+            ((0, 0), (0, 0), (0, GROUP - tables * tp * heads)),
+        )
+        little = low(jnp.concatenate([gain_parts, table_parts], axis=1))
+        little = jnp.broadcast_to(
+            little.reshape(seq, 1, cores, 4, GROUP), (seq, tp, cores, 4, GROUP)
+        )
+        both_grads, kv_far, little, gate_up_grad, down_grad, decoder_grad, memory_grad = together(
+            both_grads, kv_far, little, gate_up_grad, down_grad, decoder_grad, memory_grad
+        )
         both_grads = lax.all_to_all(both_grads, "seq", 0, 0, tiled=True)
         kv_rows = kv_rows[: seq // 2] + high(kv_far)
         step = seq // 4
@@ -1299,29 +1332,12 @@
             kv_rows = kv_rows[:step] + high(swap(low(kv_rows[step:]), "seq", step))
             step //= 2
         kv_rows = kv_rows[0]
-        memory_grad = jnp.zeros((count, memory.shape[1], first_parts[0].shape[1]), jnp.bfloat16)
-        cut = first_parts[0].shape[0]
-        for at, parts in ((0, first_parts), (cut, second_parts)):
-            for k in range(tp):
-                memory_grad = lax.dynamic_update_slice(
-                    memory_grad, parts[k][None], (t ^ k, at, 0)
-                )
-        decoder_grad = in_order([part[:, :width] for part in last_parts], jnp.float32)
-
-        table_grad = jnp.einsum(
-            "jin,hji->nh", onehot, grad_scores, preferred_element_type=jnp.float32
-        )
-        gain_parts = jnp.stack([gain.reshape(-1, GROUP) for gain in gains], axis=1)
-        table_parts = jnp.pad(
-            table_grad.reshape(seq * cores, 1, -1),
-            ((0, 0), (0, 0), (0, GROUP - tables * tp * heads)),
-        )
-        little = low(jnp.concatenate([gain_parts, table_parts], axis=1))
-        little = jnp.broadcast_to(
-            little.reshape(seq, 1, cores, 4, GROUP), (seq, tp, cores, 4, GROUP)
-        )
-        both_grads, little, gate_up_grad, down_grad, decoder_grad, kv_rows, memory_grad = together(
-            both_grads, little, gate_up_grad, down_grad, decoder_grad, kv_rows, memory_grad
+        for k in range(tp):
+            memory_grad = lax.dynamic_update_slice(
+                memory_grad, second_parts[k][None], (t ^ k, cut, 0)
+            )
+        both_grads, little, kv_rows, memory_grad = together(
+            both_grads, little, kv_rows, memory_grad
         )
         cross_kv_grad = total(
             exchange([kv_rows[:, : 2 * GROUP]] + head_blocks(low(kv_rows))[1:], "tp")

time: 364 us -> 359 us (0.986)
  local copies, waits for them, and re-layouts: 57.9 us -> 64 us
  waiting for transfers between devices: 80 us -> 74.2 us
  starting transfers between devices: 68 us -> 64.2 us
    ppermute x43, waiting for transfers between devices: 71.6 us -> 62.8 us  [swap(): lax.ppermute(value, axis, [(place, place ^ flip) for place in range(size)])]
    all_to_all x1, waiting for transfers between devices: 0.01 us -> 4.47 us  [run(): both_grads = lax.all_to_all(both_grads, 'seq', 0, 0, tiled=True)]
    unnamed x179 -> x195, local copies, waits for them, and re-layouts: 30.1 us -> 33.6 us
  transfers between devices with their start and end apart: 51 -> 51, of which waited for: 16 -> 23; matrix products, arithmetic and copies ran while one was open for 24% -> 26% of each run, Pallas kernels for 21% -> 21%
where the time goes in v4:
time: 359 us; the launch traced here: 354 us
  Pallas kernels  76.2 us (21%)
  waiting for transfers between devices  74.2 us (21%)
  starting transfers between devices  64.2 us (18%)
  local copies, waits for them, and re-layouts  64 us (18%)
  other arithmetic  34.3 us (10%)
  matrix products  25.6 us (7%)
  between operations  15.6 us (4%)
    ppermute x43, waiting for transfers between devices, swap(): lax.ppermute(value, axis, [(place, place ^ flip) for place in range(size)])  62.8 us
    ppermute x43, starting transfers between devices, swap(): lax.ppermute(value, axis, [(place, place ^ flip) for place in range(size)])  46.6 us
    pallas_call x5, Pallas kernels, with_index(): pl.pallas_call(kernel, grid_spec=pltpu.PrefetchScalarGridSpec(num_scalar_...  38.8 us
    pallas_call x7, Pallas kernels, kernel_call(): pl.pallas_call(kernel, grid=(blocks,), in_specs=specs, out_specs=[spec fo...  37.4 us
    unnamed x195, local copies, waits for them, and re-layouts  33.6 us
    dot_general x7, matrix products, dot(): return jnp.dot(left, right, preferred_element_type=jnp.float32)  15.4 us
    all_to_all x2, starting transfers between devices, exchange_all(): return lax.all_to_all(value, 'tp', 0, 0, tiled=True)  9.8 us
    dot_general x7, matrix products, dot_t(): lax.dot_general(left, right, (((1,), (1,)), ((), ())), preferred_element_...  8.29 us
  transfers between devices with their start and end apart: 51, of which 23 were waited for; matrix products, arithmetic and copies ran while one was open for 26% of the time, Pallas kernels for 21%

profile of v4, /device:TPU:0, one launch (start us, length us, event | category | flops | bytes accessed | tf_op | source)
XLA Modules:
  0.0 354.0 jit_solution(5451474064372293537)
XLA Ops:
  9.5 2.9 pack_shards.1
  12.4 5.2 %all-to-all-start = ((bf16[4,1552,128]{2,1,0:T(8,128)(2,1)}), bf16[4,1552,128]{2,1,0:T(8,128)(2,1)S(1)}, u32[]{:S(2)}, u32[]{:S(2)}) async-start(bf16[4,1552,128]{2,1,0:T(8,128)(2,1)} %get-tuple-element.161), calls=%async_computation | async-start | bytes 3178496 | tf_op jit(solution)/shard_map/all_to_all | solution.py:1049
  17.6 3.6 %collective-permute-start.3 = (bf16[784,128]{1,0:T(8,128)(2,1)}, bf16[784,128]{1,0:T(8,128)(2,1)S(1)}, u32[]{:S(2)}, u32[]{:S(2)}) collective-permute-start(bf16[784,128]{1,0:T(8,128)(2,1)} %get-tuple-element.162), channel_id=1, source_target_pairs={{0,24},{8,16},{16,8},{24,0},{1,25},{9,17},{17,9},{25,1},{2,26},{10... | collective-permute-start | bytes 602120 | tf_op jit(solution)/shard_map/ppermute | solution.py:1040
  23.3 4.2 %collective-permute-done.3 = bf16[784,128]{1,0:T(8,128)(2,1)S(1)} collective-permute-done((bf16[784,128]{1,0:T(8,128)(2,1)}, bf16[784,128]{1,0:T(8,128)(2,1)S(1)}, u32[]{:S(2)}, u32[]{:S(2)}) %collective-permute-start.3) | collective-permute-done | bytes 200736 | tf_op jit(solution)/shard_map/ppermute | solution.py:1040
  27.6 10.8 %collective-permute-done.2 = bf16[784,128]{1,0:T(8,128)(2,1)S(1)} collective-permute-done((bf16[784,128]{1,0:T(8,128)(2,1)}, bf16[784,128]{1,0:T(8,128)(2,1)S(1)}, u32[]{:S(2)}, u32[]{:S(2)}) %collective-permute-start.2) | collective-permute-done | bytes 200736 | tf_op jit(solution)/shard_map/ppermute | solution.py:1040
  42.0 4.6 %all-to-all-start.1 = ((bf16[4,3,784,128]{3,2,1,0:T(8,128)(2,1)}), bf16[4,3,784,128]{3,2,1,0:T(8,128)(2,1)}, u32[]{:S(2)}, u32[]{:S(2)}) async-start(bf16[4,3,784,128]{3,2,1,0:T(8,128)(2,1)} %broadcast_in_dim.108), calls=%async_computation.1 | async-start | bytes 4816896 | tf_op jit(solution)/shard_map/all_to_all | solution.py:1049
  49.1 2.5 collective-permute-start.7
  54.5 4.6 %collective-permute-done.7 = bf16[768,128]{1,0:T(8,128)(2,1)S(1)} collective-permute-done((bf16[768,128]{1,0:T(8,128)(2,1)}, bf16[768,128]{1,0:T(8,128)(2,1)S(1)}, u32[]{:S(2)}, u32[]{:S(2)}) %collective-permute-start.7) | collective-permute-done | bytes 196640 | tf_op jit(solution)/shard_map/ppermute | solution.py:1040
  59.1 7.9 %collective-permute-done.6 = bf16[768,128]{1,0:T(8,128)(2,1)} collective-permute-done((bf16[768,128]{1,0:T(8,128)(2,1)}, bf16[768,128]{1,0:T(8,128)(2,1)}, u32[]{:S(2)}, u32[]{:S(2)}) %collective-permute-start.6) | collective-permute-done | bytes 196640 | tf_op jit(solution)/shard_map/ppermute | solution.py:1040
  67.6 6.8 %all-to-all-done.1.refs_2_ = bf16[4,3,784,128]{3,2,1,0:T(8,128)(2,1)} async-done(((bf16[4,3,784,128]{3,2,1,0:T(8,128)(2,1)}), bf16[4,3,784,128]{3,2,1,0:T(8,128)(2,1)}, u32[]{:S(2)}, u32[]{:S(2)}) %all-to-all-start.1) | async-done | bytes 2408480 | tf_op jit(solution)/shard_map/all_to_all | solution.py:1049
  75.0 2.2 copy.151
  82.2 5.0 %unpack_heads.2 = (bf16[1024,1024]{1,0:T(8,128)(2,1)S(1)}, bf16[1024,1024]{1,0:T(8,128)(2,1)S(1)}, bf16[1024,1024]{1,0:T(8,128)(2,1)S(1)}, bf16[4,8,16,128]{3,2,1,0:T(8,128)(2,1)S(1)}) custom-call(s32[3]{0:T(128)S(1)} %pad_add_fusion.index_ref, bf16[4,1552,128]{2,1,0:T(8,128)(2,1)S(1)} %all-to-all-done.refs_0_, ...), custom_call_target="tpu_custom_call" | custom-call | bytes 12845056 | tf_op jit(solution)/shard_map/unpack_heads/pallas_call | solution.py:649
  94.7 3.7 %self_forward.1 = (bf16[128,1024]{1,0:T(8,128)(2,1)S(1)}, f32[4,2,256]{2,1,0:T(2,128)S(1)}) custom-call(bf16[128,1024]{1,0:T(8,128)(2,1)S(1)} %fusion.14.q_ref, bf16[128,1024]{1,0:T(8,128)(2,1)S(1)} %convolution_convert_fusion.3.kv_ref, f32[16,128,128]{2,1,0:T(8,128)S(1)} %copy.152.bias_ref), custom_call_target="tpu_custom_call" | custom-call | flops 67108864 | bytes 786432 | tf_op jit(solution)/shard_map/self_forward/pallas_call | solution.py:566
  98.5 8.4 %fusion.3.kv_ref = bf16[2048,1024]{1,0:T(8,128)(2,1)} fusion(bf16[1024,1024]{1,0:T(8,128)(2,1)S(1)} %copy-done.33, bf16[4,2048,1024]{2,1,0:T(8,128)(2,1)} %memory_ref.1, s32[]{:T(128)S(6)} %select_n.56), kind=kOutput, calls=%fused_computation.3 | convolution fusion | flops 4297064448 | bytes 10485764 | tf_op jit(solution)/shard_map/dot_general | solution.py:412
  112.7 5.3 %unpack_heads.3 = (bf16[1024,1024]{1,0:T(8,128)(2,1)S(1)}, bf16[1024,1024]{1,0:T(8,128)(2,1)S(1)}, bf16[1024,1024]{1,0:T(8,128)(2,1)S(1)}) custom-call(s32[3]{0:T(128)S(1)} %pad_add_fusion.index_ref, bf16[4,1552,128]{2,1,0:T(8,128)(2,1)S(1)} %all-to-all-done.refs_0_, bf16[4,1552,128]{2,1,0:T(8,128)(2,1)} %collective-permute-done.refs_1_, ...), custom_call_target="tpu_custom_call" | custom-call | bytes 12582912 | tf_op jit(solution)/shard_map/unpack_heads/pallas_call | solution.py:649
  122.5 2.2 fusion.15.q_ref
  124.7 2.2 copy-done.45
  126.9 8.4 %cross_forward.1 = (bf16[128,1024]{1,0:T(8,128)(2,1)S(1)}, f32[4,2,256]{2,1,0:T(2,128)S(1)}) custom-call(bf16[128,1024]{1,0:T(8,128)(2,1)S(1)} %fusion.15.q_ref, bf16[2048,1024]{1,0:T(8,128)(2,1)S(1)} %copy-done.45), custom_call_target="tpu_custom_call" | custom-call | flops 1073741824 | bytes 4718592 | tf_op jit(solution)/shard_map/cross_forward/pallas_call | solution.py:566
  140.1 2.2 copy-done.14
  143.3 2.0 collective-permute-done.15
  145.4 5.3 %collective-permute-done.16 = bf16[128,1024]{1,0:T(8,128)(2,1)} collective-permute-done((bf16[128,1024]{1,0:T(8,128)(2,1)S(1)}, bf16[128,1024]{1,0:T(8,128)(2,1)}, u32[]{:S(2)}, u32[]{:S(2)}) %collective-permute-start.16) | collective-permute-done | bytes 262176 | tf_op jit(solution)/shard_map/ppermute | solution.py:1040
  157.0 2.0 fusion.13
  168.5 4.8 %hidden_terms.1 = bf16[1024,2112]{1,0:T(8,128)(2,1)S(1)} custom-call(bf16[512,1024]{1,0:T(8,128)(2,1)S(1)} %constant_dynamic-update-slice_fusion.12.normed_ref, bf16[512,1408]{1,0:T(8,128)(2,1)S(1)} %pad_maximum_fusion.joined_ref, bf16[512,1024]{1,0:T(8,128)(2,1)S(1)} %pad_maximum_fusion.2.rounded_ref, bf16[512,704]{1,0:T(8,128)(2,1)S(1)} %get-tuple-element.218.hidden_ref), custom_call_target="tpu_custom_call" | custom-call | flops 2214592512 | bytes 10747904 | tf_op jit(solution)/shard_map/hidden_terms/pallas_call | solution.py:566
  173.3 2.1 copy-done
  175.4 2.7 collective-permute-done.20
  183.5 2.3 collective-permute-start.23
  186.6 13.0 %cross_backward.1 = (bf16[128,1024]{1,0:T(8,128)(2,1)S(1)}, bf16[2048,1024]{1,0:T(8,128)(2,1)S(1)}) custom-call(bf16[128,1024]{1,0:T(8,128)(2,1)S(1)} %copy-done.30, bf16[128,1024]{1,0:T(8,128)(2,1)S(1)} %convolution_convert_fusion.2.do_ref, bf16[128,1024]{1,0:T(8,128)(2,1)S(1)} %copy-done.26, bf16[2048,1024]{1,0:T(8,128)(2,1)S(1)} %copy-done.46, ...), custom_call_target="tpu_custom_call" | custom-call | flops 2684354560 | bytes 9437184 | tf_op jit(solution)/shard_map/cross_backward/pallas_call | solution.py:566
  207.6 3.5 self_backward.1
  214.8 3.3 hidden_out.1
  224.4 2.2 copy-done.48
  226.7 14.0 %memory_terms.1 = (bf16[4,128,1024]{2,1,0:T(8,128)(2,1)S(1)}, f32[4,128,1024]{2,1,0:T(8,128)S(1)}, bf16[512,256]{1,0:T(8,128)(2,1)S(1)}, bf16[512,256]{1,0:T(8,1...) custom-call(s32[3]{0:T(128)S(1)} %pad_add_fusion.index_ref, ...), custom_call_target="tpu_custom_call" | custom-call | flops 8589934592 | bytes 12582912 | tf_op jit(solution)/shard_map/memory_terms/pallas_call | solution.py:649
  245.5 2.5 fusion.28
  252.6 11.1 %head_weights.1 = (bf16[4,128,1280]{2,1,0:T(8,128)(2,1)}, f32[4,128,1280]{2,1,0:T(8,128)}) custom-call(s32[3]{0:T(128)} %copy-done.31, bf16[128,1024]{1,0:T(8,128)(2,1)} %get-tuple-element.411.refs_0_, bf16[128,1024]{1,0:T(8,128)(2,1)} %get-tuple-element.410.refs_1_, bf16[128,1024]{1,0:T(8,128)(2,1)} %get-tuple-element.409.refs_2_, ...), custom_call_target="tpu_custom_call" | custom-call | flops 1342177280 | bytes 6291456 | tf_op jit(solution)/shard_map/head_weights/pallas_call | solution.py:649
  265.8 2.5 collective-permute-start.35
  275.2 2.6 add_convert_fusion
  279.1 2.2 convert_element_type.204
  287.6 2.2 copy.170
  294.1 4.3 %all-to-all-start.2 = ((bf16[4,128,1280]{2,1,0:T(8,128)(2,1)}), bf16[4,128,1280]{2,1,0:T(8,128)(2,1)}, u32[]{:S(2)}, u32[]{:S(2)}) async-start(bf16[4,128,1280]{2,1,0:T(8,128)(2,1)} %pad_maximum_fusion.1), calls=%async_computation.3 | async-start | bytes 2621440 | tf_op jit(solution)/shard_map/all_to_all | solution.py:1328
  300.9 2.0 collective-permute-start.36
  304.8 2.2 bitcast_dynamic-update-slice_fusion.2
  306.9 2.1 bitcast_dynamic-update-slice_fusion.1
  309.0 5.4 %collective-permute-done.39 = bf16[1536,256]{1,0:T(8,128)(2,1)} collective-permute-done((bf16[1536,256]{1,0:T(8,128)(2,1)S(1)}, bf16[1536,256]{1,0:T(8,128)(2,1)}, u32[]{:S(2)}, u32[]{:S(2)}) %collective-permute-start.39) | collective-permute-done | bytes 786464 | tf_op jit(solution)/shard_map/ppermute | solution.py:1040
  314.4 2.1 bitcast_dynamic-update-slice_fusion
  316.4 9.0 %collective-permute-done.36 = bf16[1,128,1024]{2,1,0:T(8,128)(2,1)S(1)} collective-permute-done((bf16[1,128,1024]{2,1,0:T(8,128)(2,1)S(1)}, bf16[1,128,1024]{2,1,0:T(8,128)(2,1)S(1)}, u32[]{:S(2)}, u32[]{:S(2)}) %collective-permute-start.36) | collective-permute-done | bytes 262176 | tf_op jit(solution)/shard_map/ppermute | solution.py:1040
  325.5 4.5 %all-to-all-done.2 = bf16[4,128,1280]{2,1,0:T(8,128)(2,1)} async-done(((bf16[4,128,1280]{2,1,0:T(8,128)(2,1)}), bf16[4,128,1280]{2,1,0:T(8,128)(2,1)}, u32[]{:S(2)}, u32[]{:S(2)}) %all-to-all-start.2) | async-done | bytes 1310752 | tf_op jit(solution)/shard_map/all_to_all | solution.py:1328
  330.0 2.6 all-to-all-start.3
  336.7 2.7 collective-permute-start.42
  345.0 2.3 copy.209
  (397 shorter events, 126.2 us)
Async XLA Ops:
  12.4 27.8 %all-to-all-start = ((bf16[4,1552,128]{2,1,0:T(8,128)(2,1)}), bf16[4,1552,128]{2,1,0:T(8,128)(2,1)S(1)}, u32[]{:S(2)}, u32[]{:S(2)}) async-start(bf16[4,1552,128]{2,1,0:T(8,128)(2,1)} %get-tuple-element.161), calls=%async_computation | async-start | bytes 3178496 | tf_op jit(solution)/shard_map/all_to_all | solution.py:1049
  17.6 10.0 %collective-permute-start.3 = (bf16[784,128]{1,0:T(8,128)(2,1)}, bf16[784,128]{1,0:T(8,128)(2,1)S(1)}, u32[]{:S(2)}, u32[]{:S(2)}) collective-permute-start(bf16[784,128]{1,0:T(8,128)(2,1)} %get-tuple-element.162), channel_id=1, source_target_pairs={{0,24},{8,16},{16,8},{24,0},{1,25},{9,17},{17,9},{25,1},{2,26},{10... | collective-permute-start | bytes 602120 | tf_op jit(solution)/shard_map/ppermute | solution.py:1040
  21.2 17.2 %collective-permute-start.2 = (bf16[784,128]{1,0:T(8,128)(2,1)}, bf16[784,128]{1,0:T(8,128)(2,1)S(1)}, u32[]{:S(2)}, u32[]{:S(2)}) collective-permute-start(bf16[784,128]{1,0:T(8,128)(2,1)} %get-tuple-element.162), channel_id=1, source_target_pairs={{0,16},{8,24},{16,0},{24,8},{1,17},{9,25},{17,1},{25,9},{2,18},{10... | collective-permute-start | bytes 602120 | tf_op jit(solution)/shard_map/ppermute | solution.py:1040
  21.2 17.2 %collective-permute-start.1 = (bf16[784,128]{1,0:T(8,128)(2,1)}, bf16[784,128]{1,0:T(8,128)(2,1)S(1)}, u32[]{:S(2)}, u32[]{:S(2)}) collective-permute-start(bf16[784,128]{1,0:T(8,128)(2,1)} %get-tuple-element.162), channel_id=1, source_target_pairs={{0,8},{8,0},{16,24},{24,16},{1,9},{9,1},{17,25},{25,17},{2,10},{10... | collective-permute-start | bytes 602120 | tf_op jit(solution)/shard_map/ppermute | solution.py:1040
  42.0 32.5 %all-to-all-start.1 = ((bf16[4,3,784,128]{3,2,1,0:T(8,128)(2,1)}), bf16[4,3,784,128]{3,2,1,0:T(8,128)(2,1)}, u32[]{:S(2)}, u32[]{:S(2)}) async-start(bf16[4,3,784,128]{3,2,1,0:T(8,128)(2,1)} %broadcast_in_dim.108), calls=%async_computation.1 | async-start | bytes 4816896 | tf_op jit(solution)/shard_map/all_to_all | solution.py:1049
  46.6 93.4 %all-gather.3.cloned.1.call-start = ((), (), s32[]{:S(2)}) async-start(), calls=%async_computation.5 | async-start | bytes 4866048 | tf_op jit(solution)/shard_map/all_gather | solution.py:1134
  49.1 10.0 %collective-permute-start.7 = (bf16[768,128]{1,0:T(8,128)(2,1)}, bf16[768,128]{1,0:T(8,128)(2,1)S(1)}, u32[]{:S(2)}, u32[]{:S(2)}) collective-permute-start(bf16[768,128]{1,0:T(8,128)(2,1)} %get-tuple-element.170), channel_id=1, source_target_pairs={{0,24},{8,16},{16,8},{24,0},{1,25},{9,17},{17,9},{25,1},{2,26},{10... | collective-permute-start | bytes 589832 | tf_op jit(solution)/shard_map/ppermute | solution.py:1040
  51.7 15.4 %collective-permute-start.6 = (bf16[768,128]{1,0:T(8,128)(2,1)}, bf16[768,128]{1,0:T(8,128)(2,1)}, u32[]{:S(2)}, u32[]{:S(2)}) collective-permute-start(bf16[768,128]{1,0:T(8,128)(2,1)} %get-tuple-element.170), channel_id=1, source_target_pairs={{0,16},{8,24},{16,0},{24,8},{1,17},{9,25},{17,1},{25,9},{2,18},{10... | collective-permute-start | bytes 589832 | tf_op jit(solution)/shard_map/ppermute | solution.py:1040
  51.7 15.4 %collective-permute-start.5 = (bf16[768,128]{1,0:T(8,128)(2,1)}, bf16[768,128]{1,0:T(8,128)(2,1)}, u32[]{:S(2)}, u32[]{:S(2)}) collective-permute-start(bf16[768,128]{1,0:T(8,128)(2,1)} %get-tuple-element.170), channel_id=1, source_target_pairs={{0,8},{8,0},{16,24},{24,16},{1,9},{9,1},{17,25},{25,17},{2,10},{10... | collective-permute-start | bytes 589832 | tf_op jit(solution)/shard_map/ppermute | solution.py:1040
  67.0 178.3 %all-gather.5.cloned.1.call-start = ((), (), s32[]{:S(2)}) async-start(), calls=%async_computation.7 | async-start | bytes 1310720 | tf_op jit(solution)/shard_map/all_gather | solution.py:1169
  74.5 7.8 %collective-permute-start.4 = (bf16[4,3,784,128]{3,2,1,0:T(8,128)(2,1)}, bf16[4,3,784,128]{3,2,1,0:T(8,128)(2,1)}, u32[]{:S(2)}, u32[]{:S(2)}) collective-permute-start(bf16[4,3,784,128]{3,2,1,0:T(8,128)(2,1)} %all-to-all-done.1.refs_2_), channel_id=1, source_target_pairs={{0,1},{1,0},{2,3},{3,2},{4,5},{5,4},{6,7},{7,6},{8,9},{9,8},{10,11... | collective-permute-start | bytes 7225352 | tf_op jit(solution)/shard_map/ppermute | solution.py:1040
  74.5 7.5 %collective-permute-start = (bf16[4,1552,128]{2,1,0:T(8,128)(2,1)S(1)}, bf16[4,1552,128]{2,1,0:T(8,128)(2,1)}, u32[]{:S(2)}, u32[]{:S(2)}) collective-permute-start(bf16[4,1552,128]{2,1,0:T(8,128)(2,1)S(1)} %all-to-all-done.refs_0_), channel_id=1, source_target_pairs={{0,1},{1,0},{2,3},{3,2},{4,5},{5,4},{6,7},{7,6},{8,9},{9,8},{10,11... | collective-permute-start | bytes 4767752 | tf_op jit(solution)/shard_map/ppermute | solution.py:1040
  78.4 28.5 %collective-permute-start.8 = (bf16[3,768,128]{2,1,0:T(8,128)(2,1)S(1)}, bf16[3,768,128]{2,1,0:T(8,128)(2,1)}, u32[]{:S(2)}, u32[]{:S(2)}) collective-permute-start(bf16[3,768,128]{2,1,0:T(8,128)(2,1)S(1)} %pad_maximum_fusion.4.refs_2_), channel_id=1, source_target_pairs={{0,2},{2,0},{4,6},{6,4},{1,3},{3,1},{5,7},{7,5},{8,10},{10,8},{12,... | collective-permute-start | bytes 1769480 | tf_op jit(solution)/shard_map/ppermute | solution.py:1040
  79.9 27.7 %collective-permute-start.9 = (bf16[3,768,128]{2,1,0:T(8,128)(2,1)S(1)}, bf16[3,768,128]{2,1,0:T(8,128)(2,1)}, u32[]{:S(2)}, u32[]{:S(2)}) collective-permute-start(bf16[3,768,128]{2,1,0:T(8,128)(2,1)S(1)} %pad_maximum_fusion.4.refs_2_), channel_id=1, source_target_pairs={{0,4},{2,6},{4,0},{6,2},{1,5},{3,7},{5,1},{7,3},{8,12},{10,14},{12... | collective-permute-start | bytes 1769480 | tf_op jit(solution)/shard_map/ppermute | solution.py:1040
  80.4 27.1 %collective-permute-start.10 = (bf16[3,768,128]{2,1,0:T(8,128)(2,1)S(1)}, bf16[3,768,128]{2,1,0:T(8,128)(2,1)}, u32[]{:S(2)}, u32[]{:S(2)}) collective-permute-start(bf16[3,768,128]{2,1,0:T(8,128)(2,1)S(1)} %pad_maximum_fusion.4.refs_2_), channel_id=1, source_target_pairs={{0,6},{2,4},{4,2},{6,0},{1,7},{3,5},{5,3},{7,1},{8,14},{10,12},{12... | collective-permute-start | bytes 1769480 | tf_op jit(solution)/shard_map/ppermute | solution.py:1040
  108.1 4.6 %collective-permute-start.14 = (bf16[3,768,128]{2,1,0:T(8,128)(2,1)}, bf16[3,768,128]{2,1,0:T(8,128)(2,1)}, u32[]{:S(2)}, u32[]{:S(2)}) collective-permute-start(bf16[3,768,128]{2,1,0:T(8,128)(2,1)} %collective-permute-done.10.refs_5_), channel_id=1, source_target_pairs={{0,1},{1,0},{2,3},{3,2},{4,5},{5,4},{6,7},{7,6},{8,9},{9,8},{10,11... | collective-permute-start | bytes 1769480 | tf_op jit(solution)/shard_map/ppermute | solution.py:1040
  136.0 9.3 %collective-permute-start.15 = (bf16[128,1024]{1,0:T(8,128)(2,1)S(1)}, bf16[128,1024]{1,0:T(8,128)(2,1)}, u32[]{:S(2)}, u32[]{:S(2)}) collective-permute-start(bf16[128,1024]{1,0:T(8,128)(2,1)S(1)} %multiply_convert_fusion.2), channel_id=1, source_target_pairs={{0,2},{2,0},{4,6},{6,4},{1,3},{3,1},{5,7},{7,5},{8,10},{10,8},{12,... | collective-permute-start | bytes 786440 | tf_op jit(solution)/shard_map/ppermute | solution.py:1040
  137.2 13.5 %collective-permute-start.16 = (bf16[128,1024]{1,0:T(8,128)(2,1)S(1)}, bf16[128,1024]{1,0:T(8,128)(2,1)}, u32[]{:S(2)}, u32[]{:S(2)}) collective-permute-start(bf16[128,1024]{1,0:T(8,128)(2,1)S(1)} %multiply_convert_fusion.2), channel_id=1, source_target_pairs={{0,4},{2,6},{4,0},{6,2},{1,5},{3,7},{5,1},{7,3},{8,12},{10,14},{12... | collective-permute-start | bytes 786440 | tf_op jit(solution)/shard_map/ppermute | solution.py:1040
  138.2 14.1 %collective-permute-start.17 = (bf16[128,1024]{1,0:T(8,128)(2,1)S(1)}, bf16[128,1024]{1,0:T(8,128)(2,1)}, u32[]{:S(2)}, u32[]{:S(2)}) collective-permute-start(bf16[128,1024]{1,0:T(8,128)(2,1)S(1)} %multiply_convert_fusion.2), channel_id=1, source_target_pairs={{0,6},{2,4},{4,2},{6,0},{1,7},{3,5},{5,3},{7,1},{8,14},{10,12},{12... | collective-permute-start | bytes 786440 | tf_op jit(solution)/shard_map/ppermute | solution.py:1040
  139.8 139.3 %reduce-scatter.2.cloned.1.call-start = ((), (), s32[]{:S(2)}) async-start(), calls=%async_computation.8 | async-start | bytes 5013504 | tf_op jit(solution)/shard_map/reduce_scatter | solution.py:1202
  162.3 13.1 %collective-permute-start.18 = (bf16[128,1024]{1,0:T(8,128)(2,1)}, bf16[128,1024]{1,0:T(8,128)(2,1)}, u32[]{:S(2)}, u32[]{:S(2)}) collective-permute-start(bf16[128,1024]{1,0:T(8,128)(2,1)} %get-tuple-element.414), channel_id=1, source_target_pairs={{0,2},{2,0},{4,6},{6,4},{1,3},{3,1},{5,7},{7,5},{8,10},{10,8},{12,... | collective-permute-start | bytes 786440 | tf_op jit(solution)/shard_map/ppermute | solution.py:1040
  163.7 11.8 %collective-permute-start.19 = (bf16[128,1024]{1,0:T(8,128)(2,1)}, bf16[128,1024]{1,0:T(8,128)(2,1)}, u32[]{:S(2)}, u32[]{:S(2)}) collective-permute-start(bf16[128,1024]{1,0:T(8,128)(2,1)} %get-tuple-element.413), channel_id=1, source_target_pairs={{0,4},{2,6},{4,0},{6,2},{1,5},{3,7},{5,1},{7,3},{8,12},{10,14},{12... | collective-permute-start | bytes 786440 | tf_op jit(solution)/shard_map/ppermute | solution.py:1040
  165.5 12.7 %collective-permute-start.20 = (bf16[128,1024]{1,0:T(8,128)(2,1)}, bf16[128,1024]{1,0:T(8,128)(2,1)}, u32[]{:S(2)}, u32[]{:S(2)}) collective-permute-start(bf16[128,1024]{1,0:T(8,128)(2,1)} %get-tuple-element.412), channel_id=1, source_target_pairs={{0,6},{2,4},{4,2},{6,0},{1,7},{3,5},{5,3},{7,1},{8,14},{10,12},{12... | collective-permute-start | bytes 786440 | tf_op jit(solution)/shard_map/ppermute | solution.py:1040
  178.2 166.8 %all-reduce.4.cloned.1.call-start = ((), (), s32[]{:S(2)}) async-start(), calls=%async_computation.6 | async-start | bytes 2097152 | tf_op jit(solution)/shard_map/psum | solution.py:1253
  182.2 17.4 %collective-permute-start.21 = (bf16[128,1536]{1,0:T(8,128)(2,1)S(1)}, bf16[128,1536]{1,0:T(8,128)(2,1)S(1)}, u32[]{:S(2)}, u32[]{:S(2)}) collective-permute-start(bf16[128,1536]{1,0:T(8,128)(2,1)S(1)} %get-tuple-element.460), channel_id=1, source_target_pairs={{0,2},{2,0},{4,6},{6,4},{1,3},{3,1},{5,7},{7,5},{8,10},{10,8},{12,... | collective-permute-start | bytes 1179656 | tf_op jit(solution)/shard_map/ppermute | solution.py:1040
  182.8 16.8 %collective-permute-start.22 = (bf16[128,1536]{1,0:T(8,128)(2,1)S(1)}, bf16[128,1536]{1,0:T(8,128)(2,1)S(1)}, u32[]{:S(2)}, u32[]{:S(2)}) collective-permute-start(bf16[128,1536]{1,0:T(8,128)(2,1)S(1)} %get-tuple-element.461), channel_id=1, source_target_pairs={{0,4},{2,6},{4,0},{6,2},{1,5},{3,7},{5,1},{7,3},{8,12},{10,14},{12... | collective-permute-start | bytes 1179656 | tf_op jit(solution)/shard_map/ppermute | solution.py:1040
  183.5 17.3 %collective-permute-start.23 = (bf16[128,1536]{1,0:T(8,128)(2,1)S(1)}, bf16[128,1536]{1,0:T(8,128)(2,1)S(1)}, u32[]{:S(2)}, u32[]{:S(2)}) collective-permute-start(bf16[128,1536]{1,0:T(8,128)(2,1)S(1)} %get-tuple-element.459), channel_id=1, source_target_pairs={{0,6},{2,4},{4,2},{6,0},{1,7},{3,5},{5,3},{7,1},{8,14},{10,12},{12... | collective-permute-start | bytes 1179656 | tf_op jit(solution)/shard_map/ppermute | solution.py:1040
  203.2 14.9 %collective-permute-start.24 = (bf16[128,1280]{1,0:T(8,128)(2,1)}, bf16[128,1280]{1,0:T(8,128)(2,1)S(1)}, u32[]{:S(2)}, u32[]{:S(2)}) collective-permute-start(bf16[128,1280]{1,0:T(8,128)(2,1)} %get-tuple-element.452), channel_id=1, source_target_pairs={{0,2},{2,0},{4,6},{6,4},{1,3},{3,1},{5,7},{7,5},{8,10},{10,8},{12,... | collective-permute-start | bytes 983048 | tf_op jit(solution)/shard_map/ppermute | solution.py:1040
  205.0 13.1 %collective-permute-start.25 = (bf16[128,1280]{1,0:T(8,128)(2,1)}, bf16[128,1280]{1,0:T(8,128)(2,1)S(1)}, u32[]{:S(2)}, u32[]{:S(2)}) collective-permute-start(bf16[128,1280]{1,0:T(8,128)(2,1)} %get-tuple-element.453), channel_id=1, source_target_pairs={{0,4},{2,6},{4,0},{6,2},{1,5},{3,7},{5,1},{7,3},{8,12},{10,14},{12... | collective-permute-start | bytes 983048 | tf_op jit(solution)/shard_map/ppermute | solution.py:1040
  205.5 13.8 %collective-permute-start.26 = (bf16[128,1280]{1,0:T(8,128)(2,1)}, bf16[128,1280]{1,0:T(8,128)(2,1)S(1)}, u32[]{:S(2)}, u32[]{:S(2)}) collective-permute-start(bf16[128,1280]{1,0:T(8,128)(2,1)} %get-tuple-element.451), channel_id=1, source_target_pairs={{0,6},{2,4},{4,2},{6,0},{1,7},{3,5},{5,3},{7,1},{8,14},{10,12},{12... | collective-permute-start | bytes 983048 | tf_op jit(solution)/shard_map/ppermute | solution.py:1040
  219.3 26.1 %collective-permute-start.27 = (bf16[128,1536]{1,0:T(8,128)(2,1)}, bf16[128,1536]{1,0:T(8,128)(2,1)}, u32[]{:S(2)}, u32[]{:S(2)}) collective-permute-start(bf16[128,1536]{1,0:T(8,128)(2,1)} %get-tuple-element.224), channel_id=1, source_target_pairs={{0,2},{2,0},{4,6},{6,4},{1,3},{3,1},{5,7},{7,5},{8,10},{10,8},{12,... | collective-permute-start | bytes 1179656 | tf_op jit(solution)/shard_map/ppermute | solution.py:1040
  220.1 25.3 %collective-permute-start.28 = (bf16[128,1536]{1,0:T(8,128)(2,1)}, bf16[128,1536]{1,0:T(8,128)(2,1)}, u32[]{:S(2)}, u32[]{:S(2)}) collective-permute-start(bf16[128,1536]{1,0:T(8,128)(2,1)} %get-tuple-element.225), channel_id=1, source_target_pairs={{0,4},{2,6},{4,0},{6,2},{1,5},{3,7},{5,1},{7,3},{8,12},{10,14},{12... | collective-permute-start | bytes 1179656 | tf_op jit(solution)/shard_map/ppermute | solution.py:1040
  221.6 23.8 %collective-permute-start.29 = (bf16[128,1536]{1,0:T(8,128)(2,1)}, bf16[128,1536]{1,0:T(8,128)(2,1)}, u32[]{:S(2)}, u32[]{:S(2)}) collective-permute-start(bf16[128,1536]{1,0:T(8,128)(2,1)} %get-tuple-element.226), channel_id=1, source_target_pairs={{0,6},{2,4},{4,2},{6,0},{1,7},{3,5},{5,3},{7,1},{8,14},{10,12},{12... | collective-permute-start | bytes 1179656 | tf_op jit(solution)/shard_map/ppermute | solution.py:1040
  245.4 18.3 %collective-permute-start.33 = (bf16[4,128,1024]{2,1,0:T(8,128)(2,1)}, bf16[4,128,1024]{2,1,0:T(8,128)(2,1)S(1)}, u32[]{:S(2)}, u32[]{:S(2)}) collective-permute-start(bf16[4,128,1024]{2,1,0:T(8,128)(2,1)} %copy-done.35), channel_id=1, source_target_pairs={{0,1},{1,0},{2,3},{3,2},{4,5},{5,4},{6,7},{7,6},{8,9},{9,8},{10,11... | collective-permute-start | bytes 3145736 | tf_op jit(solution)/shard_map/ppermute | solution.py:1040
  248.0 16.9 %collective-permute-start.30 = (bf16[512,256]{1,0:T(8,128)(2,1)S(1)}, bf16[512,256]{1,0:T(8,128)(2,1)}, u32[]{:S(2)}, u32[]{:S(2)}) collective-permute-start(bf16[512,256]{1,0:T(8,128)(2,1)S(1)} %copy-done.44), channel_id=1, source_target_pairs={{0,2},{2,0},{4,6},{6,4},{1,3},{3,1},{5,7},{7,5},{8,10},{10,8},{12,... | collective-permute-start | bytes 786440 | tf_op jit(solution)/shard_map/ppermute | solution.py:1040
  248.9 16.1 %collective-permute-start.31 = (bf16[512,256]{1,0:T(8,128)(2,1)S(1)}, bf16[512,256]{1,0:T(8,128)(2,1)}, u32[]{:S(2)}, u32[]{:S(2)}) collective-permute-start(bf16[512,256]{1,0:T(8,128)(2,1)S(1)} %copy-done.42), channel_id=1, source_target_pairs={{0,4},{2,6},{4,0},{6,2},{1,5},{3,7},{5,1},{7,3},{8,12},{10,14},{12... | collective-permute-start | bytes 786440 | tf_op jit(solution)/shard_map/ppermute | solution.py:1040
  250.4 14.6 %collective-permute-start.32 = (bf16[512,256]{1,0:T(8,128)(2,1)S(1)}, bf16[512,256]{1,0:T(8,128)(2,1)}, u32[]{:S(2)}, u32[]{:S(2)}) collective-permute-start(bf16[512,256]{1,0:T(8,128)(2,1)S(1)} %get-tuple-element.245), channel_id=1, source_target_pairs={{0,6},{2,4},{4,2},{6,0},{1,7},{3,5},{5,3},{7,1},{8,14},{10,12},{12... | collective-permute-start | bytes 786440 | tf_op jit(solution)/shard_map/ppermute | solution.py:1040
  265.5 9.7 %collective-permute-start.34 = (bf16[4,128,1280]{2,1,0:T(8,128)(2,1)}, bf16[4,128,1280]{2,1,0:T(8,128)(2,1)}, u32[]{:S(2)}, u32[]{:S(2)}) collective-permute-start(bf16[4,128,1280]{2,1,0:T(8,128)(2,1)} %get-tuple-element.269), channel_id=1, source_target_pairs={{0,1},{1,0},{2,3},{3,2},{4,5},{5,4},{6,7},{7,6},{8,9},{9,8},{10,11... | collective-permute-start | bytes 3932168 | tf_op jit(solution)/shard_map/ppermute | solution.py:1040
  265.8 27.7 %collective-permute-start.35 = (bf16[2,128,1024]{2,1,0:T(8,128)(2,1)}, bf16[2,128,1024]{2,1,0:T(8,128)(2,1)}, u32[]{:S(2)}, u32[]{:S(2)}) collective-permute-start(bf16[2,128,1024]{2,1,0:T(8,128)(2,1)} %slice.332), channel_id=1, source_target_pairs={{0,16},{8,24},{16,0},{24,8},{1,17},{9,25},{17,1},{25,9},{2,18},{10... | collective-permute-start | bytes 1572872 | tf_op jit(solution)/shard_map/ppermute | solution.py:1040
  268.2 36.5 %collective-permute-start.37 = (bf16[1536,256]{1,0:T(8,128)(2,1)}, bf16[1536,256]{1,0:T(8,128)(2,1)}, u32[]{:S(2)}, u32[]{:S(2)}) collective-permute-start(bf16[1536,256]{1,0:T(8,128)(2,1)} %copy-done.40), channel_id=1, source_target_pairs={{0,2},{2,0},{4,6},{6,4},{1,3},{3,1},{5,7},{7,5},{8,10},{10,8},{12,... | collective-permute-start | bytes 2359304 | tf_op jit(solution)/shard_map/ppermute | solution.py:1040
  269.8 37.1 %collective-permute-start.38 = (bf16[1536,256]{1,0:T(8,128)(2,1)S(1)}, bf16[1536,256]{1,0:T(8,128)(2,1)}, u32[]{:S(2)}, u32[]{:S(2)}) collective-permute-start(bf16[1536,256]{1,0:T(8,128)(2,1)S(1)} %copy-done.39), channel_id=1, source_target_pairs={{0,4},{2,6},{4,0},{6,2},{1,5},{3,7},{5,1},{7,3},{8,12},{10,14},{12... | collective-permute-start | bytes 2359304 | tf_op jit(solution)/shard_map/ppermute | solution.py:1040
  270.1 44.2 %collective-permute-start.39 = (bf16[1536,256]{1,0:T(8,128)(2,1)S(1)}, bf16[1536,256]{1,0:T(8,128)(2,1)}, u32[]{:S(2)}, u32[]{:S(2)}) collective-permute-start(bf16[1536,256]{1,0:T(8,128)(2,1)S(1)} %copy-done.37), channel_id=1, source_target_pairs={{0,6},{2,4},{4,2},{6,0},{1,7},{3,5},{5,3},{7,1},{8,14},{10,12},{12... | collective-permute-start | bytes 2359304 | tf_op jit(solution)/shard_map/ppermute | solution.py:1040
  294.1 35.9 %all-to-all-start.2 = ((bf16[4,128,1280]{2,1,0:T(8,128)(2,1)}), bf16[4,128,1280]{2,1,0:T(8,128)(2,1)}, u32[]{:S(2)}, u32[]{:S(2)}) async-start(bf16[4,128,1280]{2,1,0:T(8,128)(2,1)} %pad_maximum_fusion.1), calls=%async_computation.3 | async-start | bytes 2621440 | tf_op jit(solution)/shard_map/all_to_all | solution.py:1328
  300.9 24.5 %collective-permute-start.36 = (bf16[1,128,1024]{2,1,0:T(8,128)(2,1)S(1)}, bf16[1,128,1024]{2,1,0:T(8,128)(2,1)S(1)}, u32[]{:S(2)}, u32[]{:S(2)}) collective-permute-start(bf16[1,128,1024]{2,1,0:T(8,128)(2,1)S(1)} %slice.333), channel_id=1, source_target_pairs={{0,8},{8,0},{16,24},{24,16},{1,9},{9,1},{17,25},{25,17},{2,10},{10... | collective-permute-start | bytes 786440 | tf_op jit(solution)/shard_map/ppermute | solution.py:1040
  330.0 11.0 %all-to-all-start.3 = ((bf16[32,4,128]{2,1,0:T(4,128)(2,1)}), bf16[32,4,128]{2,1,0:T(4,128)(2,1)S(1)}, u32[]{:S(2)}, u32[]{:S(2)}) async-start(bf16[32,4,128]{2,1,0:T(4,128)(2,1)} %bitcast.60), calls=%async_computation.4 | async-start | bytes 65536 | tf_op jit(solution)/shard_map/all_to_all | solution.py:1345
  336.7 6.0 %collective-permute-start.42 = (bf16[128,256]{1,0:T(8,128)(2,1)S(1)}, bf16[128,256]{1,0:T(8,128)(2,1)S(1)}, u32[]{:S(2)}, u32[]{:S(2)}) collective-permute-start(bf16[128,256]{1,0:T(8,128)(2,1)S(1)} %get-tuple-element.437), channel_id=1, source_target_pairs={{0,6},{2,4},{4,2},{6,0},{1,7},{3,5},{5,3},{7,1},{8,14},{10,12},{12... | collective-permute-start | bytes 196616 | tf_op jit(solution)/shard_map/ppermute | solution.py:1040
  339.4 4.6 %collective-permute-start.41 = (bf16[128,256]{1,0:T(8,128)(2,1)S(1)}, bf16[128,256]{1,0:T(8,128)(2,1)S(1)}, u32[]{:S(2)}, u32[]{:S(2)}) collective-permute-start(bf16[128,256]{1,0:T(8,128)(2,1)S(1)} %get-tuple-element.438), channel_id=1, source_target_pairs={{0,4},{2,6},{4,0},{6,2},{1,5},{3,7},{5,1},{7,3},{8,12},{10,14},{12... | collective-permute-start | bytes 196616 | tf_op jit(solution)/shard_map/ppermute | solution.py:1040
  339.9 4.3 %collective-permute-start.40 = (bf16[128,256]{1,0:T(8,128)(2,1)S(1)}, bf16[128,256]{1,0:T(8,128)(2,1)S(1)}, u32[]{:S(2)}, u32[]{:S(2)}) collective-permute-start(bf16[128,256]{1,0:T(8,128)(2,1)S(1)} %get-tuple-element.436), channel_id=1, source_target_pairs={{0,2},{2,0},{4,6},{6,4},{1,3},{3,1},{5,7},{7,5},{8,10},{10,8},{12,... | collective-permute-start | bytes 196616 | tf_op jit(solution)/shard_map/ppermute | solution.py:1040
  (91 other events, 620.7 us)
Sparse Core Ops, SparseCore 0:
  67.2 47.5 all-gather.2
  139.9 28.2 all-gather.4
  178.3 51.5 reduce-scatter.1
  265.9 74.7 all-reduce.3

commit v5 on v4

--- a/solution.py
+++ b/solution.py
@@ -807,6 +807,7 @@
         [],
         (0, 4 * value.size, 0),
         (value,),
+        limit=56,
     )
 
 
@@ -873,6 +874,7 @@
         (4 * rows * width * width, 6 * pairs.size),
         index,
         (memory, pairs, weight),
+        limit=56,
     )
 
 
@@ -1023,6 +1025,7 @@
         [],
         (2 * rows * width * columns, 4 * rows * (width + columns) + 2 * width * columns, 0),
         (normed, grad_joined, rounded, hidden),
+        limit=56,
     )[0]
 
 
@@ -1303,7 +1306,6 @@
         )
         gate_up_grad = hidden_grads[:, : 2 * hidden_width].reshape(gate_up.shape)
         down_grad = hidden_grads[:, 2 * hidden_width :].T
-        decoder_grad = in_order([part[:, :width] for part in last_parts], jnp.float32)
         cut = first_parts[0].shape[0]
         memory_grad = jnp.zeros((count, memory.shape[1], first_parts[0].shape[1]), jnp.bfloat16)
         for k in range(tp):
@@ -1322,9 +1324,10 @@
         little = jnp.broadcast_to(
             little.reshape(seq, 1, cores, 4, GROUP), (seq, tp, cores, 4, GROUP)
         )
-        both_grads, kv_far, little, gate_up_grad, down_grad, decoder_grad, memory_grad = together(
-            both_grads, kv_far, little, gate_up_grad, down_grad, decoder_grad, memory_grad
-        )
+        both_grads, kv_far, little, gate_up_grad, down_grad, last_parts, memory_grad = together(
+            both_grads, kv_far, little, gate_up_grad, down_grad, last_parts, memory_grad
+        )
+        decoder_grad = in_order([part[:, :width] for part in last_parts], jnp.float32)
         both_grads = lax.all_to_all(both_grads, "seq", 0, 0, tiled=True)
         kv_rows = kv_rows[: seq // 2] + high(kv_far)
         step = seq // 4
@@ -1336,8 +1339,8 @@
             memory_grad = lax.dynamic_update_slice(
                 memory_grad, second_parts[k][None], (t ^ k, cut, 0)
             )
-        both_grads, little, kv_rows, memory_grad = together(
-            both_grads, little, kv_rows, memory_grad
+        both_grads, little, kv_rows, memory_grad, decoder_grad = together(
+            both_grads, little, kv_rows, memory_grad, decoder_grad
         )
         cross_kv_grad = total(
             exchange([kv_rows[:, : 2 * GROUP]] + head_blocks(low(kv_rows))[1:], "tp")

time: 359 us -> 355 us (0.989)
  Pallas kernels: 76.2 us -> 90.5 us
  local copies, waits for them, and re-layouts: 64 us -> 57 us
  other arithmetic: 34.3 us -> 27.3 us
  waiting for transfers between devices: 74.2 us -> 68 us
    pallas_call x7, Pallas kernels: 37.4 us -> 47.3 us  [kernel_call(): pl.pallas_call(kernel, grid=(blocks,), in_specs=specs, out_specs=[spec fo...]
    unnamed x195 -> x181, local copies, waits for them, and re-layouts: 33.6 us -> 25.9 us
    pallas_call x5, Pallas kernels: 38.8 us -> 43.2 us  [with_index(): pl.pallas_call(kernel, grid_spec=pltpu.PrefetchScalarGridSpec(num_scalar_...]
    all_to_all x2, waiting for transfers between devices: 6.83 us -> 2.88 us  [exchange_all(): return lax.all_to_all(value, 'tp', 0, 0, tiled=True)]
  transfers between devices with their start and end apart: 51 -> 51, of which waited for: 23 -> 22; matrix products, arithmetic and copies ran while one was open for 26% -> 25% of each run, Pallas kernels for 21% -> 25%
where the time goes in v5:
time: 355 us; the launch traced here: 350 us
  Pallas kernels  90.5 us (25%)
  waiting for transfers between devices  68 us (19%)
  starting transfers between devices  64.1 us (18%)
  local copies, waits for them, and re-layouts  57 us (16%)
  other arithmetic  27.3 us (8%)
  matrix products  27.3 us (8%)
  between operations  15.5 us (4%)
    ppermute x43, waiting for transfers between devices, swap(): lax.ppermute(value, axis, [(place, place ^ flip) for place in range(size)])  60.3 us
    pallas_call x7, Pallas kernels, kernel_call(): pl.pallas_call(kernel, grid=(blocks,), in_specs=specs, out_specs=[spec fo...  47.3 us
    ppermute x43, starting transfers between devices, swap(): lax.ppermute(value, axis, [(place, place ^ flip) for place in range(size)])  46.6 us
    pallas_call x5, Pallas kernels, with_index(): pl.pallas_call(kernel, grid_spec=pltpu.PrefetchScalarGridSpec(num_scalar_...  43.2 us
    unnamed x181, local copies, waits for them, and re-layouts  25.9 us
    dot_general x7, matrix products, dot(): return jnp.dot(left, right, preferred_element_type=jnp.float32)  17.5 us
    all_to_all x2, starting transfers between devices, exchange_all(): return lax.all_to_all(value, 'tp', 0, 0, tiled=True)  9.95 us
    dot_general x7, matrix products, dot_t(): lax.dot_general(left, right, (((1,), (1,)), ((), ())), preferred_element_...  9.1 us
  transfers between devices with their start and end apart: 51, of which 22 were waited for; matrix products, arithmetic and copies ran while one was open for 25% of the time, Pallas kernels for 25%

profile of v5, /device:TPU:0, one launch (start us, length us, event | category | flops | bytes accessed | tf_op | source)
XLA Modules:
  0.0 349.5 jit_solution(10674310178002910044)
XLA Ops:
  9.5 2.9 pack_shards.1
  12.4 5.3 %all-to-all-start = ((bf16[4,1552,128]{2,1,0:T(8,128)(2,1)}), bf16[4,1552,128]{2,1,0:T(8,128)(2,1)S(1)}, u32[]{:S(2)}, u32[]{:S(2)}) async-start(bf16[4,1552,128]{2,1,0:T(8,128)(2,1)} %get-tuple-element.165), calls=%async_computation | async-start | bytes 3178496 | tf_op jit(solution)/shard_map/all_to_all | solution.py:1052
  17.7 3.6 %collective-permute-start.3 = (bf16[784,128]{1,0:T(8,128)(2,1)S(1)}, bf16[784,128]{1,0:T(8,128)(2,1)S(1)}, u32[]{:S(2)}, u32[]{:S(2)}) collective-permute-start(bf16[784,128]{1,0:T(8,128)(2,1)S(1)} %copy-done.80), channel_id=1, source_target_pairs={{0,24},{8,16},{16,8},{24,0},{1,25},{9,17},{17,9},{25,1},{2,26},{10... | collective-permute-start | bytes 602120 | tf_op jit(solution)/shard_map/ppermute | solution.py:1043
  23.5 4.0 %collective-permute-done.3 = bf16[784,128]{1,0:T(8,128)(2,1)S(1)} collective-permute-done((bf16[784,128]{1,0:T(8,128)(2,1)S(1)}, bf16[784,128]{1,0:T(8,128)(2,1)S(1)}, u32[]{:S(2)}, u32[]{:S(2)}) %collective-permute-start.3) | collective-permute-done | bytes 200736 | tf_op jit(solution)/shard_map/ppermute | solution.py:1043
  27.5 10.8 %collective-permute-done.2 = bf16[784,128]{1,0:T(8,128)(2,1)S(1)} collective-permute-done((bf16[784,128]{1,0:T(8,128)(2,1)S(1)}, bf16[784,128]{1,0:T(8,128)(2,1)S(1)}, u32[]{:S(2)}, u32[]{:S(2)}) %collective-permute-start.2) | collective-permute-done | bytes 200736 | tf_op jit(solution)/shard_map/ppermute | solution.py:1043
  40.2 1.7 broadcast_in_dim.108
  41.9 4.7 %all-to-all-start.1 = ((bf16[4,3,784,128]{3,2,1,0:T(8,128)(2,1)}), bf16[4,3,784,128]{3,2,1,0:T(8,128)(2,1)}, u32[]{:S(2)}, u32[]{:S(2)}) async-start(bf16[4,3,784,128]{3,2,1,0:T(8,128)(2,1)} %broadcast_in_dim.108), calls=%async_computation.1 | async-start | bytes 4816896 | tf_op jit(solution)/shard_map/all_to_all | solution.py:1052
  53.1 2.5 collective-permute-start.7
  55.7 1.9 collective-permute-start.5
  58.5 4.6 %collective-permute-done.7 = bf16[768,128]{1,0:T(8,128)(2,1)S(1)} collective-permute-done((bf16[768,128]{1,0:T(8,128)(2,1)}, bf16[768,128]{1,0:T(8,128)(2,1)S(1)}, u32[]{:S(2)}, u32[]{:S(2)}) %collective-permute-start.7) | collective-permute-done | bytes 196640 | tf_op jit(solution)/shard_map/ppermute | solution.py:1043
  63.1 7.8 %collective-permute-done.6 = bf16[768,128]{1,0:T(8,128)(2,1)} collective-permute-done((bf16[768,128]{1,0:T(8,128)(2,1)}, bf16[768,128]{1,0:T(8,128)(2,1)}, u32[]{:S(2)}, u32[]{:S(2)}) %collective-permute-start.6) | collective-permute-done | bytes 196640 | tf_op jit(solution)/shard_map/ppermute | solution.py:1043
  71.5 2.9 all-to-all-done.1.refs_2_
  74.9 2.2 copy.151
  82.4 5.0 %unpack_heads.2 = (bf16[1024,1024]{1,0:T(8,128)(2,1)S(1)}, bf16[1024,1024]{1,0:T(8,128)(2,1)S(1)}, bf16[1024,1024]{1,0:T(8,128)(2,1)S(1)}, bf16[4,8,16,128]{3,2,1,0:T(8,128)(2,1)S(1)}) custom-call(s32[3]{0:T(128)S(1)} %pad_add_fusion.index_ref, bf16[4,1552,128]{2,1,0:T(8,128)(2,1)S(1)} %all-to-all-done.refs_0_, ...), custom_call_target="tpu_custom_call" | custom-call | bytes 12845056 | tf_op jit(solution)/shard_map/unpack_heads/pallas_call | solution.py:649
  94.8 3.7 %self_forward.1 = (bf16[128,1024]{1,0:T(8,128)(2,1)S(1)}, f32[4,2,256]{2,1,0:T(2,128)S(1)}) custom-call(bf16[128,1024]{1,0:T(8,128)(2,1)S(1)} %fusion.14.q_ref, bf16[128,1024]{1,0:T(8,128)(2,1)S(1)} %convolution_convert_fusion.3.kv_ref, f32[16,128,128]{2,1,0:T(8,128)S(1)} %copy.152.bias_ref), custom_call_target="tpu_custom_call" | custom-call | flops 67108864 | bytes 786432 | tf_op jit(solution)/shard_map/self_forward/pallas_call | solution.py:566
  98.5 8.3 %fusion.3.kv_ref = bf16[2048,1024]{1,0:T(8,128)(2,1)} fusion(bf16[1024,1024]{1,0:T(8,128)(2,1)S(1)} %copy-done.28, bf16[4,2048,1024]{2,1,0:T(8,128)(2,1)} %memory_ref.1, s32[]{:T(128)S(6)} %select_n.56), kind=kOutput, calls=%fused_computation.3 | convolution fusion | flops 4297064448 | bytes 10485764 | tf_op jit(solution)/shard_map/dot_general | solution.py:412
  108.6 1.9 collective-permute-done.11.refs_6_
  112.6 5.4 %unpack_heads.3 = (bf16[1024,1024]{1,0:T(8,128)(2,1)S(1)}, bf16[1024,1024]{1,0:T(8,128)(2,1)S(1)}, bf16[1024,1024]{1,0:T(8,128)(2,1)S(1)}) custom-call(s32[3]{0:T(128)S(1)} %pad_add_fusion.index_ref, bf16[4,1552,128]{2,1,0:T(8,128)(2,1)S(1)} %all-to-all-done.refs_0_, bf16[4,1552,128]{2,1,0:T(8,128)(2,1)} %collective-permute-done.refs_1_, ...), custom_call_target="tpu_custom_call" | custom-call | bytes 12582912 | tf_op jit(solution)/shard_map/unpack_heads/pallas_call | solution.py:649
  122.4 2.2 fusion.15.q_ref
  124.6 2.2 copy-done.29
  126.8 8.4 %cross_forward.1 = (bf16[128,1024]{1,0:T(8,128)(2,1)S(1)}, f32[4,2,256]{2,1,0:T(2,128)S(1)}) custom-call(bf16[128,1024]{1,0:T(8,128)(2,1)S(1)} %fusion.15.q_ref, bf16[2048,1024]{1,0:T(8,128)(2,1)S(1)} %copy-done.29), custom_call_target="tpu_custom_call" | custom-call | flops 1073741824 | bytes 4718592 | tf_op jit(solution)/shard_map/cross_forward/pallas_call | solution.py:566
  141.0 6.9 %unpack_hidden.1 = (bf16[1024,1408]{1,0:T(8,128)(2,1)}, bf16[704,1024]{1,0:T(8,128)(2,1)}) custom-call(bf16[8,2112,128]{2,1,0:T(8,128)(2,1)} %bitcast.154), custom_call_target="tpu_custom_call" | custom-call | bytes 8650752 | tf_op jit(solution)/shard_map/unpack_hidden/pallas_call | solution.py:566
  147.9 2.8 collective-permute-done.16
  153.8 4.0 %fusion.62 = f32[512,1408]{1,0:T(8,128)S(1)} fusion(bf16[512,1024]{1,0:T(8,128)(2,1)S(1)} %constant_dynamic-update-slice_fusion.12.normed_ref, bf16[1024,1408]{1,0:T(8,128)(2,1)} %get-tuple-element.197), kind=kOutput, calls=%fused_computation.190 | convolution fusion | flops 1476395008 | bytes 6815744 | tf_op jit(solution)/shard_map/dot_general | solution.py:412
  157.8 2.9 fusion.13
  162.5 1.8 convolution_convert_fusion
  170.9 8.9 %hidden_terms.1 = bf16[1024,2112]{1,0:T(8,128)(2,1)} custom-call(bf16[512,1024]{1,0:T(8,128)(2,1)} %copy-done.56, bf16[512,1408]{1,0:T(8,128)(2,1)} %copy-done.41, bf16[512,1024]{1,0:T(8,128)(2,1)} %pad_maximum_fusion.2.rounded_ref, bf16[512,704]{1,0:T(8,128)(2,1)} %get-tuple-element.222.hidden_ref), custom_call_target="tpu_custom_call" | custom-call | flops 2214592512 | bytes 10747904 | tf_op jit(solution)/shard_map/hidden_terms/pallas_call | solution.py:566
  188.4 13.0 %cross_backward.1 = (bf16[128,1024]{1,0:T(8,128)(2,1)S(1)}, bf16[2048,1024]{1,0:T(8,128)(2,1)S(1)}) custom-call(bf16[128,1024]{1,0:T(8,128)(2,1)S(1)} %copy-done.25, bf16[128,1024]{1,0:T(8,128)(2,1)S(1)} %convolution_convert_fusion.2.do_ref, bf16[128,1024]{1,0:T(8,128)(2,1)S(1)} %copy-done.21, bf16[2048,1024]{1,0:T(8,128)(2,1)S(1)} %copy-done.30, ...), custom_call_target="tpu_custom_call" | custom-call | flops 2684354560 | bytes 9437184 | tf_op jit(solution)/shard_map/cross_backward/pallas_call | solution.py:566
  209.3 3.5 %self_backward.1 = (bf16[128,1024]{1,0:T(8,128)(2,1)S(1)}, bf16[128,1024]{1,0:T(8,128)(2,1)S(1)}, bf16[16,128,128]{2,1,0:T(8,128)(2,1)S(1)}) custom-call(bf16[128,1024]{1,0:T(8,128)(2,1)S(1)} %copy-done.15, bf16[128,1024]{1,0:T(8,128)(2,1)S(1)} %convolution_convert_fusion.1.do_ref, bf16[128,1024]{1,0:T(8,128)(2,1)S(1)} %get-tuple-element.203.o_ref, ...), custom_call_target="tpu_custom_call" | custom-call | flops 167772160 | bytes 1572864 | tf_op jit(solution)/shard_map/self_backward/pallas_call | solution.py:566
  216.2 3.3 hidden_out.1
  223.6 18.0 %memory_terms.1 = (bf16[4,128,1024]{2,1,0:T(8,128)(2,1)}, f32[4,128,1024]{2,1,0:T(8,128)}, bf16[512,256]{1,0:T(8,128)(2,1)}, bf16[512,256]{1,0:T(8,128)(2,1)}, b...) custom-call(s32[3]{0:T(128)} %copy-done.26, ...), custom_call_target="tpu_custom_call" | custom-call | flops 8589934592 | bytes 12582912 | tf_op jit(solution)/shard_map/memory_terms/pallas_call | solution.py:649
  247.9 11.5 %head_weights.1 = (bf16[4,128,1280]{2,1,0:T(8,128)(2,1)}, f32[4,128,1280]{2,1,0:T(8,128)}) custom-call(s32[3]{0:T(128)} %copy-done.26, bf16[128,1024]{1,0:T(8,128)(2,1)} %get-tuple-element.419.refs_0_, bf16[128,1024]{1,0:T(8,128)(2,1)} %get-tuple-element.418.refs_1_, bf16[128,1024]{1,0:T(8,128)(2,1)} %get-tuple-element.417.refs_2_, ...), custom_call_target="tpu_custom_call" | custom-call | flops 1342177280 | bytes 6291456 | tf_op jit(solution)/shard_map/head_weights/pallas_call | solution.py:649
  262.2 2.5 collective-permute-start.35
  268.7 2.2 copy-done.52
  275.7 2.4 copy.170
  278.8 10.2 %collective-permute-done.35 = bf16[2,128,1024]{2,1,0:T(8,128)(2,1)} collective-permute-done((bf16[2,128,1024]{2,1,0:T(8,128)(2,1)}, bf16[2,128,1024]{2,1,0:T(8,128)(2,1)}, u32[]{:S(2)}, u32[]{:S(2)}) %collective-permute-start.35) | collective-permute-done | bytes 524320 | tf_op jit(solution)/shard_map/ppermute | solution.py:1043
  289.7 3.7 %all-to-all-start.2 = ((bf16[4,128,1280]{2,1,0:T(8,128)(2,1)}), bf16[4,128,1280]{2,1,0:T(8,128)(2,1)S(1)}, u32[]{:S(2)}, u32[]{:S(2)}) async-start(bf16[4,128,1280]{2,1,0:T(8,128)(2,1)} %pad_maximum_fusion.1), calls=%async_computation.3 | async-start | bytes 2621440 | tf_op jit(solution)/shard_map/all_to_all | solution.py:1331
  295.5 2.0 collective-permute-start.36
  298.4 2.1 bitcast_dynamic-update-slice_fusion.2
  303.9 2.1 bitcast_dynamic-update-slice_fusion.1
  306.0 4.7 %collective-permute-done.39 = bf16[1536,256]{1,0:T(8,128)(2,1)} collective-permute-done((bf16[1536,256]{1,0:T(8,128)(2,1)}, bf16[1536,256]{1,0:T(8,128)(2,1)}, u32[]{:S(2)}, u32[]{:S(2)}) %collective-permute-start.39) | collective-permute-done | bytes 786464 | tf_op jit(solution)/shard_map/ppermute | solution.py:1043
  310.7 2.1 bitcast_dynamic-update-slice_fusion
  315.4 5.0 %collective-permute-done.36 = bf16[1,128,1024]{2,1,0:T(8,128)(2,1)S(1)} collective-permute-done((bf16[1,128,1024]{2,1,0:T(8,128)(2,1)}, bf16[1,128,1024]{2,1,0:T(8,128)(2,1)S(1)}, u32[]{:S(2)}, u32[]{:S(2)}) %collective-permute-start.36) | collective-permute-done | bytes 262176 | tf_op jit(solution)/shard_map/ppermute | solution.py:1043
  320.4 4.3 %all-to-all-done.2 = bf16[4,128,1280]{2,1,0:T(8,128)(2,1)S(1)} async-done(((bf16[4,128,1280]{2,1,0:T(8,128)(2,1)}), bf16[4,128,1280]{2,1,0:T(8,128)(2,1)S(1)}, u32[]{:S(2)}, u32[]{:S(2)}) %all-to-all-start.2) | async-done | bytes 1310752 | tf_op jit(solution)/shard_map/all_to_all | solution.py:1331
  324.7 3.0 all-to-all-start.3
  330.3 2.7 collective-permute-start.42
  337.6 1.8 collective-permute-done.41
  340.5 2.3 copy.209
  (383 shorter events, 112.3 us)
Async XLA Ops:
  12.4 27.7 %all-to-all-start = ((bf16[4,1552,128]{2,1,0:T(8,128)(2,1)}), bf16[4,1552,128]{2,1,0:T(8,128)(2,1)S(1)}, u32[]{:S(2)}, u32[]{:S(2)}) async-start(bf16[4,1552,128]{2,1,0:T(8,128)(2,1)} %get-tuple-element.165), calls=%async_computation | async-start | bytes 3178496 | tf_op jit(solution)/shard_map/all_to_all | solution.py:1052
  17.7 9.8 %collective-permute-start.3 = (bf16[784,128]{1,0:T(8,128)(2,1)S(1)}, bf16[784,128]{1,0:T(8,128)(2,1)S(1)}, u32[]{:S(2)}, u32[]{:S(2)}) collective-permute-start(bf16[784,128]{1,0:T(8,128)(2,1)S(1)} %copy-done.80), channel_id=1, source_target_pairs={{0,24},{8,16},{16,8},{24,0},{1,25},{9,17},{17,9},{25,1},{2,26},{10... | collective-permute-start | bytes 602120 | tf_op jit(solution)/shard_map/ppermute | solution.py:1043
  21.3 17.0 %collective-permute-start.2 = (bf16[784,128]{1,0:T(8,128)(2,1)S(1)}, bf16[784,128]{1,0:T(8,128)(2,1)S(1)}, u32[]{:S(2)}, u32[]{:S(2)}) collective-permute-start(bf16[784,128]{1,0:T(8,128)(2,1)S(1)} %copy-done.80), channel_id=1, source_target_pairs={{0,16},{8,24},{16,0},{24,8},{1,17},{9,25},{17,1},{25,9},{2,18},{10... | collective-permute-start | bytes 602120 | tf_op jit(solution)/shard_map/ppermute | solution.py:1043
  21.3 17.0 %collective-permute-start.1 = (bf16[784,128]{1,0:T(8,128)(2,1)S(1)}, bf16[784,128]{1,0:T(8,128)(2,1)S(1)}, u32[]{:S(2)}, u32[]{:S(2)}) collective-permute-start(bf16[784,128]{1,0:T(8,128)(2,1)S(1)} %copy-done.80), channel_id=1, source_target_pairs={{0,8},{8,0},{16,24},{24,16},{1,9},{9,1},{17,25},{25,17},{2,10},{10... | collective-permute-start | bytes 602120 | tf_op jit(solution)/shard_map/ppermute | solution.py:1043
  41.9 32.5 %all-to-all-start.1 = ((bf16[4,3,784,128]{3,2,1,0:T(8,128)(2,1)}), bf16[4,3,784,128]{3,2,1,0:T(8,128)(2,1)}, u32[]{:S(2)}, u32[]{:S(2)}) async-start(bf16[4,3,784,128]{3,2,1,0:T(8,128)(2,1)} %broadcast_in_dim.108), calls=%async_computation.1 | async-start | bytes 4816896 | tf_op jit(solution)/shard_map/all_to_all | solution.py:1052
  46.5 94.5 %all-gather.3.cloned.1.call-start = ((), (), s32[]{:S(2)}) async-start(), calls=%async_computation.5 | async-start | bytes 4866048 | tf_op jit(solution)/shard_map/all_gather | solution.py:1137
  53.1 10.0 %collective-permute-start.7 = (bf16[768,128]{1,0:T(8,128)(2,1)}, bf16[768,128]{1,0:T(8,128)(2,1)S(1)}, u32[]{:S(2)}, u32[]{:S(2)}) collective-permute-start(bf16[768,128]{1,0:T(8,128)(2,1)} %get-tuple-element.174), channel_id=1, source_target_pairs={{0,24},{8,16},{16,8},{24,0},{1,25},{9,17},{17,9},{25,1},{2,26},{10... | collective-permute-start | bytes 589832 | tf_op jit(solution)/shard_map/ppermute | solution.py:1043
  55.6 15.3 %collective-permute-start.6 = (bf16[768,128]{1,0:T(8,128)(2,1)}, bf16[768,128]{1,0:T(8,128)(2,1)}, u32[]{:S(2)}, u32[]{:S(2)}) collective-permute-start(bf16[768,128]{1,0:T(8,128)(2,1)} %get-tuple-element.174), channel_id=1, source_target_pairs={{0,16},{8,24},{16,0},{24,8},{1,17},{9,25},{17,1},{25,9},{2,18},{10... | collective-permute-start | bytes 589832 | tf_op jit(solution)/shard_map/ppermute | solution.py:1043
  55.7 15.3 %collective-permute-start.5 = (bf16[768,128]{1,0:T(8,128)(2,1)}, bf16[768,128]{1,0:T(8,128)(2,1)}, u32[]{:S(2)}, u32[]{:S(2)}) collective-permute-start(bf16[768,128]{1,0:T(8,128)(2,1)} %get-tuple-element.174), channel_id=1, source_target_pairs={{0,8},{8,0},{16,24},{24,16},{1,9},{9,1},{17,25},{25,17},{2,10},{10... | collective-permute-start | bytes 589832 | tf_op jit(solution)/shard_map/ppermute | solution.py:1043
  70.9 171.0 %all-gather.5.cloned.1.call-start = ((), (), s32[]{:S(2)}) async-start(), calls=%async_computation.7 | async-start | bytes 1310720 | tf_op jit(solution)/shard_map/all_gather | solution.py:1172
  74.4 8.0 %collective-permute-start.4 = (bf16[4,3,784,128]{3,2,1,0:T(8,128)(2,1)}, bf16[4,3,784,128]{3,2,1,0:T(8,128)(2,1)}, u32[]{:S(2)}, u32[]{:S(2)}) collective-permute-start(bf16[4,3,784,128]{3,2,1,0:T(8,128)(2,1)} %all-to-all-done.1.refs_2_), channel_id=1, source_target_pairs={{0,1},{1,0},{2,3},{3,2},{4,5},{5,4},{6,7},{7,6},{8,9},{9,8},{10,11... | collective-permute-start | bytes 7225352 | tf_op jit(solution)/shard_map/ppermute | solution.py:1043
  74.4 7.5 %collective-permute-start = (bf16[4,1552,128]{2,1,0:T(8,128)(2,1)S(1)}, bf16[4,1552,128]{2,1,0:T(8,128)(2,1)}, u32[]{:S(2)}, u32[]{:S(2)}) collective-permute-start(bf16[4,1552,128]{2,1,0:T(8,128)(2,1)S(1)} %all-to-all-done.refs_0_), channel_id=1, source_target_pairs={{0,1},{1,0},{2,3},{3,2},{4,5},{5,4},{6,7},{7,6},{8,9},{9,8},{10,11... | collective-permute-start | bytes 4767752 | tf_op jit(solution)/shard_map/ppermute | solution.py:1043
  78.4 28.4 %collective-permute-start.8 = (bf16[3,768,128]{2,1,0:T(8,128)(2,1)S(1)}, bf16[3,768,128]{2,1,0:T(8,128)(2,1)}, u32[]{:S(2)}, u32[]{:S(2)}) collective-permute-start(bf16[3,768,128]{2,1,0:T(8,128)(2,1)S(1)} %pad_maximum_fusion.4.refs_2_), channel_id=1, source_target_pairs={{0,2},{2,0},{4,6},{6,4},{1,3},{3,1},{5,7},{7,5},{8,10},{10,8},{12,... | collective-permute-start | bytes 1769480 | tf_op jit(solution)/shard_map/ppermute | solution.py:1043
  79.9 27.7 %collective-permute-start.9 = (bf16[3,768,128]{2,1,0:T(8,128)(2,1)S(1)}, bf16[3,768,128]{2,1,0:T(8,128)(2,1)}, u32[]{:S(2)}, u32[]{:S(2)}) collective-permute-start(bf16[3,768,128]{2,1,0:T(8,128)(2,1)S(1)} %pad_maximum_fusion.4.refs_2_), channel_id=1, source_target_pairs={{0,4},{2,6},{4,0},{6,2},{1,5},{3,7},{5,1},{7,3},{8,12},{10,14},{12... | collective-permute-start | bytes 1769480 | tf_op jit(solution)/shard_map/ppermute | solution.py:1043
  80.4 27.2 %collective-permute-start.10 = (bf16[3,768,128]{2,1,0:T(8,128)(2,1)S(1)}, bf16[3,768,128]{2,1,0:T(8,128)(2,1)}, u32[]{:S(2)}, u32[]{:S(2)}) collective-permute-start(bf16[3,768,128]{2,1,0:T(8,128)(2,1)S(1)} %pad_maximum_fusion.4.refs_2_), channel_id=1, source_target_pairs={{0,6},{2,4},{4,2},{6,0},{1,7},{3,5},{5,3},{7,1},{8,14},{10,12},{12... | collective-permute-start | bytes 1769480 | tf_op jit(solution)/shard_map/ppermute | solution.py:1043
  108.1 4.6 %collective-permute-start.14 = (bf16[3,768,128]{2,1,0:T(8,128)(2,1)}, bf16[3,768,128]{2,1,0:T(8,128)(2,1)}, u32[]{:S(2)}, u32[]{:S(2)}) collective-permute-start(bf16[3,768,128]{2,1,0:T(8,128)(2,1)} %collective-permute-done.10.refs_5_), channel_id=1, source_target_pairs={{0,1},{1,0},{2,3},{3,2},{4,5},{5,4},{6,7},{7,6},{8,9},{9,8},{10,11... | collective-permute-start | bytes 1769480 | tf_op jit(solution)/shard_map/ppermute | solution.py:1043
  136.0 11.9 %collective-permute-start.15 = (bf16[128,1024]{1,0:T(8,128)(2,1)S(1)}, bf16[128,1024]{1,0:T(8,128)(2,1)}, u32[]{:S(2)}, u32[]{:S(2)}) collective-permute-start(bf16[128,1024]{1,0:T(8,128)(2,1)S(1)} %multiply_convert_fusion.2), channel_id=1, source_target_pairs={{0,2},{2,0},{4,6},{6,4},{1,3},{3,1},{5,7},{7,5},{8,10},{10,8},{12,... | collective-permute-start | bytes 786440 | tf_op jit(solution)/shard_map/ppermute | solution.py:1043
  136.8 13.9 %collective-permute-start.16 = (bf16[128,1024]{1,0:T(8,128)(2,1)S(1)}, bf16[128,1024]{1,0:T(8,128)(2,1)}, u32[]{:S(2)}, u32[]{:S(2)}) collective-permute-start(bf16[128,1024]{1,0:T(8,128)(2,1)S(1)} %multiply_convert_fusion.2), channel_id=1, source_target_pairs={{0,4},{2,6},{4,0},{6,2},{1,5},{3,7},{5,1},{7,3},{8,12},{10,14},{12... | collective-permute-start | bytes 786440 | tf_op jit(solution)/shard_map/ppermute | solution.py:1043
  138.2 12.6 %collective-permute-start.17 = (bf16[128,1024]{1,0:T(8,128)(2,1)S(1)}, bf16[128,1024]{1,0:T(8,128)(2,1)}, u32[]{:S(2)}, u32[]{:S(2)}) collective-permute-start(bf16[128,1024]{1,0:T(8,128)(2,1)S(1)} %multiply_convert_fusion.2), channel_id=1, source_target_pairs={{0,6},{2,4},{4,2},{6,0},{1,7},{3,5},{5,3},{7,1},{8,14},{10,12},{12... | collective-permute-start | bytes 786440 | tf_op jit(solution)/shard_map/ppermute | solution.py:1043
  140.8 131.7 %reduce-scatter.2.cloned.1.call-start = ((), (), s32[]{:S(2)}) async-start(), calls=%async_computation.8 | async-start | bytes 5013504 | tf_op jit(solution)/shard_map/reduce_scatter | solution.py:1205
  165.3 14.4 %collective-permute-start.18 = (bf16[128,1024]{1,0:T(8,128)(2,1)}, bf16[128,1024]{1,0:T(8,128)(2,1)}, u32[]{:S(2)}, u32[]{:S(2)}) collective-permute-start(bf16[128,1024]{1,0:T(8,128)(2,1)} %get-tuple-element.422), channel_id=1, source_target_pairs={{0,2},{2,0},{4,6},{6,4},{1,3},{3,1},{5,7},{7,5},{8,10},{10,8},{12,... | collective-permute-start | bytes 786440 | tf_op jit(solution)/shard_map/ppermute | solution.py:1043
  166.5 13.3 %collective-permute-start.19 = (bf16[128,1024]{1,0:T(8,128)(2,1)}, bf16[128,1024]{1,0:T(8,128)(2,1)}, u32[]{:S(2)}, u32[]{:S(2)}) collective-permute-start(bf16[128,1024]{1,0:T(8,128)(2,1)} %get-tuple-element.421), channel_id=1, source_target_pairs={{0,4},{2,6},{4,0},{6,2},{1,5},{3,7},{5,1},{7,3},{8,12},{10,14},{12... | collective-permute-start | bytes 786440 | tf_op jit(solution)/shard_map/ppermute | solution.py:1043
  168.0 11.7 %collective-permute-start.20 = (bf16[128,1024]{1,0:T(8,128)(2,1)}, bf16[128,1024]{1,0:T(8,128)(2,1)}, u32[]{:S(2)}, u32[]{:S(2)}) collective-permute-start(bf16[128,1024]{1,0:T(8,128)(2,1)} %get-tuple-element.420), channel_id=1, source_target_pairs={{0,6},{2,4},{4,2},{6,0},{1,7},{3,5},{5,3},{7,1},{8,14},{10,12},{12... | collective-permute-start | bytes 786440 | tf_op jit(solution)/shard_map/ppermute | solution.py:1043
  179.8 160.7 %all-reduce.4.cloned.1.call-start = ((), (), s32[]{:S(2)}) async-start(), calls=%async_computation.6 | async-start | bytes 2097152 | tf_op jit(solution)/shard_map/psum | solution.py:1256
  184.0 17.4 %collective-permute-start.21 = (bf16[128,1536]{1,0:T(8,128)(2,1)S(1)}, bf16[128,1536]{1,0:T(8,128)(2,1)S(1)}, u32[]{:S(2)}, u32[]{:S(2)}) collective-permute-start(bf16[128,1536]{1,0:T(8,128)(2,1)S(1)} %get-tuple-element.468), channel_id=1, source_target_pairs={{0,2},{2,0},{4,6},{6,4},{1,3},{3,1},{5,7},{7,5},{8,10},{10,8},{12,... | collective-permute-start | bytes 1179656 | tf_op jit(solution)/shard_map/ppermute | solution.py:1043
  185.2 17.3 %collective-permute-start.22 = (bf16[128,1536]{1,0:T(8,128)(2,1)S(1)}, bf16[128,1536]{1,0:T(8,128)(2,1)S(1)}, u32[]{:S(2)}, u32[]{:S(2)}) collective-permute-start(bf16[128,1536]{1,0:T(8,128)(2,1)S(1)} %get-tuple-element.469), channel_id=1, source_target_pairs={{0,4},{2,6},{4,0},{6,2},{1,5},{3,7},{5,1},{7,3},{8,12},{10,14},{12... | collective-permute-start | bytes 1179656 | tf_op jit(solution)/shard_map/ppermute | solution.py:1043
  186.7 15.8 %collective-permute-start.23 = (bf16[128,1536]{1,0:T(8,128)(2,1)S(1)}, bf16[128,1536]{1,0:T(8,128)(2,1)S(1)}, u32[]{:S(2)}, u32[]{:S(2)}) collective-permute-start(bf16[128,1536]{1,0:T(8,128)(2,1)S(1)} %get-tuple-element.467), channel_id=1, source_target_pairs={{0,6},{2,4},{4,2},{6,0},{1,7},{3,5},{5,3},{7,1},{8,14},{10,12},{12... | collective-permute-start | bytes 1179656 | tf_op jit(solution)/shard_map/ppermute | solution.py:1043
  204.9 14.6 %collective-permute-start.24 = (bf16[128,1280]{1,0:T(8,128)(2,1)}, bf16[128,1280]{1,0:T(8,128)(2,1)}, u32[]{:S(2)}, u32[]{:S(2)}) collective-permute-start(bf16[128,1280]{1,0:T(8,128)(2,1)} %get-tuple-element.460), channel_id=1, source_target_pairs={{0,2},{2,0},{4,6},{6,4},{1,3},{3,1},{5,7},{7,5},{8,10},{10,8},{12,... | collective-permute-start | bytes 983048 | tf_op jit(solution)/shard_map/ppermute | solution.py:1043
  206.0 14.1 %collective-permute-start.25 = (bf16[128,1280]{1,0:T(8,128)(2,1)}, bf16[128,1280]{1,0:T(8,128)(2,1)}, u32[]{:S(2)}, u32[]{:S(2)}) collective-permute-start(bf16[128,1280]{1,0:T(8,128)(2,1)} %get-tuple-element.461), channel_id=1, source_target_pairs={{0,4},{2,6},{4,0},{6,2},{1,5},{3,7},{5,1},{7,3},{8,12},{10,14},{12... | collective-permute-start | bytes 983048 | tf_op jit(solution)/shard_map/ppermute | solution.py:1043
  207.6 12.5 %collective-permute-start.26 = (bf16[128,1280]{1,0:T(8,128)(2,1)}, bf16[128,1280]{1,0:T(8,128)(2,1)}, u32[]{:S(2)}, u32[]{:S(2)}) collective-permute-start(bf16[128,1280]{1,0:T(8,128)(2,1)} %get-tuple-element.459), channel_id=1, source_target_pairs={{0,6},{2,4},{4,2},{6,0},{1,7},{3,5},{5,3},{7,1},{8,14},{10,12},{12... | collective-permute-start | bytes 983048 | tf_op jit(solution)/shard_map/ppermute | solution.py:1043
  220.1 21.9 %collective-permute-start.27 = (bf16[128,1536]{1,0:T(8,128)(2,1)}, bf16[128,1536]{1,0:T(8,128)(2,1)S(1)}, u32[]{:S(2)}, u32[]{:S(2)}) collective-permute-start(bf16[128,1536]{1,0:T(8,128)(2,1)} %get-tuple-element.228), channel_id=1, source_target_pairs={{0,2},{2,0},{4,6},{6,4},{1,3},{3,1},{5,7},{7,5},{8,10},{10,8},{12,... | collective-permute-start | bytes 1179656 | tf_op jit(solution)/shard_map/ppermute | solution.py:1043
  220.9 21.2 %collective-permute-start.28 = (bf16[128,1536]{1,0:T(8,128)(2,1)}, bf16[128,1536]{1,0:T(8,128)(2,1)S(1)}, u32[]{:S(2)}, u32[]{:S(2)}) collective-permute-start(bf16[128,1536]{1,0:T(8,128)(2,1)} %get-tuple-element.229), channel_id=1, source_target_pairs={{0,4},{2,6},{4,0},{6,2},{1,5},{3,7},{5,1},{7,3},{8,12},{10,14},{12... | collective-permute-start | bytes 1179656 | tf_op jit(solution)/shard_map/ppermute | solution.py:1043
  222.4 19.6 %collective-permute-start.29 = (bf16[128,1536]{1,0:T(8,128)(2,1)}, bf16[128,1536]{1,0:T(8,128)(2,1)S(1)}, u32[]{:S(2)}, u32[]{:S(2)}) collective-permute-start(bf16[128,1536]{1,0:T(8,128)(2,1)} %get-tuple-element.230), channel_id=1, source_target_pairs={{0,6},{2,4},{4,2},{6,0},{1,7},{3,5},{5,3},{7,1},{8,14},{10,12},{12... | collective-permute-start | bytes 1179656 | tf_op jit(solution)/shard_map/ppermute | solution.py:1043
  242.1 17.3 %collective-permute-start.33 = (bf16[4,128,1024]{2,1,0:T(8,128)(2,1)}, bf16[4,128,1024]{2,1,0:T(8,128)(2,1)S(1)}, u32[]{:S(2)}, u32[]{:S(2)}) collective-permute-start(bf16[4,128,1024]{2,1,0:T(8,128)(2,1)} %get-tuple-element.251), channel_id=1, source_target_pairs={{0,1},{1,0},{2,3},{3,2},{4,5},{5,4},{6,7},{7,6},{8,9},{9,8},{10,11... | collective-permute-start | bytes 3145736 | tf_op jit(solution)/shard_map/ppermute | solution.py:1043
  243.4 18.5 %collective-permute-start.30 = (bf16[512,256]{1,0:T(8,128)(2,1)}, bf16[512,256]{1,0:T(8,128)(2,1)S(1)}, u32[]{:S(2)}, u32[]{:S(2)}) collective-permute-start(bf16[512,256]{1,0:T(8,128)(2,1)} %get-tuple-element.247), channel_id=1, source_target_pairs={{0,2},{2,0},{4,6},{6,4},{1,3},{3,1},{5,7},{7,5},{8,10},{10,8},{12,... | collective-permute-start | bytes 786440 | tf_op jit(solution)/shard_map/ppermute | solution.py:1043
  244.1 17.8 %collective-permute-start.31 = (bf16[512,256]{1,0:T(8,128)(2,1)}, bf16[512,256]{1,0:T(8,128)(2,1)S(1)}, u32[]{:S(2)}, u32[]{:S(2)}) collective-permute-start(bf16[512,256]{1,0:T(8,128)(2,1)} %get-tuple-element.248), channel_id=1, source_target_pairs={{0,4},{2,6},{4,0},{6,2},{1,5},{3,7},{5,1},{7,3},{8,12},{10,14},{12... | collective-permute-start | bytes 786440 | tf_op jit(solution)/shard_map/ppermute | solution.py:1043
  245.7 16.2 %collective-permute-start.32 = (bf16[512,256]{1,0:T(8,128)(2,1)S(1)}, bf16[512,256]{1,0:T(8,128)(2,1)S(1)}, u32[]{:S(2)}, u32[]{:S(2)}) collective-permute-start(bf16[512,256]{1,0:T(8,128)(2,1)S(1)} %copy-done.79), channel_id=1, source_target_pairs={{0,6},{2,4},{4,2},{6,0},{1,7},{3,5},{5,3},{7,1},{8,14},{10,12},{12... | collective-permute-start | bytes 786440 | tf_op jit(solution)/shard_map/ppermute | solution.py:1043
  261.9 6.8 %collective-permute-start.34 = (bf16[4,128,1280]{2,1,0:T(8,128)(2,1)}, bf16[4,128,1280]{2,1,0:T(8,128)(2,1)S(1)}, u32[]{:S(2)}, u32[]{:S(2)}) collective-permute-start(bf16[4,128,1280]{2,1,0:T(8,128)(2,1)} %get-tuple-element.273), channel_id=1, source_target_pairs={{0,1},{1,0},{2,3},{3,2},{4,5},{5,4},{6,7},{7,6},{8,9},{9,8},{10,11... | collective-permute-start | bytes 3932168 | tf_op jit(solution)/shard_map/ppermute | solution.py:1043
  262.2 26.8 %collective-permute-start.35 = (bf16[2,128,1024]{2,1,0:T(8,128)(2,1)}, bf16[2,128,1024]{2,1,0:T(8,128)(2,1)}, u32[]{:S(2)}, u32[]{:S(2)}) collective-permute-start(bf16[2,128,1024]{2,1,0:T(8,128)(2,1)} %slice.332), channel_id=1, source_target_pairs={{0,16},{8,24},{16,0},{24,8},{1,17},{9,25},{17,1},{25,9},{2,18},{10... | collective-permute-start | bytes 1572872 | tf_op jit(solution)/shard_map/ppermute | solution.py:1043
  264.8 33.7 %collective-permute-start.37 = (bf16[1536,256]{1,0:T(8,128)(2,1)}, bf16[1536,256]{1,0:T(8,128)(2,1)}, u32[]{:S(2)}, u32[]{:S(2)}) collective-permute-start(bf16[1536,256]{1,0:T(8,128)(2,1)} %get-tuple-element.299), channel_id=1, source_target_pairs={{0,2},{2,0},{4,6},{6,4},{1,3},{3,1},{5,7},{7,5},{8,10},{10,8},{12,... | collective-permute-start | bytes 2359304 | tf_op jit(solution)/shard_map/ppermute | solution.py:1043
  265.8 38.0 %collective-permute-start.38 = (bf16[1536,256]{1,0:T(8,128)(2,1)}, bf16[1536,256]{1,0:T(8,128)(2,1)}, u32[]{:S(2)}, u32[]{:S(2)}) collective-permute-start(bf16[1536,256]{1,0:T(8,128)(2,1)} %get-tuple-element.300), channel_id=1, source_target_pairs={{0,4},{2,6},{4,0},{6,2},{1,5},{3,7},{5,1},{7,3},{8,12},{10,14},{12... | collective-permute-start | bytes 2359304 | tf_op jit(solution)/shard_map/ppermute | solution.py:1043
  267.1 43.6 %collective-permute-start.39 = (bf16[1536,256]{1,0:T(8,128)(2,1)}, bf16[1536,256]{1,0:T(8,128)(2,1)}, u32[]{:S(2)}, u32[]{:S(2)}) collective-permute-start(bf16[1536,256]{1,0:T(8,128)(2,1)} %get-tuple-element.301), channel_id=1, source_target_pairs={{0,6},{2,4},{4,2},{6,0},{1,7},{3,5},{5,3},{7,1},{8,14},{10,12},{12... | collective-permute-start | bytes 2359304 | tf_op jit(solution)/shard_map/ppermute | solution.py:1043
  289.7 35.0 %all-to-all-start.2 = ((bf16[4,128,1280]{2,1,0:T(8,128)(2,1)}), bf16[4,128,1280]{2,1,0:T(8,128)(2,1)S(1)}, u32[]{:S(2)}, u32[]{:S(2)}) async-start(bf16[4,128,1280]{2,1,0:T(8,128)(2,1)} %pad_maximum_fusion.1), calls=%async_computation.3 | async-start | bytes 2621440 | tf_op jit(solution)/shard_map/all_to_all | solution.py:1331
  295.5 24.9 %collective-permute-start.36 = (bf16[1,128,1024]{2,1,0:T(8,128)(2,1)}, bf16[1,128,1024]{2,1,0:T(8,128)(2,1)S(1)}, u32[]{:S(2)}, u32[]{:S(2)}) collective-permute-start(bf16[1,128,1024]{2,1,0:T(8,128)(2,1)} %slice.333), channel_id=1, source_target_pairs={{0,8},{8,0},{16,24},{24,16},{1,9},{9,1},{17,25},{25,17},{2,10},{10... | collective-permute-start | bytes 786440 | tf_op jit(solution)/shard_map/ppermute | solution.py:1043
  324.7 10.3 %all-to-all-start.3 = ((bf16[32,4,128]{2,1,0:T(4,128)(2,1)}), bf16[32,4,128]{2,1,0:T(4,128)(2,1)S(1)}, u32[]{:S(2)}, u32[]{:S(2)}) async-start(bf16[32,4,128]{2,1,0:T(4,128)(2,1)} %bitcast.60), calls=%async_computation.4 | async-start | bytes 65536 | tf_op jit(solution)/shard_map/all_to_all | solution.py:1348
  330.3 7.3 %collective-permute-start.42 = (bf16[128,256]{1,0:T(8,128)(2,1)S(1)}, bf16[128,256]{1,0:T(8,128)(2,1)S(1)}, u32[]{:S(2)}, u32[]{:S(2)}) collective-permute-start(bf16[128,256]{1,0:T(8,128)(2,1)S(1)} %get-tuple-element.445), channel_id=1, source_target_pairs={{0,6},{2,4},{4,2},{6,0},{1,7},{3,5},{5,3},{7,1},{8,14},{10,12},{12... | collective-permute-start | bytes 196616 | tf_op jit(solution)/shard_map/ppermute | solution.py:1043
  333.0 6.5 %collective-permute-start.41 = (bf16[128,256]{1,0:T(8,128)(2,1)S(1)}, bf16[128,256]{1,0:T(8,128)(2,1)S(1)}, u32[]{:S(2)}, u32[]{:S(2)}) collective-permute-start(bf16[128,256]{1,0:T(8,128)(2,1)S(1)} %get-tuple-element.446), channel_id=1, source_target_pairs={{0,4},{2,6},{4,0},{6,2},{1,5},{3,7},{5,1},{7,3},{8,12},{10,14},{12... | collective-permute-start | bytes 196616 | tf_op jit(solution)/shard_map/ppermute | solution.py:1043
  333.6 6.1 %collective-permute-start.40 = (bf16[128,256]{1,0:T(8,128)(2,1)S(1)}, bf16[128,256]{1,0:T(8,128)(2,1)S(1)}, u32[]{:S(2)}, u32[]{:S(2)}) collective-permute-start(bf16[128,256]{1,0:T(8,128)(2,1)S(1)} %get-tuple-element.444), channel_id=1, source_target_pairs={{0,2},{2,0},{4,6},{6,4},{1,3},{3,1},{5,7},{7,5},{8,10},{10,8},{12,... | collective-permute-start | bytes 196616 | tf_op jit(solution)/shard_map/ppermute | solution.py:1043
  (84 other events, 638.5 us)
Sparse Core Ops, SparseCore 0:
  71.1 47.9 all-gather.2
  140.9 25.5 all-gather.4
  179.9 51.1 reduce-scatter.1
  262.4 77.7 all-reduce.3
